TPU v7x, 32 devices: a whole 2x2x4 slice. The times are simulated.
32 devices in a mesh: var: 4 (over x, core), ty: 2 (over y), tx: 4 (over z).
Axes of the slice: x: 2, y: 2, z: 4, core: 2. Of those that a mesh axis runs over, the one named last changes fastest.
Arguments:
- features: bfloat16 [128, 128, 180], P('ty', 'tx'), may hold values from -6 to 6
- labels: int32 [128, 128], P('ty', 'tx'), may hold values from 1 to 4
- qkv_weight: bfloat16 [2, 180, 540], replicated, may hold values from -0.4375 to 0.4375
- proj_weight: bfloat16 [2, 180, 180], replicated, may hold values from -0.4375 to 0.4375
- up_weight: bfloat16 [2, 180, 360], replicated, may hold values from -0.4375 to 0.4375
- down_weight: bfloat16 [2, 360, 180], replicated, may hold values from -0.3125 to 0.3125
- swin_bias: float32 [2, 6, 225], replicated, may hold values from -340 to 340
- recon_weight: bfloat16 [9, 180, 48], replicated, may hold values from -0.3125 to 0.3125
- refine_qkv: bfloat16 [48, 144], replicated, may hold values from -0.875 to 0.875
- refine_proj: bfloat16 [48, 48], replicated, may hold values from -0.875 to 0.875
- refine_bias: float32 [2, 225], replicated, may hold values from -340 to 340
Outputs:
- restored: float32 [3, 512, 512], P(None, 'ty', 'tx')
All inputs are finite; a program needn't handle non-finite values.
Results may differ from a plain program's by a relative error of at most 0.015.
Values may be sent and summed in bfloat16 or wider, within the bound.
No kernel may reach another device: no remote copies, remote signals or barrier semaphores. Data moves between devices by JAX's collectives and lax.ppermute only.
A program may use at most 128 MiB of HBM per device.

v0:
```python
import jax
import jax.numpy as jnp
from jax import lax
from jax.sharding import PartitionSpec as P

WIN = 8
SHIFT = 4
SCALE = 4
VAR_DEV = 2


EPSILON = 1e-05
MASKED = -1e30


def extended(cells, sides, width):
    for axis, dim in sides:
        count = lax.axis_size(axis)
        ends = count - 1
        head = lax.slice_in_dim(cells, 0, width, axis=dim)
        tail = lax.slice_in_dim(cells, cells.shape[dim] - width, cells.shape[dim], axis=dim)
        cells = jnp.concatenate(
            [
                lax.ppermute(tail, axis, [(i, (i + 1) % count) for i in range(ends)]),
                cells,
                lax.ppermute(head, axis, [((i + 1) % count, i) for i in range(ends)]),
            ],
            axis=dim,
        )
    return cells


def normalize(values):
    values = values.astype(jnp.float32)
    average = jnp.mean(values, axis=-1, keepdims=True)
    centred = values - average
    spread = jnp.mean(centred * centred, axis=-1, keepdims=True)
    return centred * lax.rsqrt(spread + EPSILON)


def to_windows(grid):
    leading, height, breadth, channels = grid.shape
    grid = grid.reshape(leading, height // WIN, WIN, breadth // WIN, WIN, channels)
    grid = grid.transpose(0, 1, 3, 2, 4, 5)
    return grid.reshape(leading, height // WIN * (breadth // WIN), WIN * WIN, channels)


def from_windows(windows, height, breadth):
    leading, window_count, cells, channels = windows.shape
    windows = windows.reshape(leading, height // WIN, breadth // WIN, WIN, WIN, channels)
    windows = windows.transpose(0, 1, 3, 2, 4, 5)
    return windows.reshape(leading, height, breadth, channels)


def bias_table(offset_table, variant_codes):
    position = jnp.arange(WIN * WIN, dtype=jnp.int32)
    row_step = (position // WIN)[:, None] - (position // WIN)[None, :]
    across = (position % WIN)[:, None] - (position % WIN)[None, :]
    transpose_bit = (variant_codes // 4)[:, None, None]
    flip_rows = (variant_codes // 2 % 2)[:, None, None]
    flip_cols = (variant_codes % 2)[:, None, None]
    row_moved = jnp.where(flip_rows == 1, -row_step, row_step)
    col_moved = jnp.where(flip_cols == 1, -across, across)
    leading_step = jnp.where(transpose_bit == 1, col_moved, row_moved)
    trailing_step = jnp.where(transpose_bit == 1, row_moved, col_moved)
    table_index = (leading_step + WIN - 1) * (2 * WIN - 1) + trailing_step + WIN - 1
    slots = jnp.arange((2 * WIN - 1) * (2 * WIN - 1), dtype=jnp.int32)
    one_hot = (table_index[..., None] == slots).astype(jnp.float32)
    return jnp.einsum("vqkt,ht->vhqk", one_hot, offset_table, precision=lax.Precision.HIGHEST)


def variant_kernels(kernel, variant_codes):
    transpose_bit = (variant_codes // 4)[:, None]
    flip_rows = (variant_codes // 2 % 2)[:, None]
    flip_cols = (variant_codes % 2)[:, None]
    kernel_spot = jnp.arange(9, dtype=jnp.int32)
    step_row = (kernel_spot // 3 - 1)[None, :]
    step_col = (kernel_spot % 3 - 1)[None, :]
    row_moved = jnp.where(flip_rows == 1, -step_row, step_row)
    col_moved = jnp.where(flip_cols == 1, -step_col, step_col)
    source_row = jnp.where(transpose_bit == 1, col_moved, row_moved)
    source_col = jnp.where(transpose_bit == 1, row_moved, col_moved)
    source = (source_row + 1) * 3 + source_col + 1
    pick_place = (source[:, :, None] == kernel_spot[None, None, :]).astype(jnp.bfloat16)
    channel = jnp.arange(kernel.shape[-1], dtype=jnp.int32)
    colour = (channel // (SCALE * SCALE))[None, :]
    sub_row = (channel % (SCALE * SCALE) // SCALE)[None, :]
    sub_col = (channel % SCALE)[None, :]
    sub_row_moved = jnp.where(flip_rows == 1, SCALE - 1 - sub_row, sub_row)
    sub_col_moved = jnp.where(flip_cols == 1, SCALE - 1 - sub_col, sub_col)
    anchor_row = jnp.where(transpose_bit == 1, sub_col_moved, sub_row_moved)
    anchor_col = jnp.where(transpose_bit == 1, sub_row_moved, sub_col_moved)
    anchor = colour * SCALE * SCALE + anchor_row * SCALE + anchor_col
    pick_channel = (channel[None, :, None] == anchor[:, None, :]).astype(jnp.bfloat16)
    placed = jnp.einsum(
        "vpq,qcs->vpcs", pick_place, kernel, preferred_element_type=jnp.float32
    ).astype(jnp.bfloat16)
    return jnp.einsum(
        "vpcs,vso->vpco", placed, pick_channel, preferred_element_type=jnp.float32
    ).astype(jnp.bfloat16)


def attend(normed, region, w_qkv, w_proj, bias_grid):
    head_count = bias_grid.shape[1]
    leading, window_count, cells, channels = normed.shape
    head_width = channels // head_count
    projected = jnp.einsum(
        "lnsc,ce->lnse", normed, w_qkv, preferred_element_type=jnp.float32
    ).astype(jnp.bfloat16)
    projected = projected.reshape(leading, window_count, cells, 3, head_count, head_width)
    queries = projected[:, :, :, 0]
    key_part = projected[:, :, :, 1]
    value_part = projected[:, :, :, 2]
    scores = jnp.einsum("lnqhd,lnkhd->lnhqk", queries, key_part, preferred_element_type=jnp.float32)
    scores = scores * head_width ** (-0.5) + bias_grid[:, None]
    matches = region[:, None, :, None] == region[:, None, None, :]
    scores = jnp.where(matches[None], scores, MASKED)
    largest = jnp.max(scores, axis=-1, keepdims=True)
    weights = jnp.exp(scores - largest)
    probabilities = (weights / jnp.sum(weights, axis=-1, keepdims=True)).astype(jnp.bfloat16)
    value_part = jnp.broadcast_to(value_part, (probabilities.shape[0],) + value_part.shape[1:])
    mixed = jnp.einsum(
        "lnhqk,lnkhd->lnqhd", probabilities, value_part, preferred_element_type=jnp.float32
    ).astype(jnp.bfloat16)
    mixed = mixed.reshape(probabilities.shape[0], window_count, cells, channels)
    return jnp.einsum("lnsc,ce->lnse", mixed, w_proj, preferred_element_type=jnp.float32)


def attention_half(tokens, region, w_qkv, w_proj, bias_grid):
    height, breadth = (tokens.shape[1], tokens.shape[2])
    windows = to_windows(tokens)
    region_windows = to_windows(region[None, :, :, None])[0, :, :, 0]
    normed = normalize(windows).astype(jnp.bfloat16)
    branch = attend(normed, region_windows, w_qkv, w_proj, bias_grid)
    result = (windows.astype(jnp.float32) + branch).astype(jnp.bfloat16)
    return from_windows(result, height, breadth)


def feed_forward(tokens, w_up, w_down):
    normed = normalize(tokens).astype(jnp.bfloat16)
    hidden = jnp.einsum("...c,ce->...e", normed, w_up, preferred_element_type=jnp.float32)
    hidden = jax.nn.gelu(hidden, approximate=False).astype(jnp.bfloat16)
    output = tokens.astype(jnp.float32) + jnp.einsum(
        "...e,ec->...c", hidden, w_down, preferred_element_type=jnp.float32
    )
    return output.astype(jnp.bfloat16)


def reconstruct(padded, kernels, height, breadth):
    accumulated = jnp.zeros((padded.shape[0], height, breadth, kernels.shape[-1]), jnp.float32)
    for kernel_spot in range(9):
        spot_row, spot_col = (kernel_spot // 3, kernel_spot % 3)
        window = padded[:, spot_row : spot_row + height, spot_col : spot_col + breadth]
        accumulated = accumulated + jnp.einsum(
            "vrcd,vde->vrce", window, kernels[:, kernel_spot], preferred_element_type=jnp.float32
        )
    return accumulated


def refine(average, region, w_qkv, w_proj, bias_grid):
    normed = normalize(average).astype(jnp.bfloat16)[None]
    return average + attend(normed, region, w_qkv, w_proj, bias_grid)[0]


def local(
    features,
    labels,
    qkv_weight,
    proj_weight,
    up_weight,
    down_weight,
    swin_bias,
    recon_weight,
    refine_qkv,
    refine_proj,
    refine_bias,
):
    height, breadth, channels = features.shape
    variant_codes = lax.axis_index("var") * VAR_DEV + jnp.arange(VAR_DEV, dtype=jnp.int32)
    first_bias = bias_table(swin_bias[0], variant_codes)
    second_bias = bias_table(swin_bias[1], variant_codes)
    region = extended(labels, (("ty", 0), ("tx", 1)), SHIFT)
    block_one = attention_half(features[None], labels, qkv_weight[0], proj_weight[0], first_bias)
    block_one = feed_forward(block_one, up_weight[0], down_weight[0])
    shifted = extended(block_one, (("ty", 1), ("tx", 2)), SHIFT)
    block_two = attention_half(shifted, region, qkv_weight[1], proj_weight[1], second_bias)
    own_tile = feed_forward(block_two[:, SHIFT:-SHIFT, SHIFT:-SHIFT], up_weight[1], down_weight[1])
    padded = extended(own_tile, (("ty", 1), ("tx", 2)), 1)
    kernels = variant_kernels(recon_weight, variant_codes)
    summed = jnp.sum(reconstruct(padded, kernels, height, breadth), axis=0)
    region_windows = to_windows(labels[None, :, :, None])[0, :, :, 0]
    refine_grid = bias_table(refine_bias, jnp.zeros((1,), jnp.int32))
    partial_sum = lax.psum_scatter(
        to_windows(summed[None])[0].astype(jnp.bfloat16), "var", scatter_dimension=0, tiled=True
    ).astype(jnp.float32)
    window_count = partial_sum.shape[0]
    first_window = lax.axis_index("var") * window_count
    part_region = lax.dynamic_slice_in_dim(region_windows, first_window, window_count, 0)
    refined = refine(partial_sum / 8.0, part_region, refine_qkv, refine_proj, refine_grid)
    refined = lax.all_gather(refined.astype(jnp.bfloat16), "var", axis=0, tiled=True).astype(
        refined.dtype
    )
    refined_grid = from_windows(refined[None], height, breadth)[0]
    picture = refined_grid.reshape(height, breadth, 3, SCALE, SCALE).transpose(2, 0, 3, 1, 4)
    return picture.reshape(3, SCALE * height, SCALE * breadth)


def solution(mesh):
    placed = (P("ty", "tx", None), P("ty", "tx"), P(), P(), P(), P(), P(), P(), P(), P(), P())
    return jax.shard_map(
        local, mesh=mesh, in_specs=placed, out_specs=P(None, "ty", "tx"), check_vma=False
    )
```

profile of v0, /device:TPU:9, one launch (start us, length us, event | category | flops | bytes accessed | tf_op | source)
XLA Modules:
  0.0 380.6 jit_solution(13849363442011120239)
XLA Ops:
  8.3 2.9 convert_bitcast_fusion.4
  12.8 5.0 %fusion.93 = f32[2,6,64,64]{3,1,2,0:T(8,128)S(1)} fusion(s32[2,64,64]{2,1,0:T(8,128)S(1)} %fusion.116, f32[1,6,225]{2,0,1:T(1,128)S(1)} %get-tuple-element.38), kind=kOutput, calls=%fused_computation.149 | convolution fusion | flops 134553600 | bytes 234776 | tf_op jit(solution)/shard_map/vqkt,ht->vhqk/dot_general | solution.py:69
  22.2 7.7 %copy.96 = bf16[32,64,540]{1,0,2:T(8,128)(2,1)} copy(bf16[32,64,540]{2,1,0:T(8,128)(2,1)S(1)} %convolution_convert_fusion.1) | data formatting | bytes 4423680 | tf_op jit(solution)/shard_map/convert_element_type | solution.py:109
  29.9 4.2 %slice_bitcast_fusion = (bf16[32,64,6,30]{1,0,3,2:T(8,128)(2,1)}, bf16[1,32,64,1,6,30]{2,1,5,4,3,0:T(8,128)(2,1)S(1)}, bf16[1,32,64,1,6,30]{2,1,5,4,3,0:T(8,128)(2,1)S(1)}) fusion(bf16[1,32,64,3,6,30]{2,1,5,4,3,0:T(8,128)(2,1)} %bitcast.295), kind=kLoop, calls=%fused_computation.144 | loop fusion | bytes 4423680 | tf_op jit(solution)/shard_map/broadcast_in_dim | solution.py:121
  38.0 2.0 copy.97
  40.0 2.7 broadcast_multiply_fusion
  42.7 11.0 %fusion.227 = (f32[2,32,6,64]{3,2,1,0:T(8,128)S(1)}, f32[2,32,6,64,64]{4,3,2,1,0:T(8,128)}) fusion(f32[2,6,64,64]{3,2,1,0:T(8,128)S(1)} %copy-done.11, f32[32,6,64,64]{3,2,1,0:T(8,128)S(1)} %broadcast_multiply_fusion, pred[32,64,64]{2,1,0:T(8,128)(4,1)S(1)} %broadcast_compare_fusion.1), kind=kOutput, calls=%fused_computation.381 | output fusion | flops 9437247 | bytes 9863168 | tf_op jit(solution)/shard_map/sub | solution.py:119
  53.7 7.1 %convert_bitcast_fusion.3 = bf16[2,32,64,6,30]{2,4,3,1,0:T(8,128)(2,1)S(1)} fusion(f32[2,32,6,64,64]{4,3,2,1,0:T(8,128)} %get-tuple-element.45, f32[2,32,6,64]{3,2,1,0:T(8,128)S(1)} %get-tuple-element.44, bf16[32,64,6,30]{1,3,2,0:T(8,128)(2,1)S(1)} %copy.97), kind=kOutput, calls=%fused_computation.98 | convolution fusion | flops 98254848 | bytes 8601600 | tf_op jit(solution)/shard_map/lnhqk,lnkhd->lnqhd/dot_general | solution.py:122
  60.8 1.9 copy.103
  64.0 2.8 add_convert_fusion.2
  74.3 2.8 fusion.89
  77.1 15.7 %add_convert_fusion.1 = bf16[2,64,32,180]{3,2,1,0:T(8,128)(2,1)S(1)} fusion(f32[2,64,32,180]{3,2,1,0:T(8,128)S(1)} %bitcast.308, f32[2,64,32,360]{3,2,1,0:T(8,128)S(1)} %get-tuple-element.46, u8[64,32,360]{2,1,0:T(8,128)(4,1)S(1)} %get-tuple-element.8, u8[64,32,360]{2,1,0:T(8,128)(4,1)S(1)} %get-tuple-element.7, bf16[1,360,180]{1,0,2:T(2,128)(2,1)S(1)} %get-tuple-element.28), kind=kOutput, calls=%fused_computation.90 | convolution fusion | flops 635535360 | bytes 11926080 | tf_op jit(solution)/shard_map/...e,ec->...c/dot_general | solution.py:143
  93.6 3.8 collective-permute-start
  98.7 4.6 %collective-permute-start.4 = (s32[4,32]{0,1:T(8,128)S(1)}, s32[4,32]{0,1:T(8,128)S(1)}, u32[]{:S(2)}, u32[]{:S(2)}) collective-permute-start(s32[4,32]{0,1:T(8,128)S(1)} %get-tuple-element.35), channel_id=1, source_target_pairs={{0,4},{1,5},{2,6},{3,7},{8,12},{9,13},{10,14},{11,15},{16,20},{17,... | collective-permute-start | bytes 1544 | tf_op jit(solution)/shard_map/ppermute | solution.py:24
  105.7 2.2 collective-permute-done.5
  107.9 3.2 collective-permute-start.6
  111.1 2.1 collective-permute-start.7
  113.2 6.3 %fusion.94 = f32[2,6,64,64]{3,1,2,0:T(8,128)} fusion(s32[2,64,64]{2,1,0:T(8,128)S(1)} %fusion.116, f32[1,6,225]{2,0,1:T(1,128)S(1)} %get-tuple-element.37), kind=kOutput, calls=%fused_computation.150 | convolution fusion | flops 134553600 | bytes 234776 | tf_op jit(solution)/shard_map/vqkt,ht->vhqk/dot_general | solution.py:69
  119.5 2.0 copy.120
  124.7 3.2 collective-permute-start.2
  127.9 2.1 collective-permute-start.3
  132.1 3.5 collective-permute-done.3
  135.6 2.9 pad_maximum_fusion
  139.3 3.2 convert_bitcast_fusion
  142.6 1.8 multiply_reduce_fusion
  144.6 1.9 multiply_convert_fusion
  146.8 5.4 %convolution_convert_fusion = bf16[2,45,64,540]{3,2,1,0:T(8,128)(2,1)} fusion(bf16[2,45,64,180]{3,2,1,0:T(8,128)(2,1)S(1)} %bitcast.307, bf16[1,180,540]{2,0,1:T(2,128)(2,1)S(1)} %get-tuple-element.25), kind=kOutput, calls=%fused_computation.76 | convolution fusion | flops 1122854400 | bytes 8488800 | tf_op jit(solution)/shard_map/lnsc,ce->lnse/dot_general | solution.py:107
  152.3 29.4 %copy.113 = bf16[2,45,64,540]{2,0,3,1:T(2,128)(2,1)} copy(bf16[2,45,64,540]{3,2,1,0:T(8,128)(2,1)} %convolution_convert_fusion) | data formatting | bytes 12441600 | tf_op jit(solution)/shard_map/convert_element_type | solution.py:109
  181.7 11.6 %fusion.218 = (bf16[2,45,64,1,6,30]{2,0,5,4,3,1:T(2,128)(2,1)}, bf16[2,45,64,1,6,30]{2,0,5,4,3,1:T(2,128)(2,1)S(1)}, bf16[2,45,64,1,6,30]{2,0,5,4,3,1:T(2,128)(2,1)}) fusion(bf16[2,45,64,3,6,30]{2,0,5,4,3,1:T(2,128)(2,1)} %bitcast.292), kind=kLoop, calls=%fused_computation.372 | loop fusion | bytes 12441600 | tf_op jit(solution)/shard_map/slice | solution.py:113
  193.3 10.8 %fusion.38 = f32[2,45,6,64,64]{3,4,2,1,0:T(8,128)} fusion(bf16[2,45,64,1,6,30]{2,0,5,4,3,1:T(2,128)(2,1)} %get-tuple-element.11, bf16[2,45,64,1,6,30]{2,0,5,4,3,1:T(2,128)(2,1)S(1)} %get-tuple-element.10), kind=kOutput, calls=%fused_computation.79 | convolution fusion | flops 132710400 | bytes 12994560 | tf_op jit(solution)/shard_map/lnqhd,lnkhd->lnhqk/dot_general | solution.py:114
  204.1 23.3 %fusion.228 = (f32[2,45,6,64]{3,2,1,0:T(8,128)S(1)}, f32[2,45,6,64,64]{3,4,2,1,0:T(8,128)}) fusion(f32[2,45,6,64,64]{3,4,2,1,0:T(8,128)} %fusion.38, f32[2,6,64,64]{2,3,1,0:T(8,128)S(1)} %copy-done.10, pred[45,64,64]{1,2,0:T(8,128)(4,1)S(1)} %broadcast_compare_fusion), kind=kOutput, calls=%fused_computation.382 | output fusion | flops 17694784 | bytes 18213888 | tf_op jit(solution)/shard_map/sub | solution.py:119
  227.3 11.9 %convert_bitcast_fusion.1 = bf16[2,45,64,6,30]{2,4,3,1,0:T(8,128)(2,1)} fusion(f32[2,45,6,64,64]{3,4,2,1,0:T(8,128)} %get-tuple-element.48, f32[2,45,6,64]{3,2,1,0:T(8,128)S(1)} %get-tuple-element.47, bf16[2,45,64,1,6,30]{2,0,5,4,3,1:T(2,128)(2,1)} %get-tuple-element.9), kind=kOutput, calls=%fused_computation.82 | convolution fusion | flops 138170880 | bytes 13132800 | tf_op jit(solution)/shard_map/lnhqk,lnkhd->lnqhd/dot_general | solution.py:122
  239.2 9.6 %copy.122 = bf16[2,45,64,6,30]{2,0,4,3,1:T(2,128)(2,1)S(1)} copy(bf16[2,45,64,6,30]{2,4,3,1,0:T(8,128)(2,1)} %convert_bitcast_fusion.1) | data formatting | bytes 4147200 | tf_op jit(solution)/shard_map/convert_element_type | solution.py:124
  248.8 3.5 copy.110
  258.3 3.3 fusion.90
  261.6 15.7 %fusion.43 = bf16[2,64,32,180]{3,2,1,0:T(8,128)(2,1)S(1)} fusion(f32[2,64,32,360]{3,2,1,0:T(8,128)S(1)} %get-tuple-element.49, bf16[2,72,40,180]{3,2,1,0:T(8,128)(2,1)S(1)} %bitcast.299, u8[64,32,360]{2,1,0:T(8,128)(4,1)S(1)} %get-tuple-element.6, u8[64,32,360]{2,1,0:T(8,128)(4,1)S(1)} %get-tuple-element.5, bf16[1,360,180]{1,0,2:T(2,128)(2,1)S(1)} %copy-done.12), kind=kOutput, calls=%fused_computation.87 | convolution fusion | flops 636272640 | bytes 10451520 | tf_op jit(solution)/shard_map/...e,ec->...c/dot_general | solution.py:143
  281.2 2.7 collective-permute-done.9
  284.1 3.2 collective-permute-start.10
  287.3 2.1 collective-permute-start.11
  290.8 2.3 collective-permute-done.11
  293.0 3.5 pad_maximum_fusion.1
  302.4 2.8 fusion.99
  306.2 21.5 %reduce-scatter.2.cloned.1.call-done = bf16[8,64,48]{1,2,0:T(8,128)(2,1)} async-done(((bf16[32,64,48]{1,2,0:T(8,128)(2,1)}), bf16[8,64,48]{1,2,0:T(8,128)(2,1)}) %reduce-scatter.2.cloned.1.call-update) | async-done | bytes 49168 | tf_op jit(solution)/shard_map/reduce_scatter | solution.py:193
  333.1 6.7 %all_gather.3 = bf16[32,64,48]{1,2,0:T(8,128)(2,1)S(1)} all-gather(bf16[8,64,48]{1,2,0:T(8,128)(2,1)S(1)} %fusion.98), channel_id=1, replica_groups=mesh['var'=4,'ty'=2,'tx'=4] {'var'}, dimensions={0}, use_global_device_ids=true | all-gather | bytes 245760 | tf_op jit(solution)/shard_map/all_gather | solution.py:200
  340.2 6.1 %copy.140 = f32[1,8,8,4,8,48]{2,1,4,3,5,0:T(8,128)} copy(f32[1,8,8,4,8,48]{5,4,2,3,1,0:T(8,128)S(1)} %convert_bitcast_fusion.5) | data formatting | bytes 786432 | tf_op jit(solution)/shard_map/reshape | solution.py:205
  346.3 4.3 %reshape.875 = f32[64,32,3,4,4]{0,1,4,3,2:T(8,128)S(1)} reshape(f32[1,8,8,4,8,48]{2,1,4,3,5,0:T(8,128)} %copy.140) | data formatting | bytes 786432 | tf_op jit(solution)/shard_map/reshape | solution.py:205
  350.6 10.9 %copy.141 = f32[3,64,4,32,4]{4,3,2,1,0:T(8,128)} copy(f32[3,64,4,32,4]{1,3,4,2,0:T(8,128)S(1)} %bitcast.310) | data formatting | bytes 786432 | tf_op jit(solution)/shard_map/reshape | solution.py:205
  361.5 12.1 %reshape.866 = f32[3,256,128]{2,1,0:T(8,128)} reshape(f32[3,64,4,32,4]{4,3,2,1,0:T(8,128)} %copy.141) | data formatting | bytes 786432 | tf_op jit(solution)/shard_map/reshape | solution.py:205
  (139 shorter events, 54.8 us)
Async XLA Ops:
  6.5 323.1 %copy-start = (bf16[48,144]{1,0:T(8,128)(2,1)S(1)}, bf16[48,144]{1,0:T(8,128)(2,1)}, u32[]{:S(2)}) copy-start(bf16[48,144]{1,0:T(8,128)(2,1)} %param.19) | copy-start | bytes 41476
  6.5 12.2 %copy-start.1 = (bf16[64,32,180]{2,1,0:T(8,128)(2,1)S(1)}, bf16[64,32,180]{2,1,0:T(8,128)(2,1)}, u32[]{:S(2)}) copy-start(bf16[64,32,180]{2,1,0:T(8,128)(2,1)} %param.11) | copy-start | bytes 2211844
  6.5 321.1 %reduce-scatter.2.cloned.1.call-start = ((), (), s32[]{:S(2)}) async-start(), calls=%async_computation.1 | async-start | bytes 491520 | tf_op jit(solution)/shard_map/reduce_scatter | solution.py:193
  8.3 12.3 %copy-start.3 = (bf16[2,180,540]{2,0,1:T(2,128)(2,1)S(1)}, bf16[2,180,540]{2,0,1:T(2,128)(2,1)}, u32[]{:S(2)}) copy-start(bf16[2,180,540]{2,0,1:T(2,128)(2,1)} %param.13) | copy-start | bytes 1166404
  29.9 4.2 %copy-start.9 = (s32[64,32]{0,1:T(8,128)S(1)}, s32[64,32]{0,1:T(8,128)}, u32[]{:S(2)}) copy-start(s32[64,32]{0,1:T(8,128)} %param.12) | copy-start | bytes 24580
  37.6 5.1 %copy-start.14 = (s32[32,64]{1,0:T(8,128)}, s32[32,64]{1,0:T(8,128)S(1)}, u32[]{:S(2)}) copy-start(s32[32,64]{1,0:T(8,128)S(1)} %eq.201) | copy-start | bytes 24580
  37.9 4.7 %copy-start.11 = (f32[2,6,64,64]{3,2,1,0:T(8,128)S(1)}, f32[2,6,64,64]{3,2,1,0:T(8,128)}, u32[]{:S(2)}) copy-start(f32[2,6,64,64]{3,2,1,0:T(8,128)} %copy.102) | copy-start | bytes 589828
  60.8 1.9 copy-start.2
  60.8 2.2 copy-start.6
  68.0 3.5 copy-start.4
  71.1 2.0 copy-start.5
  77.1 27.7 %copy-start.7 = (bf16[9,180,48]{1,2,0:T(8,128)(2,1)S(1)}, bf16[9,180,48]{1,2,0:T(8,128)(2,1)}, u32[]{:S(2)}) copy-start(bf16[9,180,48]{1,2,0:T(8,128)(2,1)} %param.18) | copy-start | bytes 466564
  93.6 30.0 %collective-permute-start = (bf16[2,4,32,180]{3,2,1,0:T(8,128)(2,1)}, bf16[2,4,32,180]{3,2,1,0:T(8,128)(2,1)}, u32[]{:S(2)}, u32[]{:S(2)}) collective-permute-start(bf16[2,4,32,180]{3,2,1,0:T(8,128)(2,1)} %get-tuple-element.23), channel_id=1, source_target_pairs={{0,4},{1,5},{2,6},{3,7},{8,12},{9,13},{10,14},{11,15},{16,20},{17,... | collective-permute-start | bytes 276488 | tf_op jit(solution)/shard_map/ppermute | solution.py:24
  97.4 26.2 %collective-permute-start.1 = (bf16[2,4,32,180]{3,2,1,0:T(8,128)(2,1)}, bf16[2,4,32,180]{3,2,1,0:T(8,128)(2,1)}, u32[]{:S(2)}, u32[]{:S(2)}) collective-permute-start(bf16[2,4,32,180]{3,2,1,0:T(8,128)(2,1)} %get-tuple-element.24), channel_id=1, source_target_pairs={{4,0},{5,1},{6,2},{7,3},{12,8},{13,9},{14,10},{15,11},{20,16},{21,... | collective-permute-start | bytes 276488 | tf_op jit(solution)/shard_map/ppermute | solution.py:26
  98.7 6.9 %collective-permute-start.4 = (s32[4,32]{0,1:T(8,128)S(1)}, s32[4,32]{0,1:T(8,128)S(1)}, u32[]{:S(2)}, u32[]{:S(2)}) collective-permute-start(s32[4,32]{0,1:T(8,128)S(1)} %get-tuple-element.35), channel_id=1, source_target_pairs={{0,4},{1,5},{2,6},{3,7},{8,12},{9,13},{10,14},{11,15},{16,20},{17,... | collective-permute-start | bytes 1544 | tf_op jit(solution)/shard_map/ppermute | solution.py:24
  103.4 4.5 %collective-permute-start.5 = (s32[4,32]{0,1:T(8,128)S(1)}, s32[4,32]{0,1:T(8,128)S(1)}, u32[]{:S(2)}, u32[]{:S(2)}) collective-permute-start(s32[4,32]{0,1:T(8,128)S(1)} %get-tuple-element.36), channel_id=1, source_target_pairs={{4,0},{5,1},{6,2},{7,3},{12,8},{13,9},{14,10},{15,11},{20,16},{21,... | collective-permute-start | bytes 1544 | tf_op jit(solution)/shard_map/ppermute | solution.py:26
  107.9 13.6 %collective-permute-start.6 = (s32[72,4]{0,1:T(4,128)S(1)}, s32[72,4]{0,1:T(4,128)S(1)}, u32[]{:S(2)}, u32[]{:S(2)}) collective-permute-start(s32[72,4]{0,1:T(4,128)S(1)} %get-tuple-element.33), channel_id=1, source_target_pairs={{0,1},{1,2},{2,3},{4,5},{5,6},{6,7},{8,9},{9,10},{10,11},{12,13},{... | collective-permute-start | bytes 3464 | tf_op jit(solution)/shard_map/ppermute | solution.py:24
  111.1 10.4 %collective-permute-start.7 = (s32[72,4]{0,1:T(4,128)S(1)}, s32[72,4]{0,1:T(4,128)S(1)}, u32[]{:S(2)}, u32[]{:S(2)}) collective-permute-start(s32[72,4]{0,1:T(4,128)S(1)} %get-tuple-element.34), channel_id=1, source_target_pairs={{1,0},{2,1},{3,2},{5,4},{6,5},{7,6},{9,8},{10,9},{11,10},{13,12},{... | collective-permute-start | bytes 3464 | tf_op jit(solution)/shard_map/ppermute | solution.py:26
  124.7 7.5 %collective-permute-start.2 = (bf16[2,72,4,180]{3,2,1,0:T(4,128)(2,1)S(1)}, bf16[2,72,4,180]{3,2,1,0:T(4,128)(2,1)S(1)}, u32[]{:S(2)}, u32[]{:S(2)}) collective-permute-start(bf16[2,72,4,180]{3,2,1,0:T(4,128)(2,1)S(1)} %get-tuple-element.15), channel_id=1, source_target_pairs={{0,1},{1,2},{2,3},{4,5},{5,6},{6,7},{8,9},{9,10},{10,11},{12,13},{... | collective-permute-start | bytes 622088 | tf_op jit(solution)/shard_map/ppermute | solution.py:24
  127.9 7.8 %collective-permute-start.3 = (bf16[2,72,4,180]{3,2,1,0:T(4,128)(2,1)S(1)}, bf16[2,72,4,180]{3,2,1,0:T(4,128)(2,1)S(1)}, u32[]{:S(2)}, u32[]{:S(2)}) collective-permute-start(bf16[2,72,4,180]{3,2,1,0:T(4,128)(2,1)S(1)} %get-tuple-element.16), channel_id=1, source_target_pairs={{1,0},{2,1},{3,2},{5,4},{6,5},{7,6},{9,8},{10,9},{11,10},{13,12},{... | collective-permute-start | bytes 622088 | tf_op jit(solution)/shard_map/ppermute | solution.py:26
  193.3 10.8 %copy-start.10 = (f32[2,6,64,64]{2,3,1,0:T(8,128)S(1)}, f32[2,6,64,64]{2,3,1,0:T(8,128)}, u32[]{:S(2)}) copy-start(f32[2,6,64,64]{2,3,1,0:T(8,128)} %copy.120) | copy-start | bytes 589828
  248.7 3.6 copy-start.8
  255.5 2.7 copy-start.13
  258.3 3.3 copy-start.12
  277.3 3.8 %collective-permute-start.8 = (bf16[2,1,32,180]{3,2,1,0:T(8,128)(2,1)S(1)}, bf16[2,1,32,180]{3,2,1,0:T(8,128)(2,1)S(1)}, u32[]{:S(2)}, u32[]{:S(2)}) collective-permute-start(bf16[2,1,32,180]{3,2,1,0:T(8,128)(2,1)S(1)} %get-tuple-element.21), channel_id=1, source_target_pairs={{0,4},{1,5},{2,6},{3,7},{8,12},{9,13},{10,14},{11,15},{16,20},{17,... | collective-permute-start | bytes 69128 | tf_op jit(solution)/shard_map/ppermute | solution.py:24
  279.2 4.7 %collective-permute-start.9 = (bf16[2,1,32,180]{3,2,1,0:T(8,128)(2,1)S(1)}, bf16[2,1,32,180]{3,2,1,0:T(8,128)(2,1)S(1)}, u32[]{:S(2)}, u32[]{:S(2)}) collective-permute-start(bf16[2,1,32,180]{3,2,1,0:T(8,128)(2,1)S(1)} %get-tuple-element.22), channel_id=1, source_target_pairs={{4,0},{5,1},{6,2},{7,3},{12,8},{13,9},{14,10},{15,11},{20,16},{21,... | collective-permute-start | bytes 69128 | tf_op jit(solution)/shard_map/ppermute | solution.py:26
  284.1 6.7 %collective-permute-start.10 = (bf16[2,66,1,180]{3,2,1,0:T(2,128)(2,1)S(1)}, bf16[2,66,1,180]{3,2,1,0:T(2,128)(2,1)S(1)}, u32[]{:S(2)}, u32[]{:S(2)}) collective-permute-start(bf16[2,66,1,180]{3,2,1,0:T(2,128)(2,1)S(1)} %get-tuple-element.20), channel_id=1, source_target_pairs={{0,1},{1,2},{2,3},{4,5},{5,6},{6,7},{8,9},{9,10},{10,11},{12,13},{... | collective-permute-start | bytes 142568 | tf_op jit(solution)/shard_map/ppermute | solution.py:24
  287.3 5.8 %collective-permute-start.11 = (bf16[2,66,1,180]{3,2,1,0:T(2,128)(2,1)S(1)}, bf16[2,66,1,180]{3,2,1,0:T(2,128)(2,1)S(1)}, u32[]{:S(2)}, u32[]{:S(2)}) collective-permute-start(bf16[2,66,1,180]{3,2,1,0:T(2,128)(2,1)S(1)} %get-tuple-element.19), channel_id=1, source_target_pairs={{1,0},{2,1},{3,2},{5,4},{6,5},{7,6},{9,8},{10,9},{11,10},{13,12},{... | collective-permute-start | bytes 142568 | tf_op jit(solution)/shard_map/ppermute | solution.py:26
  300.0 2.4 copy-start.15
  300.0 2.4 copy-start.17
  301.3 30.7 %copy-start.16 = (bf16[48,48]{1,0:T(8,128)(2,1)S(1)}, bf16[48,48]{1,0:T(8,128)(2,1)}, u32[]{:S(2)}) copy-start(bf16[48,48]{1,0:T(8,128)(2,1)} %param.20) | copy-start | bytes 13828
Sparse Core Ops, SparseCore 0:
  302.5 25.1 reduce-scatter.1
where the time goes:
time: 388 us; the launch traced here: 381 us
  local copies, waits for them, and re-layouts  121 us (31%)
  matrix products  106 us (27%)
  other arithmetic  69.1 us (18%)
  waiting for transfers between devices  33.6 us (9%)
  starting transfers between devices  30 us (8%)
  between operations  14.6 us (4%)
  blocking collectives  6.67 us (2%)
    convert_element_type x3, local copies, waits for them, and re-layouts, attend(): projected = jnp.einsum('lnsc,ce->lnse', normed, w_qkv, preferred_element_...  37.3 us
    sub x2, other arithmetic, attend(): weights = jnp.exp(scores - largest)  34.2 us
    reshape x4, local copies, waits for them, and re-layouts, local(): return picture.reshape(3, SCALE * height, SCALE * breadth)  33.4 us
    dot_general x2, matrix products, feed_forward(): jnp.einsum('...e,ec->...c', hidden, w_down, preferred_element_type=jnp.fl...  31.4 us
    reduce_scatter x1, waiting for transfers between devices, local(): lax.psum_scatter(to_windows(summed[None])[0].astype(jnp.bfloat16), 'var',...  21.5 us
    ppermute x6, starting transfers between devices, extended(): lax.ppermute(tail, axis, [(i, (i + 1) % count) for i in range(ends)])  19.9 us
    dot_general x3, matrix products, attend(): jnp.einsum('lnhqk,lnkhd->lnqhd', probabilities, value_part, preferred_ele...  19.3 us
    dot_general x3, matrix products, bias_table(): jnp.einsum('vqkt,ht->vhqk', one_hot, offset_table, precision=lax.Precisio...  14.2 us
  transfers between devices with their start and end apart: 13, of which 6 were waited for; matrix products, arithmetic and copies ran while one was open for 5% of the time, Pallas kernels for 0%

commit v1 on v0

v1 whole, which is shorter than its diff:
```python
import functools

import jax
import jax.numpy as jnp
from jax import lax
from jax.experimental import pallas as pl
from jax.experimental.pallas import tpu as pltpu
from jax.sharding import PartitionSpec as P

WIN = 8
CELLS = WIN * WIN
SHIFT = 4
SCALE = 4
VAR_DEV = 2
LANES = 128
HEAD_ROWS = 32
CLASSES = 4
SIDE = 2 * WIN - 1

EPSILON = 1e-05
LOG2E = 1.4426950408889634
BIG = float(2.0**100)
ERF_TANH = (
    7.97884207935252e-01,
    3.63342879e-02,
    -3.31288562e-05,
    -5.52410746e-05,
    3.96927395e-06,
    -1.33457816e-07,
    1.80588519e-09,
)

NN = (((1,), (0,)), ((), ()))
NT = (((1,), (1,)), ((), ()))


def dot(a, b, dims=NN):
    return lax.dot_general(a, b, dims, preferred_element_type=jnp.float32)


def gelu(x):
    square = x * x
    series = jnp.full_like(square, ERF_TANH[-1])
    for factor in ERF_TANH[-2::-1]:
        series = series * square + factor
    half = 0.5 * x
    return half + half * jnp.tanh(x * series)


def normalize(x, channels):
    inside = lax.broadcasted_iota(jnp.int32, (1, x.shape[1]), 1) < channels
    x = jnp.where(inside, x, 0.0)
    mean = jnp.sum(x, axis=1, keepdims=True) * (1.0 / channels)
    centred = jnp.where(inside, x - mean, 0.0)
    spread = jnp.sum(centred * centred, axis=1, keepdims=True) * (1.0 / channels)
    return centred * lax.rsqrt(spread + EPSILON)


def label_columns(x, channels):
    lane = lax.broadcasted_iota(jnp.int32, (1, x.shape[1]), 1) - channels
    in_class = (lane >= 0) & (lane < CLASSES)
    flag = lane == CLASSES
    key_gain = jnp.where(in_class, 1.0, jnp.where(flag, -1.0, 0.0))
    key_side = x * key_gain + jnp.where(flag, 1.0, 0.0)
    query_side = x * jnp.where(in_class, BIG, 0.0) + jnp.where(in_class | flag, -BIG, 0.0)
    return key_side, query_side


def head_masks(heads, width, channels, lanes):
    lane = lax.broadcasted_iota(jnp.int32, (1, lanes), 1)
    return [
        ((lane >= h * width) & (lane < (h + 1) * width)) | (lane >= channels) for h in range(heads)
    ]


def expand_bias(rows_ref, bias_ref, variant, first_head, heads):
    lane = lax.broadcasted_iota(jnp.int32, (WIN, LANES), 1)
    for pair in range(heads // 2):
        even = rows_ref[variant, first_head + 2 * pair]
        odd = rows_ref[variant, first_head + 2 * pair + 1]
        for key_row in range(WIN):
            start = (WIN - 1 - key_row) * WIN
            left = pltpu.roll(even, (LANES - start) % LANES, 1)
            right = pltpu.roll(odd, (LANES - start + CELLS) % LANES, 1)
            bias_ref[
                variant, key_row * WIN : (key_row + 1) * WIN, pair * LANES : (pair + 1) * LANES
            ] = jnp.where(lane < CELLS, left, right)


def soft(scores):
    largest = jnp.max(scores, axis=0, keepdims=True)
    return jnp.exp2(scores - largest).astype(jnp.bfloat16)


def mix_pair(values, first, second, heads, ones_row):
    zero = jnp.zeros((CELLS, LANES), jnp.bfloat16)
    lane = lax.broadcasted_iota(jnp.int32, (HEAD_ROWS, 2 * LANES), 1) % LANES
    mixed = []
    for pair in range(heads // 2):
        cut = slice(pair * LANES, (pair + 1) * LANES)
        stationary = jnp.concatenate(
            [
                jnp.concatenate([first[:, cut], zero], axis=1),
                jnp.concatenate([zero, second[:, cut]], axis=1),
            ],
            axis=0,
        )
        result = dot(values[pair * CELLS : (pair + 1) * CELLS], stationary)
        joined = jnp.where(lane < CELLS, result[:HEAD_ROWS], result[HEAD_ROWS:])
        mixed.append(joined * pl.reciprocal(joined[ones_row : ones_row + 1]))
    return mixed


def attend_pairs(x, n, scale, heads, w_qk, w_vt, pairs, key_bias):
    channels = heads * (w_vt.shape[0] // heads - 2)
    lanes = x.shape[1]
    projected = dot(n, w_qk)
    key_side, query_side = label_columns(x, channels)
    queries = (projected[:, :lanes] * scale + query_side).astype(jnp.bfloat16)
    keys = (projected[:, lanes:] + key_side).astype(jnp.bfloat16)
    values = dot(w_vt, n, NT)
    row = lax.broadcasted_iota(jnp.int32, values.shape, 0) % HEAD_ROWS
    values = jnp.where(row == channels // heads, 1.0, values).astype(jnp.bfloat16)
    masks = head_masks(heads, channels // heads, channels, lanes)
    scores = []
    for group in range(x.shape[0] // CELLS):
        q = queries[group * CELLS : (group + 1) * CELLS]
        stacked = jnp.concatenate([jnp.where(m, q, jnp.zeros_like(q)) for m in masks], axis=0)
        scores.append(dot(keys[group * CELLS : (group + 1) * CELLS], stacked, NT))
    outputs = []
    pad = jnp.zeros((LANES - heads // 2 * HEAD_ROWS, 2 * LANES), jnp.float32)
    for pair, first_bias, second_bias in pairs:
        first = soft(scores[2 * pair] + key_bias(first_bias))
        second = soft(scores[2 * pair + 1] + key_bias(second_bias))
        mixed = mix_pair(
            values[:, pair * LANES : (pair + 1) * LANES], first, second, heads, channels // heads
        )
        block = jnp.concatenate(mixed + [pad], axis=0).astype(jnp.bfloat16)
        for half in range(2):
            turned = block[:, half * LANES : (half + 1) * LANES].T
            outputs.append(jnp.concatenate([turned[:CELLS], turned[CELLS:]], axis=1))
    return jnp.concatenate(outputs, axis=0)


def feed_forward(h, channels, w_up, w_down):
    n = normalize(h, channels).astype(jnp.bfloat16)
    hidden = gelu(dot(n, w_up)).astype(jnp.bfloat16)
    return h + dot(hidden, w_down)


def round_bf16(x):
    return x.astype(jnp.bfloat16).astype(jnp.float32)


def first_kernel(
    heads, channels, x_ref, rows_ref, w_qk, w_vt, w_proj, w_up, w_down, y_ref, bias_ref
):
    @pl.when(pl.program_id(0) == 0)
    def _():
        for variant in range(VAR_DEV):
            expand_bias(rows_ref, bias_ref, variant, 0, heads)

    grid = x_ref[...].astype(jnp.float32)
    breadth, lanes = grid.shape[1:]
    count = breadth // WIN
    x = jnp.concatenate(
        [grid[:, w * WIN : (w + 1) * WIN].reshape(CELLS, lanes) for w in range(count)], axis=0
    )
    n = normalize(x, channels).astype(jnp.bfloat16)
    scale = (channels // heads) ** -0.5 * LOG2E
    pairs = [(pair, v, v) for v in range(VAR_DEV) for pair in range(count // 2)]
    o = attend_pairs(x, n, scale, heads, w_qk[...], w_vt[...], pairs, lambda v: bias_ref[v])
    branch = dot(o, w_proj[...])
    h = round_bf16(jnp.concatenate([x] * VAR_DEV, axis=0) + branch)
    y = feed_forward(h, channels, w_up[...], w_down[...])
    y = y.reshape(VAR_DEV, count, WIN, WIN, lanes)
    for v in range(VAR_DEV):
        y_ref[v] = jnp.concatenate([y[v, w] for w in range(count)], axis=1).astype(jnp.bfloat16)


def second_kernel(
    heads,
    channels,
    own_ref,
    top_ref,
    bottom_ref,
    left_ref,
    right_ref,
    rows_ref,
    w_qk,
    w_vt,
    w_proj,
    w_up,
    w_down,
    w_recon,
    out_ref,
    padded,
    bias_ref,
    acc,
):
    step = pl.program_id(0)
    height, breadth, lanes = own_ref.shape[1:]
    tall, wide = height + 2 * SHIFT, breadth + 2 * SHIFT
    count = wide // WIN

    @pl.when(step == 0)
    def _():
        for v in range(VAR_DEV):
            expand_bias(rows_ref, bias_ref, v, heads, heads)
            padded[v, 0:SHIFT, SHIFT : SHIFT + breadth] = top_ref[v].astype(jnp.float32)
            padded[v, tall - SHIFT : tall, SHIFT : SHIFT + breadth] = bottom_ref[v].astype(
                jnp.float32
            )
            for r in range(0, height, WIN):
                padded[v, SHIFT + r : SHIFT + r + WIN, SHIFT : SHIFT + breadth] = own_ref[
                    v, r : r + WIN
                ].astype(jnp.float32)
            for r in range(0, tall, WIN):
                cut = slice(r * SHIFT, (r + WIN) * SHIFT)
                padded[v, r : r + WIN, 0:SHIFT] = (
                    left_ref[v, cut].astype(jnp.float32).reshape(WIN, SHIFT, lanes)
                )
                padded[v, r : r + WIN, wide - SHIFT : wide] = (
                    right_ref[v, cut].astype(jnp.float32).reshape(WIN, SHIFT, lanes)
                )
        acc[...] = jnp.zeros_like(acc)

    base = pl.multiple_of(step * WIN, WIN)
    grids = [padded[v, pl.ds(base, WIN)] for v in range(VAR_DEV)]
    x = jnp.concatenate(
        [
            grids[v][:, w * WIN : (w + 1) * WIN].reshape(CELLS, lanes)
            for w in range(count)
            for v in range(VAR_DEV)
        ],
        axis=0,
    )
    n = normalize(x, channels).astype(jnp.bfloat16)
    scale = (channels // heads) ** -0.5 * LOG2E
    pairs = [(pair, 0, 1) for pair in range(count)]
    o = attend_pairs(x, n, scale, heads, w_qk[...], w_vt[...], pairs, lambda v: bias_ref[v])
    h = round_bf16(x + dot(o, w_proj[...]))
    y = feed_forward(h, channels, w_up[...], w_down[...])
    valid = x[:, channels + CLASSES : channels + CLASSES + 1]
    y = (y * valid).astype(jnp.bfloat16)
    total = None
    for v in range(VAR_DEV):
        tokens = jnp.concatenate(
            [y[(VAR_DEV * w + v) * CELLS : (VAR_DEV * w + v + 1) * CELLS] for w in range(count)],
            axis=0,
        )
        part = dot(tokens, w_recon[v])
        total = part if total is None else total + part
    total = total.reshape(count, WIN, WIN, 3 * lanes)
    for e in range(3):
        for w in range(count):
            acc[pl.ds(base + 2 - e, WIN), w * WIN : (w + 1) * WIN] += total[
                w, :, :, e * lanes : (e + 1) * lanes
            ]

    @pl.when(step == pl.num_programs(0) - 1)
    def _():
        out_channels = out_ref.shape[1]
        for strip in range(height // WIN):
            rows = slice(1 + SHIFT + strip * WIN, 1 + SHIFT + (strip + 1) * WIN)
            middle = acc[rows, SHIFT : SHIFT + breadth, :LANES]
            middle = pltpu.roll(middle.reshape(WIN * breadth, LANES), LANES - out_channels, 1)
            result = (
                acc[rows, SHIFT - 1 : SHIFT - 1 + breadth, :LANES]
                + middle.reshape(WIN, breadth, LANES)
                + acc[rows, SHIFT + 1 : SHIFT + 1 + breadth, LANES : 2 * LANES]
            )
            tokens = jnp.concatenate(
                [
                    result[:, w * WIN : (w + 1) * WIN].reshape(CELLS, LANES)
                    for w in range(breadth // WIN)
                ],
                axis=0,
            )
            out_ref[strip] = tokens.T[:out_channels].astype(jnp.bfloat16)


def third_kernel(heads, parts_ref, x_ref, rows_ref, w_qk, w_vt, w_projt, out_ref, bias_ref, final):
    expand_bias(rows_ref, bias_ref, 0, rows_ref.shape[1] - heads, heads)
    sources, strips, channels, strip_tokens = parts_ref.shape
    lanes = x_ref.shape[-1]
    breadth = strip_tokens // WIN
    width = channels // heads
    label_lane = w_qk.shape[1] // 2
    z = jnp.concatenate(
        [
            sum(parts_ref[s, strip].astype(jnp.float32) for s in range(sources))
            for strip in range(strips)
        ],
        axis=1,
    ) * (1.0 / (sources * VAR_DEV))
    mean = jnp.sum(z, axis=0, keepdims=True) * (1.0 / channels)
    centred = z - mean
    spread = jnp.sum(centred * centred, axis=0, keepdims=True) * (1.0 / channels)
    normed = centred * lax.rsqrt(spread + EPSILON)
    nt = normed.astype(jnp.bfloat16)
    tall = jnp.concatenate(
        [normed, jnp.zeros((LANES - channels, normed.shape[1]), jnp.float32)], axis=0
    )
    n = tall.T.astype(jnp.bfloat16)
    labels = x_ref[...].astype(jnp.float32)
    x = jnp.concatenate(
        [
            labels[s * WIN : (s + 1) * WIN, w * WIN : (w + 1) * WIN].reshape(CELLS, lanes)
            for s in range(strips)
            for w in range(breadth // WIN)
        ],
        axis=0,
    )
    spare = lanes - label_lane
    del spare
    lane = lax.broadcasted_iota(jnp.int32, (1, lanes), 1)
    x = jnp.where(lane >= LABEL_LANE(lanes), x, 0.0)
    key_side, query_side = label_columns(x, LABEL_LANE(lanes))
    projected = dot(n, w_qk[...])
    queries = (projected[:, :lanes] * (width**-0.5 * LOG2E) + query_side).astype(jnp.bfloat16)
    keys = (projected[:, lanes:] + key_side).astype(jnp.bfloat16)
    values = dot(w_vt[...], nt)
    row = lax.broadcasted_iota(jnp.int32, values.shape, 0) % HEAD_ROWS
    values = jnp.where(row == width, 1.0, values).astype(jnp.bfloat16)
    masks = head_masks(heads, width, LABEL_LANE(lanes), lanes)
    probabilities = []
    for group in range(x.shape[0] // CELLS):
        q = queries[group * CELLS : (group + 1) * CELLS]
        stacked = jnp.concatenate([jnp.where(m, q, jnp.zeros_like(q)) for m in masks], axis=0)
        scores = dot(keys[group * CELLS : (group + 1) * CELLS], stacked, NT)
        probabilities.append(soft(scores + bias_ref[0]))
    lane128 = lax.broadcasted_iota(jnp.int32, (channels, LANES), 1)
    branches = []
    for pair in range(len(probabilities) // 2):
        mixed = mix_pair(
            values[:, pair * LANES : (pair + 1) * LANES],
            probabilities[2 * pair],
            probabilities[2 * pair + 1],
            heads,
            width,
        )[0].astype(jnp.bfloat16)
        both = dot(w_projt[...], mixed)
        even, odd = both[:channels], both[channels:]
        sides = []
        for half in range(2):
            cut = slice(half * LANES, (half + 1) * LANES)
            sides.append(even[:, cut] + pltpu.roll(odd[:, cut], CELLS, 1))
        branches.append(jnp.where(lane128 < CELLS, sides[0], pltpu.roll(sides[1], CELLS, 1)))
    refined = (z + jnp.concatenate(branches, axis=1)).astype(jnp.bfloat16)
    stacked = jnp.concatenate(
        [refined[:, s * strip_tokens : (s + 1) * strip_tokens] for s in range(strips)], axis=0
    )
    token = lax.broadcasted_iota(jnp.int32, (strip_tokens, WIN * breadth * SCALE), 0)
    place = lax.broadcasted_iota(jnp.int32, (strip_tokens, WIN * breadth * SCALE), 1)
    cell = place // SCALE
    source = (cell % breadth // WIN) * CELLS + (cell // breadth) * WIN + cell % WIN
    spread_matrix = jnp.where(token == source, 1.0, 0.0).astype(jnp.bfloat16)
    wide = dot(stacked, spread_matrix)
    sub = lax.broadcasted_iota(jnp.int32, wide.shape, 1) % SCALE
    own = lax.broadcasted_iota(jnp.int32, wide.shape, 0) % SCALE
    wide = jnp.where(sub == own, wide, 0.0).astype(jnp.bfloat16)
    folded_rows = wide.shape[0] // SCALE
    pick_row = lax.broadcasted_iota(jnp.int32, (folded_rows, wide.shape[0]), 0)
    pick_col = lax.broadcasted_iota(jnp.int32, (folded_rows, wide.shape[0]), 1)
    pick = jnp.where(pick_col // SCALE == pick_row, 1.0, 0.0).astype(jnp.bfloat16)
    folded = dot(pick, wide)
    colours = channels // (SCALE * SCALE)
    row_lanes = breadth * SCALE
    for s in range(strips):
        for c in range(colours):
            first = (s * colours + c) * SCALE
            for y in range(WIN):
                start = (s * WIN + y) * SCALE
                final[c, start : start + SCALE] = folded[
                    first : first + SCALE, y * row_lanes : (y + 1) * row_lanes
                ]
    out_ref[...] = final[...].astype(jnp.bfloat16)


def LABEL_LANE(lanes):
    return 180 * lanes // 256


def shifted(strip, axis, step):
    count = lax.axis_size(axis)
    pairs = [(i, i + step) for i in range(count) if 0 <= i + step < count]
    return lax.ppermute(strip, axis, pairs)


def variant_steps(codes, row_step, col_step):
    shape = (-1,) + (1,) * row_step.ndim
    turn = (codes // 4).reshape(shape) == 1
    row = jnp.where((codes // 2 % 2).reshape(shape) == 1, -row_step, row_step)
    col = jnp.where((codes % 2).reshape(shape) == 1, -col_step, col_step)
    return jnp.where(turn, col, row), jnp.where(turn, row, col)


def bias_rows(tables, codes):
    place = jnp.arange(LANES, dtype=jnp.int32)
    row_step = jnp.broadcast_to((place // WIN - (WIN - 1))[None, :], (WIN, LANES))
    key_col = jnp.arange(WIN, dtype=jnp.int32)[:, None]
    col_step = (place % WIN)[None, :] - key_col
    lead, trail = variant_steps(codes, row_step, col_step)
    index = (lead + WIN - 1) * SIDE + trail + WIN - 1
    slots = jnp.arange(SIDE * SIDE, dtype=jnp.int32)
    one_hot = (index[:, None] == slots[None, :, None, None]).astype(jnp.float32)
    return jnp.einsum("ht,vtkp->vhkp", tables, one_hot, precision=lax.Precision.HIGHEST)


def variant_recon(kernel, codes, rows, lanes):
    spot = jnp.arange(9, dtype=jnp.int32)
    out = kernel.shape[-1]
    lead, trail = variant_steps(codes, spot // 3 - 1, spot % 3 - 1)
    source = (lead + 1) * 3 + trail + 1
    pick_place = (source[:, :, None] == spot).astype(jnp.bfloat16)
    channel = jnp.arange(out, dtype=jnp.int32)
    colour = channel // (SCALE * SCALE)
    turn = (codes // 4)[:, None] == 1
    sub_row = jnp.broadcast_to(channel % (SCALE * SCALE) // SCALE, (codes.shape[0], out))
    sub_col = jnp.broadcast_to(channel % SCALE, (codes.shape[0], out))
    sub_row = jnp.where((codes // 2 % 2)[:, None] == 1, SCALE - 1 - sub_row, sub_row)
    sub_col = jnp.where((codes % 2)[:, None] == 1, SCALE - 1 - sub_col, sub_col)
    anchor_row = jnp.where(turn, sub_col, sub_row)
    anchor_col = jnp.where(turn, sub_row, sub_col)
    anchor = colour * SCALE * SCALE + anchor_row * SCALE + anchor_col
    pick_channel = (channel[None, :, None] == anchor[:, None, :]).astype(jnp.bfloat16)
    placed = jnp.einsum("vpq,qcs->vpcs", pick_place, kernel)
    placed = jnp.einsum("vpcs,vso->vpco", placed, pick_channel)
    placed = placed.reshape(codes.shape[0], 3, 3, kernel.shape[1], out)
    blank = jnp.zeros_like(placed[:, :, 0])
    joined = jnp.concatenate([placed[:, :, 0], placed[:, :, 1]], axis=-1)
    joined = jnp.pad(joined, ((0, 0),) * 3 + ((0, LANES - 2 * out),))
    last = jnp.pad(placed[:, :, 2], ((0, 0),) * 3 + ((0, lanes - LANES - out),))
    del blank
    joined = jnp.concatenate([joined, last], axis=-1)
    joined = joined.transpose(0, 2, 1, 3).reshape(codes.shape[0], kernel.shape[1], 3 * lanes)
    return jnp.pad(joined, ((0, 0), (0, rows - kernel.shape[1]), (0, 0)))


def pad_to(array, *shape):
    return jnp.pad(array, [(0, want - have) for have, want in zip(array.shape, shape)])


def head_rows(weight, heads):
    channels = weight.shape[0]
    split = weight.T.reshape(heads, weight.shape[1] // heads, channels)
    return pad_to(split, heads, HEAD_ROWS, channels).reshape(heads * HEAD_ROWS, channels)


def local(
    features,
    labels,
    qkv_weight,
    proj_weight,
    up_weight,
    down_weight,
    swin_bias,
    recon_weight,
    refine_qkv,
    refine_proj,
    refine_bias,
):
    height, breadth, channels = features.shape
    heads = swin_bias.shape[1]
    out_channels = recon_weight.shape[-1]
    refine_heads = refine_bias.shape[0]
    lanes = -(-(channels + CLASSES + 1) // LANES) * LANES
    hidden = -(-up_weight.shape[-1] // LANES) * LANES
    codes = lax.axis_index("var") * VAR_DEV + jnp.arange(VAR_DEV, dtype=jnp.int32)

    lane = jnp.arange(lanes - channels, dtype=jnp.int32)
    marks = (labels[:, :, None] == lane + 1) & (lane < CLASSES) | (lane == CLASSES)
    x = jnp.concatenate([features, marks.astype(jnp.bfloat16)], axis=-1)

    tables = jnp.concatenate([swin_bias[0], swin_bias[1], refine_bias], axis=0) * LOG2E
    rows = bias_rows(tables[: 2 * heads], codes)
    refine_rows = bias_rows(tables[2 * heads :], jnp.zeros((1,), jnp.int32))

    def qk(weight, rows):
        size = weight.shape[1] // 3
        return jnp.concatenate(
            [
                pad_to(weight[:, :size], rows, lanes),
                pad_to(weight[:, size : 2 * size], rows, lanes),
            ],
            axis=1,
        )

    def proj(weight):
        split = weight.reshape(heads // 2, 2, channels // heads, channels)
        split = jnp.pad(split, ((0, 0), (0, 0), (0, HEAD_ROWS - channels // heads), (0, 0)))
        split = split.transpose(1, 0, 2, 3).reshape(2, heads // 2 * HEAD_ROWS, channels)
        return pad_to(split, 2, LANES, lanes).reshape(2 * LANES, lanes)

    blocks = []
    for i in range(2):
        blocks.append(
            (
                qk(qkv_weight[i], lanes),
                pad_to(
                    head_rows(qkv_weight[i][:, 2 * channels :], heads), heads * HEAD_ROWS, lanes
                ),
                proj(proj_weight[i]),
                pad_to(up_weight[i], lanes, hidden),
                pad_to(down_weight[i], hidden, lanes),
            )
        )
    recon = variant_recon(recon_weight, codes, lanes, lanes)

    whole = lambda a: pl.BlockSpec(a.shape, lambda *i: (0,) * a.ndim)
    params = pltpu.CompilerParams(
        dimension_semantics=("arbitrary",), vmem_limit_bytes=56 * 1024 * 1024
    )
    y1 = pl.pallas_call(
        functools.partial(first_kernel, heads, channels),
        grid=(height // WIN,),
        in_specs=[
            pl.BlockSpec((WIN, breadth, lanes), lambda i: (i, 0, 0)),
            whole(rows),
            *[whole(w) for w in blocks[0]],
        ],
        out_specs=pl.BlockSpec((VAR_DEV, WIN, breadth, lanes), lambda i: (0, i, 0, 0)),
        out_shape=jax.ShapeDtypeStruct((VAR_DEV, height, breadth, lanes), jnp.bfloat16),
        scratch_shapes=[pltpu.VMEM((VAR_DEV, CELLS, heads * CELLS), jnp.float32)],
        compiler_params=params,
        name="block_one",
    )(x, rows, *blocks[0])

    top = shifted(y1[:, height - SHIFT :], "ty", 1)
    bottom = shifted(y1[:, :SHIFT], "ty", -1)
    sides = []
    for cut, step in ((slice(breadth - SHIFT, breadth), 1), (slice(0, SHIFT), -1)):
        strip = jnp.concatenate([top[:, :, cut], y1[:, :, cut], bottom[:, :, cut]], axis=1)
        sides.append(shifted(strip.reshape(VAR_DEV, -1, lanes), "tx", step))

    operands = (y1, top, bottom, *sides, rows, *blocks[1], recon)
    partial = pl.pallas_call(
        functools.partial(second_kernel, heads, channels),
        grid=((height + 2 * SHIFT) // WIN,),
        in_specs=[whole(a) for a in operands],
        out_specs=pl.BlockSpec(
            (height // WIN, out_channels, WIN * breadth), lambda i: (0, 0, 0)
        ),
        out_shape=jax.ShapeDtypeStruct(
            (height // WIN, out_channels, WIN * breadth), jnp.bfloat16
        ),
        scratch_shapes=[
            pltpu.VMEM((VAR_DEV, height + 2 * SHIFT, breadth + 2 * SHIFT, lanes), jnp.float32),
            pltpu.VMEM((VAR_DEV, CELLS, heads * CELLS), jnp.float32),
            pltpu.VMEM((height + 2 * SHIFT + WIN, breadth + 2 * SHIFT, lanes), jnp.float32),
        ],
        compiler_params=params,
        name="block_two",
    )(*operands)

    sharers = lax.axis_size("var")
    strips = height // WIN // sharers
    parts = lax.all_to_all(
        partial.reshape(sharers, strips, out_channels, WIN * breadth), "var", 0, 0
    )
    part_x = lax.dynamic_slice_in_dim(
        x, lax.axis_index("var") * strips * WIN, strips * WIN, axis=0
    )
    w_qk = qk(refine_qkv, LANES)
    w_vt = head_rows(refine_qkv[:, 2 * out_channels :], refine_heads)
    w_projt = refine_proj.T.reshape(out_channels, refine_heads, out_channels // refine_heads)
    w_projt = pad_to(w_projt, out_channels, refine_heads, HEAD_ROWS)
    w_projt = w_projt.transpose(1, 0, 2).reshape(refine_heads * out_channels, HEAD_ROWS)
    colours = out_channels // (SCALE * SCALE)
    final = (colours, strips * WIN * SCALE, breadth * SCALE)
    operands = (parts, part_x, refine_rows, w_qk, w_vt, w_projt)
    strip = pl.pallas_call(
        functools.partial(third_kernel, refine_heads),
        grid=(1,),
        in_specs=[whole(a) for a in operands],
        out_specs=pl.BlockSpec(final, lambda i: (0, 0, 0)),
        out_shape=jax.ShapeDtypeStruct(final, jnp.bfloat16),
        scratch_shapes=[
            pltpu.VMEM((1, CELLS, refine_heads * CELLS), jnp.float32),
            pltpu.VMEM(final, jnp.float32),
        ],
        compiler_params=params,
        name="refinement",
    )(*operands)
    gathered = lax.all_gather(strip, "var", axis=0)
    picture = gathered.transpose(1, 0, 2, 3).reshape(colours, height * SCALE, breadth * SCALE)
    return picture.astype(jnp.float32)


def solution(mesh):
    placed = (P("ty", "tx", None), P("ty", "tx"), P(), P(), P(), P(), P(), P(), P(), P(), P())
    return jax.shard_map(
        local, mesh=mesh, in_specs=placed, out_specs=P(None, "ty", "tx"), check_vma=False
    )
```

time: 388 us -> 129 us (0.33); the launches traced: 381 us -> 127 us
  matrix products: 106 us -> 1.88 us
  local copies, waits for them, and re-layouts: 121 us -> 24.8 us
  Pallas kernels: 0 us -> 64.5 us
  other arithmetic: 69.1 us -> 7.12 us
  waiting for transfers between devices: 33.6 us -> 6.1 us
  between operations: 14.6 us -> 0.43 us
  starting transfers between devices: 30 us -> 16 us
    dot_general x30 -> x4, matrix products: 105 us -> 1.88 us  [the longest x2 1.14 us: bias_rows(): jnp.einsum('ht,vtkp->vhkp', tables, one_hot, precision=lax.Precision.HIGH...]
    pallas_call x0 -> x3, Pallas kernels: none -> 64.5 us  [the longest x1 41.3 us: local(): pl.pallas_call(functools.partial(second_kernel, heads, channels), grid=((...]
    convert_element_type x13 -> x1, local copies, waits for them, and re-layouts: 55.1 us -> 0.77 us  [local(): return picture.astype(jnp.float32)]
    sub x5, other arithmetic: 34.4 us -> 0.11 us  [the longest x2 0.09 us: bias_rows(): index = (lead + WIN - 1) * SIDE + trail + WIN - 1]
    reshape x4 -> x6, local copies, waits for them, and re-layouts: 33.4 us -> 0.95 us  [the longest x1 0.64 us: variant_recon(): joined.transpose(0, 2, 1, 3)]
    reduce_scatter x1 -> x0, waiting for transfers between devices: 21.5 us -> none  [local(): lax.psum_scatter(to_windows(summed[None])[0].astype(jnp.bfloat16), 'var',...]
    ppermute x12 -> x4, starting transfers between devices: 30 us -> 10.5 us  [shifted(): return lax.ppermute(strip, axis, pairs)]
    convert_element_type x7 -> x2, other arithmetic: 12.9 us -> 0.36 us  [the longest x1 0.34 us: local(): x = jnp.concatenate([features, marks.astype(jnp.bfloat16)], axis=-1)]
  transfers between devices with their start and end apart: 13 -> 5, of which waited for: 6 -> 3; matrix products, arithmetic and copies ran while one was open for 5% -> 12% of each run, Pallas kernels for 0% -> 0%
where the time goes in v1:
time: 129 us; the launch traced here: 127 us
  Pallas kernels  64.5 us (50%)
  local copies, waits for them, and re-layouts  24.8 us (19%)
  starting transfers between devices  16 us (12%)
  other arithmetic  7.12 us (6%)
  blocking collectives  6.51 us (5%)
  waiting for transfers between devices  6.1 us (5%)
  matrix products  1.88 us (1%)
    pallas_call x1, Pallas kernels, local(): pl.pallas_call(functools.partial(second_kernel, heads, channels), grid=((...  41.3 us
    pallas_call x1, Pallas kernels, local(): pl.pallas_call(functools.partial(first_kernel, heads, channels), grid=(he...  20 us
    ppermute x4, starting transfers between devices, shifted(): return lax.ppermute(strip, axis, pairs)  10.5 us
    pad x12, local copies, waits for them, and re-layouts, pad_to(): jnp.pad(array, [(0, want - have) for have, want in zip(array.shape, shape)])  6.68 us
    all_gather x1, blocking collectives, local(): gathered = lax.all_gather(strip, 'var', axis=0)  6.51 us
    all_to_all x1, starting transfers between devices, local(): lax.all_to_all(partial.reshape(sharers, strips, out_channels, WIN * bread...  5.49 us
    ppermute x4, waiting for transfers between devices, shifted(): return lax.ppermute(strip, axis, pairs)  5.13 us
    pallas_call x1, Pallas kernels, local(): pl.pallas_call(functools.partial(third_kernel, refine_heads), grid=(1,),...  3.11 us
  transfers between devices with their start and end apart: 5, of which 3 were waited for; matrix products, arithmetic and copies ran while one was open for 12% of the time, Pallas kernels for 0%

profile of v1, /device:TPU:9, one launch (start us, length us, event | category | flops | bytes accessed | tf_op | source)
XLA Modules:
  0.0 127.3 jit_solution(14628902191474618830)
XLA Ops:
  0.1 0.8 fusion.64
  0.9 0.7 maximum_multiply_fusion
  1.7 0.7 fusion
  2.4 0.7 copy.131
  3.1 2.0 %fusion.57 = (bf16[1,180,540]{2,0,1:T(2,128)(2,1)S(1)}, bf16[1,180,540]{2,0,1:T(2,128)(2,1)S(1)}) fusion(bf16[2,180,540]{2,0,1:T(2,128)(2,1)} %param.13), kind=kLoop, calls=%fused_computation.136 | loop fusion | bytes 777600 | tf_op jit(solution)/shard_map/slice | solution.py:500
  5.5 0.7 pad.85.w_vt
  6.8 0.7 pad.89.w_down
  7.6 1.1 fusion.60
  8.7 0.7 pad.88.w_up
  9.4 0.8 slice_reduce_fusion
  10.2 0.7 pad.87
  10.9 0.7 fusion.19.w_qk
  12.0 1.3 %pad_maximum_fusion.x_ref = bf16[64,32,256]{2,1,0:T(8,128)(2,1)} fusion(bf16[64,32,76]{2,1,0:T(8,128)(2,1)S(1)} %or_convert_fusion, bf16[64,32,180]{2,1,0:T(8,128)(2,1)S(1)} %copy-done), kind=kLoop, calls=%fused_computation.5 | loop fusion | flops 2097152 | bytes 2097152 | tf_op jit(solution)/shard_map/concatenate | solution.py:474
  13.3 20.0 %block_one.1.own_ref = bf16[2,64,32,256]{3,2,1,0:T(8,128)(2,1)} custom-call(bf16[64,32,256]{2,1,0:T(8,128)(2,1)} %pad_maximum_fusion.x_ref, f32[2,12,8,128]{3,2,1,0:T(8,128)} %bitcast.85, bf16[256,512]{1,0:T(8,128)(2,1)} %fusion.19.w_qk, bf16[192,256]{1,0:T(8,128)(2,1)} %pad.85.w_vt, bf16[256,256]{1,0:T(8,128)(2,1)} %bitcast.94, bf16[256,384]{1,0:T(8,128)(2,1)} %pad.88.w_up, ...), custom_call_target="tpu_custom_call" | custom-call | tf_op jit(solution)/shard_map/block_one/pallas_call | solution.py:515
  33.3 1.7 %fusion.56 = (bf16[2,4,32,256]{3,2,1,0:T(8,128)(2,1)}, bf16[2,4,32,256]{3,2,1,0:T(8,128)(2,1)}) fusion(bf16[2,64,32,256]{3,2,1,0:T(8,128)(2,1)} %block_one.1.own_ref), kind=kLoop, calls=%fused_computation.135 | loop fusion | bytes 524288 | tf_op jit(solution)/shard_map/slice | solution.py:531
  35.0 3.8 %collective-permute-start = (bf16[2,4,32,256]{3,2,1,0:T(8,128)(2,1)}, bf16[2,4,32,256]{3,2,1,0:T(8,128)(2,1)}, u32[]{:S(2)}, u32[]{:S(2)}) collective-permute-start(bf16[2,4,32,256]{3,2,1,0:T(8,128)(2,1)} %get-tuple-element.10), channel_id=1, source_target_pairs={{0,4},{1,5},{2,6},{3,7},{8,12},{9,13},{10,14},{11,15},{16,20},{17,... | collective-permute-start | bytes 393224 | tf_op jit(solution)/shard_map/ppermute | solution.py:388
  38.8 1.3 %collective-permute-start.1 = (bf16[2,4,32,256]{3,2,1,0:T(8,128)(2,1)}, bf16[2,4,32,256]{3,2,1,0:T(8,128)(2,1)}, u32[]{:S(2)}, u32[]{:S(2)}) collective-permute-start(bf16[2,4,32,256]{3,2,1,0:T(8,128)(2,1)} %get-tuple-element.9), channel_id=1, source_target_pairs={{4,0},{5,1},{6,2},{7,3},{12,8},{13,9},{14,10},{15,11},{20,16},{21,... | collective-permute-start | bytes 393224 | tf_op jit(solution)/shard_map/ppermute | solution.py:388
  40.0 2.2 %fusion.55 = (bf16[2,64,4,256]{3,2,1,0:T(4,128)(2,1)}, bf16[2,64,4,256]{3,2,1,0:T(4,128)(2,1)}) fusion(bf16[2,64,32,256]{3,2,1,0:T(8,128)(2,1)} %block_one.1.own_ref), kind=kLoop, calls=%fused_computation.134 | loop fusion | bytes 1048576 | tf_op jit(solution)/shard_map/slice | solution.py:534
  42.4 0.4 fusion.15
  44.1 0.6 fusion.18
  44.7 0.4 fusion.5
  45.2 0.6 reshape.533
  45.8 0.9 pad.100.w_recon
  47.1 0.6 pad.93.w_vt
  48.0 0.7 pad.97.w_down
  48.7 0.7 pad.96.w_up
  49.5 0.7 pad.95
  50.1 0.4 fusion.3
  50.5 0.8 fusion.61
  51.3 0.8 fusion.62
  52.5 2.3 %collective-permute-start.3 = (bf16[2,288,256]{2,1,0:T(8,128)(2,1)S(1)}, bf16[2,288,256]{2,1,0:T(8,128)(2,1)S(1)}, u32[]{:S(2)}, u32[]{:S(2)}) collective-permute-start(bf16[2,288,256]{2,1,0:T(8,128)(2,1)S(1)} %reshape.527), channel_id=1, source_target_pairs={{1,0},{2,1},{3,2},{5,4},{6,5},{7,6},{9,8},{10,9},{11,10},{13,12},{... | collective-permute-start | bytes 884744 | tf_op jit(solution)/shard_map/ppermute | solution.py:388
  55.0 3.2 %collective-permute-start.2 = (bf16[2,288,256]{2,1,0:T(8,128)(2,1)S(1)}, bf16[2,288,256]{2,1,0:T(8,128)(2,1)S(1)}, u32[]{:S(2)}, u32[]{:S(2)}) collective-permute-start(bf16[2,288,256]{2,1,0:T(8,128)(2,1)S(1)} %reshape.526), channel_id=1, source_target_pairs={{0,1},{1,2},{2,3},{4,5},{5,6},{6,7},{8,9},{9,10},{10,11},{12,13},{... | collective-permute-start | bytes 884744 | tf_op jit(solution)/shard_map/ppermute | solution.py:388
  58.2 0.7 fusion.20.w_qk
  59.1 2.8 %collective-permute-done.3.right_ref = bf16[2,288,256]{2,1,0:T(8,128)(2,1)S(1)} collective-permute-done((bf16[2,288,256]{2,1,0:T(8,128)(2,1)S(1)}, bf16[2,288,256]{2,1,0:T(8,128)(2,1)S(1)}, u32[]{:S(2)}, u32[]{:S(2)}) %collective-permute-start.3) | collective-permute-done | bytes 294944 | tf_op jit(solution)/shard_map/ppermute | solution.py:388
  61.9 2.3 %collective-permute-done.2.left_ref = bf16[2,288,256]{2,1,0:T(8,128)(2,1)S(1)} collective-permute-done((bf16[2,288,256]{2,1,0:T(8,128)(2,1)S(1)}, bf16[2,288,256]{2,1,0:T(8,128)(2,1)S(1)}, u32[]{:S(2)}, u32[]{:S(2)}) %collective-permute-start.2) | collective-permute-done | bytes 294944 | tf_op jit(solution)/shard_map/ppermute | solution.py:388
  64.2 0.7 copy-done.10
  64.9 41.3 %block_two.1 = bf16[8,48,256]{2,1,0:T(8,128)(2,1)} custom-call(bf16[2,64,32,256]{3,2,1,0:T(8,128)(2,1)} %block_one.1.own_ref, bf16[2,4,32,256]{3,2,1,0:T(8,128)(2,1)} %collective-permute-done.top_ref, bf16[2,4,32,256]{3,2,1,0:T(8,128)(2,1)} %collective-permute-done.1.bottom_ref, bf16[2,288,256]{2,1,0:T(8,128)(2,1)} %copy-done.10, ...), custom_call_target="tpu_custom_call" | custom-call | tf_op jit(solution)/shard_map/block_two/pallas_call | solution.py:538
  106.2 5.5 %all-to-all-start = ((bf16[4,2,48,256]{3,2,1,0:T(8,128)(2,1)}), bf16[4,2,48,256]{3,2,1,0:T(8,128)(2,1)S(1)}, u32[]{:S(2)}, u32[]{:S(2)}) async-start(bf16[4,2,48,256]{3,2,1,0:T(8,128)(2,1)} %bitcast.87), calls=%async_computation | async-start | bytes 393216 | tf_op jit(solution)/shard_map/all_to_all | solution.py:559
  111.7 0.7 fusion.24.w_qk
  112.4 0.6 copy.132
  113.1 0.6 pad.103
  113.8 0.6 pad.104
  114.4 0.8 fusion.21.x_ref
  115.2 1.0 all-to-all-done.parts_ref
  116.2 0.7 copy-done.6
  116.9 3.1 %refinement.1 = bf16[3,64,128]{2,1,0:T(8,128)(2,1)} custom-call(bf16[4,2,48,256]{3,2,1,0:T(8,128)(2,1)} %copy-done.6, bf16[16,32,256]{2,1,0:T(8,128)(2,1)} %fusion.21.x_ref, f32[1,2,8,128]{3,2,1,0:T(8,128)} %bitcast.102, bf16[128,512]{1,0:T(8,128)(2,1)} %fusion.24.w_qk, bf16[64,48]{1,0:T(8,128)(2,1)} %bitcast.100, bf16[96,32]{1,0:T(8,128)(2,1)} %bitcast.99), custom_call_target="tpu_custom_call" | custom-call | tf_op jit(solution)/shard_map/refinement/pallas_call | solution.py:573
  120.0 6.5 %all-gather = bf16[12,64,128]{2,1,0:T(8,128)(2,1)S(1)} all-gather(bf16[3,64,128]{2,1,0:T(8,128)(2,1)} %refinement.1), channel_id=2, replica_groups=mesh['var'=4,'ty'=2,'tx'=4] {'var'}, dimensions={0}, use_global_device_ids=true | all-gather | bytes 245760 | tf_op jit(solution)/shard_map/all_gather | solution.py:586
  126.5 0.8 copy.97
  (83 shorter events, 4.5 us)
Async XLA Ops:
  1.6 0.8 copy-start.13
  3.1 3.1 %copy-start.12 = (s32[64,32]{0,1:T(8,128)S(1)}, s32[64,32]{0,1:T(8,128)}, u32[]{:S(2)}) copy-start(s32[64,32]{0,1:T(8,128)} %param.12) | copy-start | bytes 24580
  3.1 3.1 %copy-start.2 = (bf16[2,360,180]{1,0,2:T(2,128)(2,1)S(1)}, bf16[2,360,180]{1,0,2:T(2,128)(2,1)}, u32[]{:S(2)}) copy-start(bf16[2,360,180]{1,0,2:T(2,128)(2,1)} %param.16) | copy-start | bytes 777604
  5.2 2.4 %copy-start.3 = (bf16[2,180,360]{2,0,1:T(2,128)(2,1)S(1)}, bf16[2,180,360]{2,0,1:T(2,128)(2,1)}, u32[]{:S(2)}) copy-start(bf16[2,180,360]{2,0,1:T(2,128)(2,1)} %param.15) | copy-start | bytes 777604
  6.2 3.1 %copy-start.7 = (bf16[2,180,180]{2,0,1:T(2,128)(2,1)S(1)}, bf16[2,180,180]{2,0,1:T(2,128)(2,1)}, u32[]{:S(2)}) copy-start(bf16[2,180,180]{2,0,1:T(2,128)(2,1)} %param.14) | copy-start | bytes 388804
  7.5 4.4 %copy-start = (bf16[64,32,180]{2,1,0:T(8,128)(2,1)S(1)}, bf16[64,32,180]{2,1,0:T(8,128)(2,1)}, u32[]{:S(2)}) copy-start(bf16[64,32,180]{2,1,0:T(8,128)(2,1)} %param.11) | copy-start | bytes 2211844
  13.3 29.2 %copy-start.8 = (bf16[9,180,48]{1,2,0:T(8,128)(2,1)S(1)}, bf16[9,180,48]{1,2,0:T(8,128)(2,1)}, u32[]{:S(2)}) copy-start(bf16[9,180,48]{1,2,0:T(8,128)(2,1)} %param.18) | copy-start | bytes 466564
  35.0 15.6 %collective-permute-start = (bf16[2,4,32,256]{3,2,1,0:T(8,128)(2,1)}, bf16[2,4,32,256]{3,2,1,0:T(8,128)(2,1)}, u32[]{:S(2)}, u32[]{:S(2)}) collective-permute-start(bf16[2,4,32,256]{3,2,1,0:T(8,128)(2,1)} %get-tuple-element.10), channel_id=1, source_target_pairs={{0,4},{1,5},{2,6},{3,7},{8,12},{9,13},{10,14},{11,15},{16,20},{17,... | collective-permute-start | bytes 393224 | tf_op jit(solution)/shard_map/ppermute | solution.py:388
  38.8 12.6 %collective-permute-start.1 = (bf16[2,4,32,256]{3,2,1,0:T(8,128)(2,1)}, bf16[2,4,32,256]{3,2,1,0:T(8,128)(2,1)}, u32[]{:S(2)}, u32[]{:S(2)}) collective-permute-start(bf16[2,4,32,256]{3,2,1,0:T(8,128)(2,1)} %get-tuple-element.9), channel_id=1, source_target_pairs={{4,0},{5,1},{6,2},{7,3},{12,8},{13,9},{14,10},{15,11},{20,16},{21,... | collective-permute-start | bytes 393224 | tf_op jit(solution)/shard_map/ppermute | solution.py:388
  45.8 2.8 %copy-start.1 = (bf16[1,180,360]{2,0,1:T(2,128)(2,1)S(1)}, bf16[1,180,360]{2,0,1:T(2,128)(2,1)}, u32[]{:S(2)}) copy-start(bf16[1,180,360]{2,0,1:T(2,128)(2,1)} %get-tuple-element.18) | copy-start | bytes 388804
  46.8 3.3 %copy-start.14 = (f32[14,225]{1,0:T(8,128)S(1)}, f32[14,225]{1,0:T(8,128)}, u32[]{:S(2)}) copy-start(f32[14,225]{1,0:T(8,128)} %copy-done.13) | copy-start | bytes 37804
  46.9 5.2 %copy-start.5 = (bf16[2,64,4,256]{3,2,1,0:T(4,128)(2,1)S(1)}, bf16[2,64,4,256]{3,2,1,0:T(4,128)(2,1)}, u32[]{:S(2)}) copy-start(bf16[2,64,4,256]{3,2,1,0:T(4,128)(2,1)} %get-tuple-element.7) | copy-start | bytes 786436
  47.7 7.0 %copy-start.4 = (bf16[2,64,4,256]{3,2,1,0:T(4,128)(2,1)S(1)}, bf16[2,64,4,256]{3,2,1,0:T(4,128)(2,1)}, u32[]{:S(2)}) copy-start(bf16[2,64,4,256]{3,2,1,0:T(4,128)(2,1)} %get-tuple-element.8) | copy-start | bytes 786436
  49.4 9.6 %copy-start.11 = (bf16[48,144]{1,0:T(8,128)(2,1)S(1)}, bf16[48,144]{1,0:T(8,128)(2,1)}, u32[]{:S(2)}) copy-start(bf16[48,144]{1,0:T(8,128)(2,1)} %param.19) | copy-start | bytes 41476
  52.5 9.5 %collective-permute-start.3 = (bf16[2,288,256]{2,1,0:T(8,128)(2,1)S(1)}, bf16[2,288,256]{2,1,0:T(8,128)(2,1)S(1)}, u32[]{:S(2)}, u32[]{:S(2)}) collective-permute-start(bf16[2,288,256]{2,1,0:T(8,128)(2,1)S(1)} %reshape.527), channel_id=1, source_target_pairs={{1,0},{2,1},{3,2},{5,4},{6,5},{7,6},{9,8},{10,9},{11,10},{13,12},{... | collective-permute-start | bytes 884744 | tf_op jit(solution)/shard_map/ppermute | solution.py:388
  55.0 9.2 %collective-permute-start.2 = (bf16[2,288,256]{2,1,0:T(8,128)(2,1)S(1)}, bf16[2,288,256]{2,1,0:T(8,128)(2,1)S(1)}, u32[]{:S(2)}, u32[]{:S(2)}) collective-permute-start(bf16[2,288,256]{2,1,0:T(8,128)(2,1)S(1)} %reshape.526), channel_id=1, source_target_pairs={{0,1},{1,2},{2,3},{4,5},{5,6},{6,7},{8,9},{9,10},{10,11},{12,13},{... | collective-permute-start | bytes 884744 | tf_op jit(solution)/shard_map/ppermute | solution.py:388
  61.9 2.3 %copy-start.9 = (bf16[2,288,256]{2,1,0:T(8,128)(2,1)}, bf16[2,288,256]{2,1,0:T(8,128)(2,1)S(1)}, u32[]{:S(2)}) copy-start(bf16[2,288,256]{2,1,0:T(8,128)(2,1)S(1)} %collective-permute-done.3.right_ref) | copy-start | bytes 884740
  64.2 0.7 copy-start.10
  64.9 48.8 %copy-start.15 = (bf16[48,48]{1,0:T(8,128)(2,1)S(1)}, bf16[48,48]{1,0:T(8,128)(2,1)}, u32[]{:S(2)}) copy-start(bf16[48,48]{1,0:T(8,128)(2,1)} %param.20) | copy-start | bytes 13828
  106.2 10.0 %all-to-all-start = ((bf16[4,2,48,256]{3,2,1,0:T(8,128)(2,1)}), bf16[4,2,48,256]{3,2,1,0:T(8,128)(2,1)S(1)}, u32[]{:S(2)}, u32[]{:S(2)}) async-start(bf16[4,2,48,256]{3,2,1,0:T(8,128)(2,1)} %bitcast.87), calls=%async_computation | async-start | bytes 393216 | tf_op jit(solution)/shard_map/all_to_all | solution.py:559
  116.2 0.7 copy-start.6

commit v2 on v0

v2 whole, which is shorter than its diff:
```python
import functools

import jax
import jax.numpy as jnp
from jax import lax
from jax.experimental import pallas as pl
from jax.experimental.pallas import tpu as pltpu
from jax.sharding import PartitionSpec as P

WIN = 8
CELLS = WIN * WIN
SHIFT = 4
SCALE = 4
VAR_DEV = 2
LANES = 128
HEAD_ROWS = 32
CLASSES = 4
MARKS = CLASSES + 2
SIDE = 2 * WIN - 1

EPSILON = 1e-05
LOG2E = 1.4426950408889634
BIG = float(2.0**100)
ERF_TANH = (
    7.97884207935252e-01,
    3.63342879e-02,
    -3.31288562e-05,
    -5.52410746e-05,
    3.96927395e-06,
    -1.33457816e-07,
    1.80588519e-09,
)

NN = (((1,), (0,)), ((), ()))
NT = (((1,), (1,)), ((), ()))
F32 = jnp.float32
BF16 = jnp.bfloat16


def dot(a, b, dims=NN):
    return lax.dot_general(a, b, dims, preferred_element_type=F32)


def iota(shape, dim):
    return lax.broadcasted_iota(jnp.int32, shape, dim)


def round_up(size, multiple):
    return -(-size // multiple) * multiple


def one_hot(condition):
    return jnp.where(condition, 1.0, 0.0).astype(BF16)


def exact(a, b, dims=NN):
    return dot(a, b, dims).astype(BF16)


def pad_matrix(rows, size):
    return one_hot(iota((rows, size), 0) == iota((rows, size), 1))


def head_matrix(rows, size, heads, width, first=0):
    row = iota((rows, size), 0)
    unit = row % HEAD_ROWS
    source = first + row // HEAD_ROWS * width + unit
    keep = (unit < width) & (row < heads * HEAD_ROWS)
    return one_hot(keep & (iota((rows, size), 1) == source))


def query_labels(rows, lanes, first_row, first_lane):
    row = iota((rows, lanes), 0) - first_row
    lane = iota((rows, lanes), 1) - first_lane
    is_class = (row >= 0) & (row < CLASSES)
    is_pad = row == CLASSES
    same = is_class & (row == lane)
    always = lane == CLASSES + 1
    return jnp.where(same, BIG, 0.0) - jnp.where(always & (is_class | is_pad), BIG, 0.0)


def key_labels(rows, lanes, first_row, first_lane):
    row = iota((rows, lanes), 0) - first_row
    lane = iota((rows, lanes), 1) - first_lane
    is_class = (lane >= 0) & (lane < CLASSES)
    is_pad = lane == CLASSES
    add = is_class & (row == lane) | is_pad & (row == CLASSES + 1)
    return jnp.where(add, 1.0, 0.0) - jnp.where(is_pad & (row == CLASSES), 1.0, 0.0)


def bias_rows(table, turn, flip_rows, flip_cols):
    shape = (1, WIN * LANES)
    lane = iota(shape, 1)
    row_step = lane % LANES // WIN - (WIN - 1)
    col_step = lane % WIN - lane // LANES
    row_step = jnp.where(flip_rows, -row_step, row_step)
    col_step = jnp.where(flip_cols, -col_step, col_step)
    lead = jnp.where(turn, col_step, row_step)
    trail = jnp.where(turn, row_step, col_step)
    index = (lead + WIN - 1) * SIDE + trail + WIN - 1
    pick = one_hot(iota((table.shape[1], WIN * LANES), 0) == index)
    rest = table * LOG2E
    parts = []
    for _ in range(3):
        parts.append(rest.astype(BF16))
        rest = rest - parts[-1].astype(F32)
    moved = dot(jnp.concatenate(parts, axis=0), pick)
    size = table.shape[0]
    return moved[:size] + moved[size : 2 * size] + moved[2 * size :]


def bias_grid(rows, rows_ref, store):
    heads = rows.shape[0]
    for key_col in range(WIN):
        rows_ref[0:heads, key_col, :] = rows[:, key_col * LANES : (key_col + 1) * LANES]
    half = iota((WIN, LANES), 1)
    for pair in range(heads // 2):
        even, odd = rows_ref[2 * pair], rows_ref[2 * pair + 1]
        for key_row in range(WIN):
            start = (WIN - 1 - key_row) * WIN
            left = pltpu.roll(even, (LANES - start) % LANES, 1)
            right = pltpu.roll(odd, (LANES - start + CELLS) % LANES, 1)
            store(key_row, pair, jnp.where(half < CELLS, left, right))


def prepare_kernel(
    heads,
    channels,
    codes_ref,
    packed_ref,
    swin_bias_ref,
    recon_ref,
    refine_qkv_ref,
    refine_proj_ref,
    refine_bias_ref,
    qvt_out,
    key_out,
    proj_out,
    up_out,
    down_out,
    recon_out,
    bias_out,
    refine_qvt_out,
    refine_key_out,
    refine_proj_out,
    refine_bias_out,
    rows_ref,
    tables_ref,
):
    blocks = packed_ref.shape[0]
    width = channels // heads
    lanes = key_out.shape[1]
    hidden = up_out.shape[2]
    head_rows = heads * HEAD_ROWS
    mark_rows = head_rows + 16
    picked = head_matrix(lanes, lanes, heads, width)
    shape = (2 * LANES, lanes)
    row = iota(shape, 0)
    head, unit = row % LANES // HEAD_ROWS * 2 + row // LANES, row % HEAD_ROWS
    proj_rows = one_hot((head < heads) & (unit < width) & (iota(shape, 1) == head * width + unit))
    identity = one_hot(iota((hidden, hidden), 0) == iota((hidden, hidden), 1))
    query_add = query_labels(mark_rows, lanes, head_rows, channels)
    key_add = key_labels(lanes, lanes, channels, head_rows)
    for i in range(blocks):
        at = [0]

        def piece(size):
            at[0] += size
            return packed_ref[i, :, at[0] - size : at[0]]

        query, key, value, proj = (piece(lanes) for _ in range(4))
        qvt_out[i, :mark_rows] = (dot(picked[:mark_rows], query, NT) + query_add).astype(BF16)
        qvt_out[i, mark_rows:] = exact(picked[:head_rows], value, NT)
        key_out[i] = (dot(key, picked, NT) + key_add).astype(BF16)
        proj_out[i] = exact(proj_rows, proj)
        up_out[i] = piece(hidden)
        down_out[i] = exact(identity, piece(hidden), NT)

    taps, out, _ = recon_ref.shape
    kernel = recon_ref[...].reshape(taps * out, channels)
    pad = one_hot(iota((lanes, channels), 0) == iota((lanes, channels), 1))
    for i in range(blocks):
        tables_ref[i * heads : (i + 1) * heads] = swin_bias_ref[:, i]
    for v in range(VAR_DEV):
        code = codes_ref[v]
        turn, flip_rows, flip_cols = code // 4 == 1, code // 2 % 2 == 1, code % 2 == 1
        rows = bias_rows(tables_ref[: blocks * heads], turn, flip_rows, flip_cols)
        tables = [rows[i * heads : (i + 1) * heads] for i in range(blocks)]
        for i in range(blocks):

            def store(key_row, pair, value):
                bias_out[
                    i,
                    v,
                    key_row * WIN : (key_row + 1) * WIN,
                    pair * LANES : (pair + 1) * LANES,
                ] = value

            bias_grid(tables[i], rows_ref, store)
        shape = (3 * lanes, 1)
        row = iota(shape, 0)
        row_step = row // lanes - 1
        lane = row % lanes
        col_step = jnp.where(lane >= LANES, 1, jnp.where(lane >= out, 0, -1))
        channel = jnp.where(lane >= LANES, lane - LANES, jnp.where(lane >= out, lane - out, lane))
        row_step = jnp.where(flip_rows, -row_step, row_step)
        col_step = jnp.where(flip_cols, -col_step, col_step)
        tap = (jnp.where(turn, col_step, row_step) + 1) * 3
        tap = tap + jnp.where(turn, row_step, col_step) + 1
        sub_row = channel % (SCALE * SCALE) // SCALE
        sub_col = channel % SCALE
        sub_row = jnp.where(flip_rows, SCALE - 1 - sub_row, sub_row)
        sub_col = jnp.where(flip_cols, SCALE - 1 - sub_col, sub_col)
        source = channel // (SCALE * SCALE) * SCALE * SCALE
        source = source + jnp.where(turn, sub_col, sub_row) * SCALE
        source = tap * out + source + jnp.where(turn, sub_row, sub_col)
        source = jnp.where(channel < out, source, -1)
        moved = exact(one_hot(iota((3 * lanes, taps * out), 1) == source), kernel)
        recon_out[v] = exact(pad, moved, NT)

    refine_heads = refine_bias_ref.shape[0]
    refine_width = out // refine_heads
    never = codes_ref[0] < 0
    rows = bias_rows(refine_bias_ref[...], never, never, never)

    def store_refine(key_row, pair, value):
        refine_bias_out[key_row * WIN : (key_row + 1) * WIN] = value

    bias_grid(rows, rows_ref, store_refine)
    refine_rows = refine_heads * HEAD_ROWS
    values = head_matrix(refine_rows, 3 * out, refine_heads, refine_width, 2 * out)
    queries = head_matrix(refine_rows + 16, 3 * out, refine_heads, refine_width)
    keys = head_matrix(LANES, 3 * out, refine_heads, refine_width, out)
    out_pad = one_hot(iota((LANES, out), 0) == iota((LANES, out), 1))
    weight = refine_qkv_ref[...]
    mark = channels % LANES
    refine_qvt_out[: refine_rows + 16] = (
        dot(exact(queries, weight, NT), out_pad, NT)
        + query_labels(refine_rows + 16, LANES, refine_rows, mark)
    ).astype(BF16)
    refine_qvt_out[refine_rows + 16 :] = exact(exact(values, weight, NT), out_pad, NT)
    refine_key_out[...] = (
        dot(out_pad, exact(keys, weight, NT), NT) + key_labels(LANES, LANES, mark, refine_rows)
    ).astype(BF16)
    for h in range(refine_heads):
        shape = (LANES, out)
        row = iota(shape, 0)
        rows = one_hot((row < refine_width) & (iota(shape, 1) == row + h * refine_width))
        square = dot(exact(rows, refine_proj_ref[...]), out_pad, NT)
        refine_proj_out[h * out : (h + 1) * out] = square.T[:out].astype(BF16)


def gelu(x):
    square = x * x
    series = jnp.full_like(square, ERF_TANH[-1])
    for factor in ERF_TANH[-2::-1]:
        series = series * square + factor
    half = 0.5 * x
    return half + half * jnp.tanh(x * series)


def normalize(x, channels):
    inside = iota((1, x.shape[1]), 1) < channels
    mean = jnp.sum(jnp.where(inside, x, 0.0), axis=1, keepdims=True) * (1.0 / channels)
    centred = jnp.where(inside, x - mean, 0.0)
    spread = jnp.sum(centred * centred, axis=1, keepdims=True) * (1.0 / channels)
    return jnp.where(inside, centred * lax.rsqrt(spread + EPSILON), x).astype(BF16)


def split_queries(queries, heads):
    pairs = heads // 2
    head_rows = heads * HEAD_ROWS
    left = iota((1, LANES), 1) < CELLS
    turned = pltpu.roll(queries, CELLS, 1).astype(BF16)
    queries = queries.astype(BF16)
    depth = round_up(queries.shape[0], LANES)
    zero = jnp.zeros((HEAD_ROWS, LANES), BF16)
    results = []
    for even, odd in ((queries, turned), (turned, queries)):
        marks = jnp.where(left, even[head_rows:], odd[head_rows:])
        columns = []
        for pair in range(pairs):
            at = pair * 2 * HEAD_ROWS
            rows = [zero] * heads
            rows[2 * pair] = jnp.where(left, even[at : at + HEAD_ROWS], zero)
            rows[2 * pair + 1] = jnp.where(left, zero, odd[at + HEAD_ROWS : at + 2 * HEAD_ROWS])
            rows.append(marks)
            rows.append(jnp.zeros((depth - queries.shape[0], LANES), BF16))
            columns.append(jnp.concatenate(rows, axis=0))
        results.append(jnp.concatenate(columns, axis=1) if pairs > 1 else columns[0])
    return results


def heads_of(n, scale, heads, width, w_qvt, w_key):
    mark_rows = heads * HEAD_ROWS + 16
    both = dot(w_qvt, n, NT)
    row = iota((mark_rows, 1), 0)
    queries = both[:mark_rows] * jnp.where(row < heads * HEAD_ROWS, scale, 1.0)
    values = both[mark_rows:]
    row = iota((heads * HEAD_ROWS, 1), 0) % HEAD_ROWS
    values = jnp.where(row == width, 1.0, values).astype(BF16)
    keys = dot(n, w_key).astype(BF16)
    scores = []
    for place in range(n.shape[0] // LANES):
        cut = slice(place * LANES, (place + 1) * LANES)
        for half, stationary in enumerate(split_queries(queries[:, cut], heads)):
            at = place * LANES + half * CELLS
            scores.append(dot(keys[at : at + CELLS], stationary))
    return scores, values


def soft(scores):
    largest = jnp.max(scores, axis=0, keepdims=True)
    return jnp.exp2(scores - largest).astype(BF16)


def mix_pair(values, first, second, heads, ones_row):
    zero = jnp.zeros((CELLS, LANES), BF16)
    lane = iota((HEAD_ROWS, 2 * LANES), 1) % LANES
    mixed = []
    for pair in range(heads // 2):
        cut = slice(pair * LANES, (pair + 1) * LANES)
        stationary = jnp.concatenate(
            [
                jnp.concatenate([first[:, cut], zero], axis=1),
                jnp.concatenate([zero, second[:, cut]], axis=1),
            ],
            axis=0,
        )
        result = dot(values[pair * CELLS : (pair + 1) * CELLS], stationary)
        joined = jnp.where(lane < CELLS, result[:HEAD_ROWS], result[HEAD_ROWS:])
        mixed.append(joined * pl.reciprocal(joined[ones_row : ones_row + 1]))
    return mixed


def swin_block(x, pairs, heads, channels, bias, w_qvt, w_key, w_proj, w_up, w_down):
    width = channels // heads
    n = normalize(x, channels)
    scale = width**-0.5 * LOG2E
    scores, values = heads_of(n, scale, heads, width, w_qvt[...], w_key[...])
    pad = jnp.zeros((LANES - heads // 2 * HEAD_ROWS, 2 * LANES), F32)
    weights = [
        (soft(scores[2 * place] + bias(a)), soft(scores[2 * place + 1] + bias(b)))
        for place, a, b in pairs
    ]
    blocks = []
    for (place, _, _), (first, second) in zip(pairs, weights):
        cut = slice(place * LANES, (place + 1) * LANES)
        mixed = mix_pair(values[:, cut], first, second, heads, width)
        blocks.append(jnp.concatenate(mixed + [pad], axis=0).astype(BF16))
    outputs = []
    for block in blocks:
        for half in range(2):
            turned = block[:, half * LANES : (half + 1) * LANES].T
            outputs.append(jnp.concatenate([turned[:CELLS], turned[CELLS:]], axis=1))
    outputs = jnp.concatenate(outputs, axis=0)
    places = [place for place, _, _ in pairs]
    if places != list(range(x.shape[0] // LANES)):
        x = jnp.concatenate([x[place * LANES : (place + 1) * LANES] for place in places], axis=0)
    h = (x + dot(outputs, w_proj[...])).astype(BF16).astype(F32)
    hidden = gelu(dot(normalize(h, channels), w_up[...])).astype(BF16)
    y = h + dot(hidden, w_down[...])
    return [y[i * LANES : (i + 1) * LANES] for i in range(len(pairs))]


def windows_of(grid):
    lanes = grid.shape[2]
    return jnp.concatenate(
        [
            grid[:, w * WIN : (w + 1) * WIN].reshape(CELLS, lanes)
            for w in range(grid.shape[1] // WIN)
        ],
        axis=0,
    )


def first_kernel(
    heads, channels, ends, xa_ref, xb_ref, labels_ref, bias_ref, *refs
):
    *weights, y_ref, left_ref, right_ref = refs[:8]
    held, side = refs[-2:]
    step = pl.program_id(0)
    breadth = xa_ref.shape[1]
    count = breadth // WIN
    tokens, lanes = held.shape
    part = tokens // 2
    rows_total = labels_ref.shape[1]
    strips = (0, rows_total // WIN - 1) if ends else (2 * step + 1, 2 * step + 2)
    for k, ref in enumerate((xa_ref, xb_ref)):
        held[k * part : (k + 1) * part, :channels] = windows_of(ref[...].astype(F32))
    token = iota((tokens, rows_total), 0)
    strip = jnp.where(token < part, strips[0], strips[1])
    at_row = strip * WIN + token % CELLS // WIN == iota((tokens, rows_total), 1)
    by_row = dot(one_hot(at_row), labels_ref[...].astype(F32).astype(BF16), NT)
    token = iota((tokens, breadth), 0)
    at_col = token % part // CELLS * WIN + token % WIN == iota((tokens, breadth), 1)
    label = dot(jnp.where(at_col, by_row, 0.0).astype(BF16), jnp.ones((breadth, LANES), BF16))
    lane = iota((tokens, LANES), 1) - channels % LANES
    marks = jnp.where(
        (label == (lane + 1).astype(F32)) & (lane < CLASSES)
        | (lane >= CLASSES) & (lane < MARKS),
        1.0,
        0.0,
    )
    tail = jnp.where(lane < 0, held[:, lanes - LANES :], marks)
    x = jnp.concatenate([held[:, : lanes - LANES], tail], axis=1)
    places = tokens // LANES
    pairs = [(place, v, v) for v in range(VAR_DEV) for place in range(places)]
    results = swin_block(x, pairs, heads, channels, lambda v: bias_ref[v], *weights)
    for v in range(VAR_DEV):
        for k in range(2):
            windows = []
            for w in range(count):
                group = k * count + w
                block = results[v * places + group // 2]
                at = group % 2 * CELLS
                windows.append(block[at : at + CELLS].reshape(WIN, WIN, lanes))
            y_ref[v, k * WIN : (k + 1) * WIN] = jnp.concatenate(windows, axis=1).astype(BF16)
            at = k * WIN * SHIFT
            for r in range(WIN):
                rows = slice(at + r * SHIFT, at + (r + 1) * SHIFT)
                side[0, rows] = windows[0][r, :SHIFT]
                side[1, rows] = windows[-1][r, SHIFT:]
        left_ref[v] = side[0].astype(BF16)
        right_ref[v] = side[1].astype(BF16)
    if ends:
        top_ref, bottom_ref = refs[8:10]
        top_ref[...] = y_ref[:, :SHIFT]
        bottom_ref[...] = y_ref[:, 2 * WIN - SHIFT :]


def place_rows(store, ends_ref, middle_ref, v):
    store(0, ends_ref[v, :WIN])
    for r in range(0, middle_ref.shape[1], WIN):
        store(WIN + r, middle_ref[v, r : r + WIN])
    store(WIN + middle_ref.shape[1], ends_ref[v, WIN:])


def inner_kernel(
    heads, channels, group, ends_ref, middle_ref, bias_ref, *refs
):
    *weights, y_ref, marks_ref, held, x_held = refs
    height, breadth, lanes = held.shape
    count = breadth // WIN - 1

    @pl.when(pl.program_id(0) == 0)
    def _():
        for v in range(VAR_DEV):

            def store(first, rows):
                rows = rows.astype(F32)
                held[first : first + WIN] = rows
                if v == 0:
                    marks_ref[first // WIN] = windows_of(rows[:, :, lanes - LANES :]).astype(BF16)

            place_rows(store, ends_ref, middle_ref, v)
            for strip in range(height // WIN - 1):
                rows = slice(strip * WIN + SHIFT, (strip + 1) * WIN + SHIFT)
                for w in range(count):
                    at = SHIFT + w * WIN
                    x_held[strip * count + w, v] = held[rows, at : at + WIN].reshape(CELLS, lanes)

    base = pl.program_id(0) * group
    x = x_held[pl.ds(base, group)].reshape(group * VAR_DEV * CELLS, lanes)
    pairs = [(w, 0, 1) for w in range(group)]
    results = swin_block(x, pairs, heads, channels, lambda v: bias_ref[v], *weights)
    for w in range(group):
        y_ref[w] = results[w].astype(BF16).reshape(VAR_DEV, CELLS, lanes)


def outer_kernel(
    heads,
    channels,
    group,
    ends_ref,
    middle_ref,
    top_ref,
    bottom_ref,
    left_ref,
    right_ref,
    inner_ref,
    bias_ref,
    *refs,
):
    *weights, w_recon, out_ref, rows_held, sides_held, x_held, y_held, acc = refs
    lanes = middle_ref.shape[3]
    height, breadth = middle_ref.shape[1] + 2 * WIN, middle_ref.shape[2]
    tall, wide = height + 2 * SHIFT, breadth + 2 * SHIFT
    strips, count = tall // WIN, wide // WIN
    always = iota((1, lanes), 1) == channels + CLASSES + 1

    def marked(received):
        return jnp.where(always, 1.0, received.astype(F32))

    for v in range(VAR_DEV):
        for end in range(2):
            outside, inside = (0, SHIFT) if end == 0 else (SHIFT, 0)
            corner = 0 if end == 0 else (tall - SHIFT) * SHIFT
            received = top_ref if end == 0 else bottom_ref
            first = 0 if end == 0 else 2 * WIN - SHIFT
            across = slice(SHIFT, SHIFT + breadth)
            rows_held[outside : outside + SHIFT, across] = marked(received[v])
            rows_held[inside : inside + SHIFT, across] = ends_ref[
                v, first : first + SHIFT
            ].astype(F32)
            side_first = SHIFT * SHIFT if end == 0 else (tall - 2 * SHIFT) * SHIFT
            for ref, at in ((left_ref, 0), (right_ref, wide - SHIFT)):
                for rows, start in ((outside, corner), (inside, side_first)):
                    piece = marked(ref[v, start : start + SHIFT * SHIFT])
                    rows_held[rows : rows + SHIFT, at : at + SHIFT] = piece.reshape(
                        SHIFT, SHIFT, lanes
                    )
            for w in range(count):
                x_held[end * count + w, v] = rows_held[:, w * WIN : (w + 1) * WIN].reshape(
                    CELLS, lanes
                )

        def store(first, rows):
            sides_held[first : first + WIN, :WIN] = rows[:, :WIN].astype(F32)
            sides_held[first : first + WIN, WIN:] = rows[:, breadth - WIN :].astype(F32)

        place_rows(store, ends_ref, middle_ref, v)
        for strip in range(1, strips - 1):
            rows = slice(strip * WIN - SHIFT, (strip + 1) * WIN - SHIFT)
            cut = slice(strip * WIN * SHIFT, (strip + 1) * WIN * SHIFT)
            for end in range(2):
                ref = left_ref if end == 0 else right_ref
                piece = marked(ref[v, cut]).reshape(WIN, SHIFT, lanes)
                at = 0 if end == 0 else WIN + SHIFT
                own = sides_held[rows, at : at + SHIFT]
                both = [piece, own] if end == 0 else [own, piece]
                slot = 2 * count + 2 * (strip - 1) + end
                x_held[slot, v] = jnp.concatenate(both, axis=1).reshape(CELLS, lanes)

    slots = x_held.shape[0]

    def border(step, carry):
        x = x_held[pl.ds(step * group, group)].reshape(group * VAR_DEV * CELLS, lanes)
        pairs = [(w, 0, 1) for w in range(group)]
        results = swin_block(x, pairs, heads, channels, lambda v: bias_ref[v], *weights)
        at = channels + CLASSES
        for w in range(group):
            block = x[w * LANES : (w + 1) * LANES]
            y = results[w] * block[:, at : at + 1]
            y_held[step * group + w] = y.astype(BF16).reshape(VAR_DEV, CELLS, lanes)
        return carry

    lax.fori_loop(0, slots // group, border, 0)

    acc[...] = jnp.zeros_like(acc)

    def scatter(strip, windows):
        total = None
        for v in range(VAR_DEV):
            part = dot(jnp.concatenate(windows(v), axis=0), w_recon[v])
            total = part if total is None else total + part
        total = total.reshape(count, WIN, WIN, 3 * lanes)
        for e in range(3):
            for w in range(count):
                acc[pl.ds(strip * WIN + 2 - e, WIN), w * WIN : (w + 1) * WIN] += total[
                    w, :, :, e * lanes : (e + 1) * lanes
                ]

    def middle(strip, carry):
        slot = 2 * count + 2 * (strip - 1)
        first = (strip - 1) * (count - 2)
        scatter(
            strip,
            lambda v: [
                y_held[slot, v],
                *[inner_ref[first + w, v] for w in range(count - 2)],
                y_held[slot + 1, v],
            ],
        )
        return carry

    scatter(0, lambda v: [y_held[w, v] for w in range(count)])
    lax.fori_loop(1, strips - 1, middle, 0)
    scatter(strips - 1, lambda v: [y_held[count + w, v] for w in range(count)])

    out_channels = out_ref.shape[1]

    def finish(strip, carry):
        rows = pl.ds(1 + SHIFT + strip * WIN, WIN)
        centre = acc[rows, SHIFT : SHIFT + breadth, :LANES]
        centre = pltpu.roll(centre.reshape(WIN * breadth, LANES), LANES - out_channels, 1)
        result = (
            acc[rows, SHIFT - 1 : SHIFT - 1 + breadth, :LANES]
            + centre.reshape(WIN, breadth, LANES)
            + acc[rows, SHIFT + 1 : SHIFT + 1 + breadth, LANES : 2 * LANES]
        )
        out_ref[strip] = windows_of(result).T[:out_channels].astype(BF16)
        return carry

    lax.fori_loop(0, height // WIN, finish, 0)


def refine_kernel(
    heads, first_mark, place_ref, parts_ref, marks_ref, bias_ref, w_qvt, w_key, w_projt, out_ref, final
):
    sources, strips, channels, strip_tokens = parts_ref.shape
    breadth = strip_tokens // WIN
    width = channels // heads
    z = jnp.concatenate(
        [
            sum(parts_ref[s, strip].astype(F32) for s in range(sources))
            for strip in range(strips)
        ],
        axis=1,
    ) * (1.0 / (sources * VAR_DEV))
    mean = jnp.sum(z, axis=0, keepdims=True) * (1.0 / channels)
    centred = z - mean
    spread = jnp.sum(centred * centred, axis=0, keepdims=True) * (1.0 / channels)
    normed = centred * lax.rsqrt(spread + EPSILON)
    tall = jnp.concatenate([normed, jnp.zeros((LANES - channels, normed.shape[1]), F32)], axis=0)
    marks = jnp.concatenate([marks_ref[s].astype(F32) for s in range(strips)], axis=0)
    lane = iota((1, LANES), 1)
    is_mark = (lane >= first_mark) & (lane < first_mark + MARKS)
    n = jnp.where(is_mark, marks, tall.T).astype(BF16)
    scores, values = heads_of(
        n, width**-0.5 * LOG2E, heads, width, w_qvt[...], w_key[...]
    )
    probabilities = [soft(s + bias_ref[...]) for s in scores]
    lane = iota((channels, LANES), 1)
    branches = []
    for pair in range(len(probabilities) // 2):
        mixed = mix_pair(
            values[:, pair * LANES : (pair + 1) * LANES],
            probabilities[2 * pair],
            probabilities[2 * pair + 1],
            heads,
            width,
        )[0].astype(BF16)
        both = dot(w_projt[...][:, :HEAD_ROWS], mixed)
        even, odd = both[:channels], both[channels:]
        halves = []
        for half in range(2):
            cut = slice(half * LANES, (half + 1) * LANES)
            halves.append(even[:, cut] + pltpu.roll(odd[:, cut], CELLS, 1))
        branches.append(jnp.where(lane < CELLS, halves[0], pltpu.roll(halves[1], CELLS, 1)))
    refined = (z + jnp.concatenate(branches, axis=1)).astype(BF16)
    stacked = jnp.concatenate(
        [refined[:, s * strip_tokens : (s + 1) * strip_tokens] for s in range(strips)], axis=0
    )
    shape = (strip_tokens, WIN * breadth * SCALE)
    cell = iota(shape, 1) // SCALE
    source = (cell % breadth // WIN) * CELLS + (cell // breadth) * WIN + cell % WIN
    wide = dot(stacked, one_hot(iota(shape, 0) == source))
    own = iota(wide.shape, 1) % SCALE == iota(wide.shape, 0) % SCALE
    wide = jnp.where(own, wide, 0.0).astype(BF16)
    shape = (wide.shape[0] // SCALE, wide.shape[0])
    folded = dot(one_hot(iota(shape, 1) // SCALE == iota(shape, 0)), wide)
    colours = channels // (SCALE * SCALE)
    row_lanes = breadth * SCALE
    for s in range(strips):
        for c in range(colours):
            first = (s * colours + c) * SCALE
            for y in range(WIN):
                start = (s * WIN + y) * SCALE
                final[c, start : start + SCALE] = folded[
                    first : first + SCALE, y * row_lanes : (y + 1) * row_lanes
                ]
    out_ref[...] = final[...].astype(BF16)


def exchanged(last, first, axis):
    count = lax.axis_size(axis)
    up = [(i, i + 1) for i in range(count - 1)]
    down = [(i + 1, i) for i in range(count - 1)]
    if count != 2:
        return lax.ppermute(last, axis, up), lax.ppermute(first, axis, down)
    at_start = lax.axis_index(axis) == 0
    received = lax.ppermute(jnp.where(at_start, last, first), axis, up + down)
    zero = jnp.zeros_like(received)
    return jnp.where(at_start, zero, received), jnp.where(at_start, received, zero)


def whole(a):
    return pl.BlockSpec(a.shape, lambda *i: (0,) * a.ndim)


def params():
    return pltpu.CompilerParams(
        dimension_semantics=("arbitrary",), vmem_limit_bytes=56 * 1024 * 1024
    )


def local(
    features,
    labels,
    qkv_weight,
    proj_weight,
    up_weight,
    down_weight,
    swin_bias,
    recon_weight,
    refine_qkv,
    refine_proj,
    refine_bias,
):
    height, breadth, channels = features.shape
    heads = swin_bias.shape[1]
    out_channels = recon_weight.shape[-1]
    refine_heads = refine_bias.shape[0]
    lanes = round_up(channels + MARKS, LANES)
    hidden = round_up(up_weight.shape[-1], LANES)
    position = lax.axis_index("var")
    codes = position * VAR_DEV + jnp.arange(VAR_DEV, dtype=jnp.int32)

    def widen(weight, size):
        return jnp.pad(weight, ((0, 0), (0, lanes - channels), (0, size - weight.shape[2])))

    packed = jnp.concatenate(
        [
            *[
                widen(qkv_weight[:, :, i * channels : (i + 1) * channels], lanes)
                for i in range(3)
            ],
            widen(proj_weight, lanes),
            widen(up_weight, hidden),
            widen(jnp.swapaxes(down_weight, 1, 2), hidden),
        ],
        axis=2,
    )
    operands = (
        codes,
        packed,
        jnp.swapaxes(swin_bias, 0, 1),
        jnp.swapaxes(recon_weight, 1, 2),
        refine_qkv,
        refine_proj,
        refine_bias,
    )
    head_rows, refine_rows = heads * HEAD_ROWS, refine_heads * HEAD_ROWS
    shapes = [
        ((2, 2 * head_rows + 16, lanes), BF16),
        ((2, lanes, lanes), BF16),
        ((2, 2 * LANES, lanes), BF16),
        ((2, lanes, hidden), BF16),
        ((2, hidden, lanes), BF16),
        ((VAR_DEV, lanes, 3 * lanes), BF16),
        ((2, VAR_DEV, CELLS, heads * CELLS), F32),
        ((2 * refine_rows + 16, LANES), BF16),
        ((LANES, LANES), BF16),
        ((refine_heads * out_channels, LANES), BF16),
        ((CELLS, refine_heads * CELLS), F32),
    ]
    shapes = [jax.ShapeDtypeStruct(*s) for s in shapes]
    prepared = pl.pallas_call(
        functools.partial(prepare_kernel, heads, channels),
        grid=(1,),
        in_specs=[pl.BlockSpec(memory_space=pltpu.SMEM)] + [whole(a) for a in operands[1:]],
        out_specs=[whole(s) for s in shapes],
        out_shape=shapes,
        scratch_shapes=[
            pltpu.VMEM((heads, WIN, LANES), F32),
            pltpu.VMEM((round_up(2 * heads, 8), swin_bias.shape[2]), F32),
        ],
        compiler_params=params(),
        name="prepare",
    )(*operands)
    *swin, recon, bias, refine_qvt, refine_key, refine_projt, refine_grid = prepared

    def block_specs(i):
        arrays = (bias, *swin)
        return arrays, [
            pl.BlockSpec((None,) + a.shape[1:], lambda *_, n=a.ndim: (i,) + (0,) * (n - 1))
            for a in arrays
        ]

    def cost(windows):
        return pl.CostEstimate(
            flops=windows * 400_000_000, bytes_accessed=windows * 200_000, transcendentals=0
        )

    arrays, specs = block_specs(0)
    strips = height // WIN
    tokens = WIN * breadth
    side_rows = 2 * WIN * SHIFT
    labels_across = labels.T

    def block_one(ends):
        steps = 1 if ends else strips // 2 - 1
        first = (lambda i: 0) if ends else (lambda i: 2 * i + 1)
        second = (lambda i: strips - 1) if ends else (lambda i: 2 * i + 2)
        outs = [
            ((VAR_DEV, steps * 2 * WIN, breadth, lanes), BF16),
            ((VAR_DEV, steps * side_rows, lanes), BF16),
            ((VAR_DEV, steps * side_rows, lanes), BF16),
        ]
        out_specs = [
            pl.BlockSpec((VAR_DEV, 2 * WIN, breadth, lanes), lambda i: (0, i, 0, 0)),
            pl.BlockSpec((VAR_DEV, side_rows, lanes), lambda i: (0, i, 0)),
            pl.BlockSpec((VAR_DEV, side_rows, lanes), lambda i: (0, i, 0)),
        ]
        if ends:
            outs += [((VAR_DEV, SHIFT, breadth, lanes), BF16)] * 2
            out_specs += [
                pl.BlockSpec((VAR_DEV, SHIFT, breadth, lanes), lambda i: (0, 0, 0, 0))
            ] * 2
        return pl.pallas_call(
            functools.partial(first_kernel, heads, channels, ends),
            grid=(steps,),
            in_specs=[
                pl.BlockSpec((WIN, breadth, channels), lambda i: (first(i), 0, 0)),
                pl.BlockSpec((WIN, breadth, channels), lambda i: (second(i), 0, 0)),
                whole(labels_across),
                *specs,
            ],
            out_specs=out_specs,
            out_shape=[jax.ShapeDtypeStruct(*o) for o in outs],
            scratch_shapes=[
                pltpu.VMEM((2 * tokens, lanes), F32),
                pltpu.VMEM((2, side_rows, lanes), F32),
            ],
            compiler_params=params(),
            cost_estimate=cost(steps * breadth // WIN * 4),
            name="block_one_ends" if ends else "block_one_middle",
        )(features, features, labels_across, *arrays)

    y_ends, left_ends, right_ends, top_own, bottom_own = block_one(True)
    top, bottom = exchanged(bottom_own, top_own, "ty")
    y_middle, left_middle, right_middle = block_one(False)
    half = side_rows // 2
    strips_out = []
    for ends, middle, cut in (
        (right_ends, right_middle, slice(breadth - SHIFT, breadth)),
        (left_ends, left_middle, slice(0, SHIFT)),
    ):
        corners = [a[:, :, cut].reshape(VAR_DEV, SHIFT * SHIFT, lanes) for a in (top, bottom)]
        strips_out.append(
            jnp.concatenate(
                [corners[0], ends[:, :half], middle, ends[:, half:], corners[1]], axis=1
            )
        )
    sides = exchanged(*strips_out, "tx")

    arrays, specs = block_specs(1)
    inner_count = (strips - 1) * (breadth // WIN - 1)
    group = next(g for g in range(7, 0, -1) if inner_count % g == 0)
    inner, marks = pl.pallas_call(
        functools.partial(inner_kernel, heads, channels, group),
        grid=(inner_count // group,),
        in_specs=[whole(y_ends), whole(y_middle), *specs],
        out_specs=[
            pl.BlockSpec((group, VAR_DEV, CELLS, lanes), lambda i: (i, 0, 0, 0)),
            pl.BlockSpec((strips, tokens, LANES), lambda i: (0, 0, 0)),
        ],
        out_shape=[
            jax.ShapeDtypeStruct((inner_count, VAR_DEV, CELLS, lanes), BF16),
            jax.ShapeDtypeStruct((strips, tokens, LANES), BF16),
        ],
        scratch_shapes=[
            pltpu.VMEM((height, breadth, lanes), F32),
            pltpu.VMEM((inner_count, VAR_DEV, CELLS, lanes), F32),
        ],
        compiler_params=params(),
        cost_estimate=cost(inner_count * VAR_DEV),
        name="block_two_inner",
    )(y_ends, y_middle, *arrays)

    tall, wide = height + 2 * SHIFT, breadth + 2 * SHIFT
    slots = 2 * (tall + wide) // WIN - 4
    group = next(g for g in range(8, 0, -1) if slots % g == 0)
    operands = (y_ends, y_middle, top, bottom, *sides, inner)
    partial_shape = jax.ShapeDtypeStruct((strips, out_channels, tokens), BF16)
    partial = pl.pallas_call(
        functools.partial(outer_kernel, heads, channels, group),
        grid=(1,),
        in_specs=[*[whole(a) for a in operands], *specs, whole(recon)],
        out_specs=whole(partial_shape),
        out_shape=partial_shape,
        scratch_shapes=[
            pltpu.VMEM((WIN, wide, lanes), F32),
            pltpu.VMEM((height, 2 * WIN, lanes), F32),
            pltpu.VMEM((slots, VAR_DEV, CELLS, lanes), F32),
            pltpu.VMEM((slots, VAR_DEV, CELLS, lanes), BF16),
            pltpu.VMEM((tall + WIN, wide, lanes), F32),
        ],
        compiler_params=params(),
        name="block_two_border",
    )(*operands, *arrays, recon)

    sharers = lax.axis_size("var")
    strips = strips // sharers
    parts = lax.all_to_all(
        partial.reshape(sharers, strips, out_channels, tokens), "var", 0, 0
    )
    colours = out_channels // (SCALE * SCALE)
    final = (colours, strips * WIN * SCALE, breadth * SCALE)
    operands = (parts, marks, refine_grid, refine_qvt, refine_key, refine_projt)
    in_specs = [
        pl.BlockSpec(a.shape, lambda i, place, n=a.ndim: (0,) * n) for a in operands
    ]
    in_specs[1] = pl.BlockSpec((strips, tokens, LANES), lambda i, place: (place[0], 0, 0))
    strip = pl.pallas_call(
        functools.partial(refine_kernel, refine_heads, channels % LANES),
        grid_spec=pltpu.PrefetchScalarGridSpec(
            num_scalar_prefetch=1,
            grid=(1,),
            in_specs=in_specs,
            out_specs=pl.BlockSpec(final, lambda i, place: (0, 0, 0)),
            scratch_shapes=[pltpu.VMEM(final, F32)],
        ),
        out_shape=jax.ShapeDtypeStruct(final, BF16),
        compiler_params=params(),
        name="refinement",
    )(position[None], *operands)
    gathered = lax.all_gather(strip, "var", axis=0)
    picture = gathered.transpose(1, 0, 2, 3).reshape(colours, height * SCALE, breadth * SCALE)
    return picture.astype(F32)


def solution(mesh):
    placed = (P("ty", "tx", None), P("ty", "tx"), P(), P(), P(), P(), P(), P(), P(), P(), P())
    return jax.shard_map(
        local, mesh=mesh, in_specs=placed, out_specs=P(None, "ty", "tx"), check_vma=False
    )
```

time: 388 us -> 94.2 us (0.24); the launches traced: 381 us -> 92.8 us
  local copies, waits for them, and re-layouts: 121 us -> 7.84 us
  matrix products: 106 us -> 0 us
  other arithmetic: 69.1 us -> 1.51 us
  Pallas kernels: 0 us -> 59.8 us
  waiting for transfers between devices: 33.6 us -> 0.01 us
  starting transfers between devices: 30 us -> 6.77 us
  between operations: 14.6 us -> 0.34 us
  blocking collectives: 6.67 us -> 16.5 us
    dot_general x30 -> x0, matrix products: 105 us -> none  [the longest x2 31.4 us: feed_forward(): jnp.einsum('...e,ec->...c', hidden, w_down, preferred_element_type=jnp.fl...]
    pallas_call x0 -> x6, Pallas kernels: none -> 59.8 us  [the longest x1 19.6 us: local(): pl.pallas_call(functools.partial(outer_kernel, heads, channels, group), g...]
    convert_element_type x13 -> x1, local copies, waits for them, and re-layouts: 55.1 us -> 0.77 us  [local(): return picture.astype(F32)]
    sub x5 -> x0, other arithmetic: 34.4 us -> none  [the longest x2 34.2 us: attend(): weights = jnp.exp(scores - largest)]
    reshape x4, local copies, waits for them, and re-layouts: 33.4 us -> 0.05 us  [local(): a[:, :, cut].reshape(VAR_DEV, SHIFT * SHIFT, lanes)]
    ppermute x12 -> x3, starting transfers between devices: 30 us -> 6.77 us  [the longest x2 5.46 us: exchanged(): return (lax.ppermute(last, axis, up), lax.ppermute(first, axis, down))]
    reduce_scatter x1 -> x0, waiting for transfers between devices: 21.5 us -> none  [local(): lax.psum_scatter(to_windows(summed[None])[0].astype(jnp.bfloat16), 'var',...]
    slice x9 -> x3, local copies, waits for them, and re-layouts: 17 us -> 0.61 us  [the longest x1 0.57 us: local(): qkv_weight[:, :, i * channels:(i + 1) * channels]]
  transfers between devices with their start and end apart: 13 -> 3, of which waited for: 6 -> 0; matrix products, arithmetic and copies ran while one was open for 5% -> 0% of each run, Pallas kernels for 0% -> 28%
where the time goes in v2:
time: 94.2 us; the launch traced here: 92.8 us
  Pallas kernels  59.8 us (63%)
  blocking collectives  16.5 us (18%)
  local copies, waits for them, and re-layouts  7.84 us (8%)
  starting transfers between devices  6.77 us (7%)
  other arithmetic  1.51 us (2%)
    pallas_call x1, Pallas kernels, local(): pl.pallas_call(functools.partial(outer_kernel, heads, channels, group), g...  19.6 us
    pallas_call x2, Pallas kernels, block_one(): pl.pallas_call(functools.partial(first_kernel, heads, channels, ends), gr...  17.6 us
    pallas_call x1, Pallas kernels, local(): pl.pallas_call(functools.partial(inner_kernel, heads, channels, group), g...  13.8 us
    all_to_all x1, blocking collectives, local(): lax.all_to_all(partial.reshape(sharers, strips, out_channels, tokens), 'v...  10.2 us
    all_gather x1, blocking collectives, local(): gathered = lax.all_gather(strip, 'var', axis=0)  6.38 us
    unnamed x34, local copies, waits for them, and re-layouts  6.34 us
    pallas_call x1, Pallas kernels, local(): pl.pallas_call(functools.partial(prepare_kernel, heads, channels), grid=(...  5.77 us
    ppermute x2, starting transfers between devices, exchanged(): return (lax.ppermute(last, axis, up), lax.ppermute(first, axis, down))  5.46 us
  transfers between devices with their start and end apart: 3, of which 0 were waited for; matrix products, arithmetic and copies ran while one was open for 0% of the time, Pallas kernels for 28%

profile of v2, /device:TPU:9, one launch (start us, length us, event | category | flops | bytes accessed | tf_op | source)
XLA Modules:
  0.0 92.8 jit_solution(11187355414564862638)
XLA Ops:
  0.0 0.0 copy-start.3
  0.0 0.5 iota_add_fusion.codes_ref
  0.5 0.9 %copy.22 = bf16[2,180,180]{2,1,0:T(8,128)(2,1)S(1)} copy(bf16[2,180,180]{2,0,1:T(2,128)(2,1)} %param.14) | data formatting | bytes 259200 | tf_op args[3]
  1.5 1.0 %copy.23 = bf16[2,180,360]{2,1,0:T(8,128)(2,1)S(1)} copy(bf16[2,180,360]{2,0,1:T(2,128)(2,1)} %param.15) | data formatting | bytes 518400 | tf_op args[4]
  2.5 1.0 %copy.30 = bf16[2,360,180]{1,2,0:T(8,128)(2,1)S(1)} copy(bf16[2,360,180]{1,0,2:T(2,128)(2,1)} %param.16) | data formatting | bytes 518400 | tf_op args[5]
  3.5 0.0 copy-done.3
  3.5 0.6 fusion
  4.3 0.1 pad_dynamic-update-slice_fusion.1
  4.4 0.1 pad_dynamic-update-slice_fusion.packed_ref
  4.4 0.0 copy-start
  4.5 1.2 %copy-done = bf16[2,256,1792]{2,1,0:T(8,128)(2,1)} copy-done((bf16[2,256,1792]{2,1,0:T(8,128)(2,1)}, bf16[2,256,1792]{2,1,0:T(8,128)(2,1)S(1)}, u32[]{:S(2)}) %copy-start) | copy-done | bytes 1835032
  5.7 5.8 %prepare.1 = (bf16[2,400,256]{2,1,0:T(8,128)(2,1)}, bf16[2,256,256]{2,1,0:T(8,128)(2,1)}, bf16[2,256,256]{2,1,0:T(8,128)(2,1)}, bf16[2,256,384]{2,1,0:T(8,128)(2...) custom-call(s32[2]{0:T(128)} %iota_add_fusion.codes_ref, ...), custom_call_target="tpu_custom_call" | custom-call | tf_op jit(solution)/shard_map/prepare/pallas_call | solution.py:749
  11.5 5.5 %block_one_ends.1 = (bf16[2,16,32,256]{3,2,1,0:T(8,128)(2,1)}, bf16[2,64,256]{2,1,0:T(8,128)(2,1)}, bf16[2,64,256]{2,1,0:T(8,128)(2,1)}, bf16[2,4,32,256]{3,2,1,0:T(8,128)(2,1)}, bf16[2,4,32,256]{3,2,1,0:T(8,128)(2,1)}) custom-call(bf16[64,32,180]{2,1,0:T(8,128)(2,1)} %xb_ref.3, bf16[64,32,180]{2,1,0:T(8,128)(2,1)} %xb_ref.3, s32[32,64]{1,0:T(8,128)} %bitcast.18, ...), custom_call_target="tpu_custom_call" | custom-call | flops 6400000000 | bytes 3200000 | tf_op jit(solution)/shard_map/block_one_ends/pallas_call | solution.py:801
  17.0 0.9 broadcast_select_fusion.2
  17.9 0.0 copy-start.7
  17.9 0.0 copy-start.6
  18.0 1.3 %collective-permute-start = (bf16[2,4,32,256]{3,2,1,0:T(8,128)(2,1)S(1)}, bf16[2,4,32,256]{3,2,1,0:T(8,128)(2,1)S(1)}, u32[]{:S(2)}, u32[]{:S(2)}) collective-permute-start(bf16[2,4,32,256]{3,2,1,0:T(8,128)(2,1)S(1)} %broadcast_select_fusion.2), channel_id=1, source_target_pairs={{0,4},{4,0},{1,5},{5,1},{2,6},{6,2},{3,7},{7,3},{8,12},{12,8},{9,1... | collective-permute-start | bytes 393224 | tf_op jit(solution)/shard_map/ppermute | solution.py:673
  19.3 12.1 %block_one_middle.1 = (bf16[2,48,32,256]{3,2,1,0:T(8,128)(2,1)}, bf16[2,192,256]{2,1,0:T(8,128)(2,1)}, bf16[2,192,256]{2,1,0:T(8,128)(2,1)}) custom-call(bf16[64,32,180]{2,1,0:T(8,128)(2,1)} %xb_ref.3, bf16[64,32,180]{2,1,0:T(8,128)(2,1)} %xb_ref.3, s32[32,64]{1,0:T(8,128)} %bitcast.19, f32[2,2,64,384]{3,2,1,0:T(8,128)} %get-tuple-element.26.bias_ref, ...), custom_call_target="tpu_custom_call" | custom-call | flops 19200000000 | bytes 9600000 | tf_op jit(solution)/shard_map/block_one_middle/pallas_call | solution.py:801
  31.4 0.0 collective-permute-done
  31.4 0.0 copy-start.1
  31.4 0.0 copy-start.2
  31.6 0.0 copy-done.7
  31.6 0.0 copy-done.6
  31.6 1.1 %constant_dynamic-update-slice_fusion.2 = (bf16[2,288,256]{2,1,0:T(8,128)(2,1)S(1)}, bf16[2,288,256]{2,1,0:T(8,128)(2,1)S(1)}) fusion(bf16[2,288,256]{2,1,0:T(8,128)(2,1)S(1)} %constant_dynamic-update-slice_fusion.3, bf16[2,192,256]{2,1,0:T(8,128)(2,1)} %get-tuple-element.37, bf16[2,288,256]{2,1,0:T(8,128)(2,1)S(1)} %constant_dynamic-update-slice_fusion.8, ...), kind=kLoop, calls=%fused_computation.13 | loop fusion | bytes 786432
  32.7 2.1 %collective-permute-start.2 = (bf16[2,288,256]{2,1,0:T(8,128)(2,1)S(1)}, bf16[2,288,256]{2,1,0:T(8,128)(2,1)S(1)}, u32[]{:S(2)}, u32[]{:S(2)}) collective-permute-start(bf16[2,288,256]{2,1,0:T(8,128)(2,1)S(1)} %constant_dynamic-update-slice_fusion.5), channel_id=1, source_target_pairs={{1,0},{2,1},{3,2},{5,4},{6,5},{7,6},{9,8},{10,9},{11,10},{13,12},{... | collective-permute-start | bytes 884744 | tf_op jit(solution)/shard_map/ppermute | solution.py:671
  34.8 3.4 %collective-permute-start.1 = (bf16[2,288,256]{2,1,0:T(8,128)(2,1)S(1)}, bf16[2,288,256]{2,1,0:T(8,128)(2,1)S(1)}, u32[]{:S(2)}, u32[]{:S(2)}) collective-permute-start(bf16[2,288,256]{2,1,0:T(8,128)(2,1)S(1)} %constant_dynamic-update-slice_fusion), channel_id=1, source_target_pairs={{0,1},{1,2},{2,3},{4,5},{5,6},{6,7},{8,9},{9,10},{10,11},{12,13},{... | collective-permute-start | bytes 884744 | tf_op jit(solution)/shard_map/ppermute | solution.py:671
  38.2 13.8 %block_two_inner.1 = (bf16[21,2,64,256]{3,2,1,0:T(8,128)(2,1)}, bf16[8,256,128]{2,1,0:T(8,128)(2,1)}) custom-call(bf16[2,16,32,256]{3,2,1,0:T(8,128)(2,1)} %get-tuple-element.32.ends_ref, bf16[2,48,32,256]{3,2,1,0:T(8,128)(2,1)} %get-tuple-element.33.middle_ref, f32[2,2,64,384]{3,2,1,0:T(8,128)} %get-tuple-element.26.bias_ref, ...), custom_call_target="tpu_custom_call" | custom-call | flops 16800000000 | bytes 8400000 | tf_op jit(solution)/shard_map/block_two_inner/pallas_call | solution.py:841
  52.0 0.0 copy-done.1
  52.0 0.0 copy-done.2
  52.0 0.0 collective-permute-done.2.right_ref
  52.0 0.0 copy-start.4
  52.0 0.0 collective-permute-done.1.left_ref
  52.0 0.0 copy-start.5
  52.0 0.7 copy-done.4
  52.7 0.1 copy-done.5
  52.9 19.6 %block_two_border.1 = bf16[8,48,256]{2,1,0:T(8,128)(2,1)} custom-call(bf16[2,16,32,256]{3,2,1,0:T(8,128)(2,1)} %get-tuple-element.32.ends_ref, bf16[2,48,32,256]{3,2,1,0:T(8,128)(2,1)} %get-tuple-element.33.middle_ref, bf16[2,4,32,256]{3,2,1,0:T(8,128)(2,1)} %copy-done.2, bf16[2,4,32,256]{3,2,1,0:T(8,128)(2,1)} %copy-done.1, bf16[2,288,256]{2,1,0:T(8,128)(2,1)} %copy-done.5, ...), custom_call_target="tpu_custom_call" | custom-call | tf_op jit(solution)/shard_map/block_two_border/pallas_call | solution.py:867
  72.5 10.2 %all_to_all.5.parts_ref = bf16[4,2,48,256]{3,2,1,0:T(8,128)(2,1)} all-to-all(bf16[4,2,48,256]{3,2,1,0:T(8,128)(2,1)} %bitcast.15), channel_id=1, replica_groups=mesh['var'=4,'ty'=2,'tx'=4] {'var'}, dimensions={0} | all-to-all | bytes 393216 | tf_op jit(solution)/shard_map/all_to_all | solution.py:886
  82.7 2.9 %refinement.1 = bf16[3,64,128]{2,1,0:T(8,128)(2,1)} custom-call(s32[1]{0:T(128)} %bitcast.place_ref, bf16[4,2,48,256]{3,2,1,0:T(8,128)(2,1)} %all_to_all.5.parts_ref, bf16[8,256,128]{2,1,0:T(8,128)(2,1)} %get-tuple-element.42.marks_ref, f32[64,128]{1,0:T(8,128)} %get-tuple-element.43.bias_ref, bf16[144,128]{1,0:T(8,128)(2,1)} %get-tuple-element.44.w_qvt, ...), custom_call_target="tpu_custom_call" | custom-call | tf_op jit(solution)/shard_map/refinement/pallas_call | solution.py:896
  85.6 6.4 %all-gather = bf16[12,64,128]{2,1,0:T(8,128)(2,1)S(1)} all-gather(bf16[3,64,128]{2,1,0:T(8,128)(2,1)} %refinement.1), channel_id=2, replica_groups=mesh['var'=4,'ty'=2,'tx'=4] {'var'}, dimensions={0}, use_global_device_ids=true | all-gather | bytes 245760 | tf_op jit(solution)/shard_map/all_gather | solution.py:909
  92.0 0.8 copy.25
  (23 shorter events, 0.4 us)
Async XLA Ops:
  0.0 3.5 %copy-start.3 = (bf16[2,180,540]{2,0,1:T(2,128)(2,1)S(1)}, bf16[2,180,540]{2,0,1:T(2,128)(2,1)}, u32[]{:S(2)}) copy-start(bf16[2,180,540]{2,0,1:T(2,128)(2,1)} %param.13) | copy-start | bytes 1166404
  4.4 1.3 %copy-start = (bf16[2,256,1792]{2,1,0:T(8,128)(2,1)}, bf16[2,256,1792]{2,1,0:T(8,128)(2,1)S(1)}, u32[]{:S(2)}) copy-start(bf16[2,256,1792]{2,1,0:T(8,128)(2,1)S(1)} %pad_dynamic-update-slice_fusion.packed_ref) | copy-start | bytes 5505028
  17.9 13.6 %copy-start.7 = (bf16[2,64,256]{2,1,0:T(8,128)(2,1)S(1)}, bf16[2,64,256]{2,1,0:T(8,128)(2,1)}, u32[]{:S(2)}) copy-start(bf16[2,64,256]{2,1,0:T(8,128)(2,1)} %get-tuple-element.36) | copy-start | bytes 196612
  17.9 13.6 %copy-start.6 = (bf16[2,64,256]{2,1,0:T(8,128)(2,1)S(1)}, bf16[2,64,256]{2,1,0:T(8,128)(2,1)}, u32[]{:S(2)}) copy-start(bf16[2,64,256]{2,1,0:T(8,128)(2,1)} %get-tuple-element.38) | copy-start | bytes 196612
  18.0 13.4 %collective-permute-start = (bf16[2,4,32,256]{3,2,1,0:T(8,128)(2,1)S(1)}, bf16[2,4,32,256]{3,2,1,0:T(8,128)(2,1)S(1)}, u32[]{:S(2)}, u32[]{:S(2)}) collective-permute-start(bf16[2,4,32,256]{3,2,1,0:T(8,128)(2,1)S(1)} %broadcast_select_fusion.2), channel_id=1, source_target_pairs={{0,4},{4,0},{1,5},{5,1},{2,6},{6,2},{3,7},{7,3},{8,12},{12,8},{9,1... | collective-permute-start | bytes 393224 | tf_op jit(solution)/shard_map/ppermute | solution.py:673
  31.4 20.6 %copy-start.1 = (bf16[2,4,32,256]{3,2,1,0:T(8,128)(2,1)}, bf16[2,4,32,256]{3,2,1,0:T(8,128)(2,1)S(1)}, u32[]{:S(2)}) copy-start(bf16[2,4,32,256]{3,2,1,0:T(8,128)(2,1)S(1)} %get-tuple-element.54.bottom_ref) | copy-start | bytes 393220
  31.4 20.6 %copy-start.2 = (bf16[2,4,32,256]{3,2,1,0:T(8,128)(2,1)}, bf16[2,4,32,256]{3,2,1,0:T(8,128)(2,1)S(1)}, u32[]{:S(2)}) copy-start(bf16[2,4,32,256]{3,2,1,0:T(8,128)(2,1)S(1)} %get-tuple-element.55.top_ref) | copy-start | bytes 393220
  32.7 19.3 %collective-permute-start.2 = (bf16[2,288,256]{2,1,0:T(8,128)(2,1)S(1)}, bf16[2,288,256]{2,1,0:T(8,128)(2,1)S(1)}, u32[]{:S(2)}, u32[]{:S(2)}) collective-permute-start(bf16[2,288,256]{2,1,0:T(8,128)(2,1)S(1)} %constant_dynamic-update-slice_fusion.5), channel_id=1, source_target_pairs={{1,0},{2,1},{3,2},{5,4},{6,5},{7,6},{9,8},{10,9},{11,10},{13,12},{... | collective-permute-start | bytes 884744 | tf_op jit(solution)/shard_map/ppermute | solution.py:671
  34.8 17.2 %collective-permute-start.1 = (bf16[2,288,256]{2,1,0:T(8,128)(2,1)S(1)}, bf16[2,288,256]{2,1,0:T(8,128)(2,1)S(1)}, u32[]{:S(2)}, u32[]{:S(2)}) collective-permute-start(bf16[2,288,256]{2,1,0:T(8,128)(2,1)S(1)} %constant_dynamic-update-slice_fusion), channel_id=1, source_target_pairs={{0,1},{1,2},{2,3},{4,5},{5,6},{6,7},{8,9},{9,10},{10,11},{12,13},{... | collective-permute-start | bytes 884744 | tf_op jit(solution)/shard_map/ppermute | solution.py:671
  52.0 0.7 copy-start.4
  52.0 0.8 copy-start.5

commit v3 on v2

--- a/solution.py
+++ b/solution.py
@@ -21,15 +21,8 @@
 EPSILON = 1e-05
 LOG2E = 1.4426950408889634
 BIG = float(2.0**100)
-ERF_TANH = (
-    7.97884207935252e-01,
-    3.63342879e-02,
-    -3.31288562e-05,
-    -5.52410746e-05,
-    3.96927395e-06,
-    -1.33457816e-07,
-    1.80588519e-09,
-)
+ERF_TANH = (0.7975076, 0.0370060, -0.00035159)
+REACH = 36.0
 
 NN = (((1,), (0,)), ((), ()))
 NT = (((1,), (1,)), ((), ()))
@@ -125,9 +118,10 @@
 
 def prepare_kernel(
     heads,
-    channels,
-    codes_ref,
-    packed_ref,
+    qkv_ref,
+    proj_ref,
+    up_ref,
+    down_ref,
     swin_bias_ref,
     recon_ref,
     refine_qkv_ref,
@@ -147,56 +141,26 @@
     rows_ref,
     tables_ref,
 ):
-    blocks = packed_ref.shape[0]
+    blocks, channels, hidden = up_ref.shape
     width = channels // heads
     lanes = key_out.shape[1]
-    hidden = up_out.shape[2]
     head_rows = heads * HEAD_ROWS
     mark_rows = head_rows + 16
-    picked = head_matrix(lanes, lanes, heads, width)
-    shape = (2 * LANES, lanes)
-    row = iota(shape, 0)
-    head, unit = row % LANES // HEAD_ROWS * 2 + row // LANES, row % HEAD_ROWS
-    proj_rows = one_hot((head < heads) & (unit < width) & (iota(shape, 1) == head * width + unit))
-    identity = one_hot(iota((hidden, hidden), 0) == iota((hidden, hidden), 1))
-    query_add = query_labels(mark_rows, lanes, head_rows, channels)
-    key_add = key_labels(lanes, lanes, channels, head_rows)
-    for i in range(blocks):
-        at = [0]
-
-        def piece(size):
-            at[0] += size
-            return packed_ref[i, :, at[0] - size : at[0]]
-
-        query, key, value, proj = (piece(lanes) for _ in range(4))
-        qvt_out[i, :mark_rows] = (dot(picked[:mark_rows], query, NT) + query_add).astype(BF16)
-        qvt_out[i, mark_rows:] = exact(picked[:head_rows], value, NT)
-        key_out[i] = (dot(key, picked, NT) + key_add).astype(BF16)
-        proj_out[i] = exact(proj_rows, proj)
-        up_out[i] = piece(hidden)
-        down_out[i] = exact(identity, piece(hidden), NT)
-
     taps, out, _ = recon_ref.shape
-    kernel = recon_ref[...].reshape(taps * out, channels)
+    refine_heads = refine_bias_ref.shape[0]
+    refine_width = out // refine_heads
+    refine_rows = refine_heads * HEAD_ROWS
+    mark = channels % LANES
     pad = one_hot(iota((lanes, channels), 0) == iota((lanes, channels), 1))
+
     for i in range(blocks):
         tables_ref[i * heads : (i + 1) * heads] = swin_bias_ref[:, i]
+    rows, moved = [], []
+    kernel = recon_ref[...].reshape(taps * out, channels)
     for v in range(VAR_DEV):
-        code = codes_ref[v]
+        code = lax.axis_index("var") * VAR_DEV + v
         turn, flip_rows, flip_cols = code // 4 == 1, code // 2 % 2 == 1, code % 2 == 1
-        rows = bias_rows(tables_ref[: blocks * heads], turn, flip_rows, flip_cols)
-        tables = [rows[i * heads : (i + 1) * heads] for i in range(blocks)]
-        for i in range(blocks):
-
-            def store(key_row, pair, value):
-                bias_out[
-                    i,
-                    v,
-                    key_row * WIN : (key_row + 1) * WIN,
-                    pair * LANES : (pair + 1) * LANES,
-                ] = value
-
-            bias_grid(tables[i], rows_ref, store)
+        rows.append(bias_rows(tables_ref[: blocks * heads], turn, flip_rows, flip_cols))
         shape = (3 * lanes, 1)
         row = iota(shape, 0)
         row_step = row // lanes - 1
@@ -215,47 +179,85 @@
         source = source + jnp.where(turn, sub_col, sub_row) * SCALE
         source = tap * out + source + jnp.where(turn, sub_row, sub_col)
         source = jnp.where(channel < out, source, -1)
-        moved = exact(one_hot(iota((3 * lanes, taps * out), 1) == source), kernel)
-        recon_out[v] = exact(pad, moved, NT)
-
-    refine_heads = refine_bias_ref.shape[0]
-    refine_width = out // refine_heads
-    never = codes_ref[0] < 0
-    rows = bias_rows(refine_bias_ref[...], never, never, never)
-
-    def store_refine(key_row, pair, value):
-        refine_bias_out[key_row * WIN : (key_row + 1) * WIN] = value
-
-    bias_grid(rows, rows_ref, store_refine)
-    refine_rows = refine_heads * HEAD_ROWS
-    values = head_matrix(refine_rows, 3 * out, refine_heads, refine_width, 2 * out)
-    queries = head_matrix(refine_rows + 16, 3 * out, refine_heads, refine_width)
-    keys = head_matrix(LANES, 3 * out, refine_heads, refine_width, out)
-    out_pad = one_hot(iota((LANES, out), 0) == iota((LANES, out), 1))
+        moved.append(exact(one_hot(iota((3 * lanes, taps * out), 1) == source), kernel))
+    never = lax.axis_index("var") < 0
+    refine_table = bias_rows(refine_bias_ref[...], never, never, never)
+    keys = [
+        exact(qkv_ref[i], head_matrix(lanes, 3 * channels, heads, width, channels), NT)
+        for i in range(blocks)
+    ]
     weight = refine_qkv_ref[...]
-    mark = channels % LANES
-    refine_qvt_out[: refine_rows + 16] = (
-        dot(exact(queries, weight, NT), out_pad, NT)
-        + query_labels(refine_rows + 16, LANES, refine_rows, mark)
-    ).astype(BF16)
-    refine_qvt_out[refine_rows + 16 :] = exact(exact(values, weight, NT), out_pad, NT)
-    refine_key_out[...] = (
-        dot(out_pad, exact(keys, weight, NT), NT) + key_labels(LANES, LANES, mark, refine_rows)
-    ).astype(BF16)
+    refine_queries = exact(
+        head_matrix(refine_rows + 16, 3 * out, refine_heads, refine_width), weight, NT
+    )
+    refine_values = exact(
+        head_matrix(refine_rows, 3 * out, refine_heads, refine_width, 2 * out), weight, NT
+    )
+    refine_keys = exact(head_matrix(LANES, 3 * out, refine_heads, refine_width, out), weight, NT)
+    refine_proj = []
     for h in range(refine_heads):
         shape = (LANES, out)
         row = iota(shape, 0)
-        rows = one_hot((row < refine_width) & (iota(shape, 1) == row + h * refine_width))
-        square = dot(exact(rows, refine_proj_ref[...]), out_pad, NT)
+        pick = one_hot((row < refine_width) & (iota(shape, 1) == row + h * refine_width))
+        refine_proj.append(exact(pick, refine_proj_ref[...]))
+
+    queries = head_matrix(mark_rows, 3 * channels, heads, width)
+    values = head_matrix(head_rows, 3 * channels, heads, width, 2 * channels)
+    query_add = query_labels(mark_rows, lanes, head_rows, channels).astype(BF16)
+    key_add = key_labels(lanes, lanes, channels, head_rows)
+    shape = (2 * LANES, channels)
+    row = iota(shape, 0)
+    head, unit = row % LANES // HEAD_ROWS * 2 + row // LANES, row % HEAD_ROWS
+    proj_rows = one_hot((head < heads) & (unit < width) & (iota(shape, 1) == head * width + unit))
+    shape = (down_out.shape[1], hidden)
+    down_rows = one_hot(iota(shape, 0) == iota(shape, 1))
+    for i in range(blocks):
+        for ref in (qvt_out, proj_out, up_out, down_out):
+            ref[i] = jnp.zeros(ref.shape[1:], BF16)
+        qvt_out[i, :mark_rows] = query_add
+        qvt_out[i, :mark_rows, :channels] = exact(queries, qkv_ref[i], NT)
+        qvt_out[i, mark_rows:, :channels] = exact(values, qkv_ref[i], NT)
+        proj_out[i, :, :channels] = exact(proj_rows, proj_ref[i])
+        up_out[i, :, :hidden] = exact(pad, up_ref[i])
+        down_out[i, :, :channels] = exact(down_rows, down_ref[i], NT)
+
+    for i in range(blocks):
+        key_out[i] = (dot(pad, keys[i]) + key_add).astype(BF16)
+    for v in range(VAR_DEV):
+        recon_out[v] = exact(pad, moved[v], NT)
+    out_pad = one_hot(iota((LANES, out), 0) == iota((LANES, out), 1))
+    refine_qvt_out[: refine_rows + 16] = (
+        dot(refine_queries, out_pad, NT)
+        + query_labels(refine_rows + 16, LANES, refine_rows, mark)
+    ).astype(BF16)
+    refine_qvt_out[refine_rows + 16 :] = exact(refine_values, out_pad, NT)
+    refine_key_out[...] = (
+        dot(out_pad, refine_keys, NT) + key_labels(LANES, LANES, mark, refine_rows)
+    ).astype(BF16)
+    for h in range(refine_heads):
+        square = dot(refine_proj[h], out_pad, NT)
         refine_proj_out[h * out : (h + 1) * out] = square.T[:out].astype(BF16)
+    for v in range(VAR_DEV):
+        for i in range(blocks):
+
+            def store(key_row, pair, value):
+                at = slice(key_row * WIN, (key_row + 1) * WIN)
+                bias_out[i, v, at, pair * LANES : (pair + 1) * LANES] = value
+
+            bias_grid(rows[v][i * heads : (i + 1) * heads], rows_ref, store)
+
+    def store_refine(key_row, pair, value):
+        refine_bias_out[key_row * WIN : (key_row + 1) * WIN] = value
+
+    bias_grid(refine_table, rows_ref, store_refine)
 
 
 def gelu(x):
-    square = x * x
-    series = jnp.full_like(square, ERF_TANH[-1])
-    for factor in ERF_TANH[-2::-1]:
-        series = series * square + factor
-    half = 0.5 * x
+    x = x.astype(BF16)
+    square = jnp.minimum(x * x, BF16(REACH))
+    first, second, third = (BF16(factor) for factor in ERF_TANH)
+    series = (square * third + second) * square + first
+    half = BF16(0.5) * x
     return half + half * jnp.tanh(x * series)
 
 
@@ -358,7 +360,7 @@
     if places != list(range(x.shape[0] // LANES)):
         x = jnp.concatenate([x[place * LANES : (place + 1) * LANES] for place in places], axis=0)
     h = (x + dot(outputs, w_proj[...])).astype(BF16).astype(F32)
-    hidden = gelu(dot(normalize(h, channels), w_up[...])).astype(BF16)
+    hidden = gelu(dot(normalize(h, channels), w_up[...]))
     y = h + dot(hidden, w_down[...])
     return [y[i * LANES : (i + 1) * LANES] for i in range(len(pairs))]
 
@@ -374,22 +376,22 @@
     )
 
 
-def first_kernel(
-    heads, channels, ends, xa_ref, xb_ref, labels_ref, bias_ref, *refs
-):
+def first_kernel(heads, channels, strips, x_ref, labels_ref, bias_ref, *refs):
+    ends = strips[0] == 0
     *weights, y_ref, left_ref, right_ref = refs[:8]
     held, side = refs[-2:]
-    step = pl.program_id(0)
-    breadth = xa_ref.shape[1]
+    breadth = x_ref.shape[1]
     count = breadth // WIN
     tokens, lanes = held.shape
-    part = tokens // 2
+    part = tokens // len(strips)
     rows_total = labels_ref.shape[1]
-    strips = (0, rows_total // WIN - 1) if ends else (2 * step + 1, 2 * step + 2)
-    for k, ref in enumerate((xa_ref, xb_ref)):
-        held[k * part : (k + 1) * part, :channels] = windows_of(ref[...].astype(F32))
+    for k, strip in enumerate(strips):
+        rows = x_ref[strip * WIN : (strip + 1) * WIN].astype(F32)
+        held[k * part : (k + 1) * part, :channels] = windows_of(rows)
     token = iota((tokens, rows_total), 0)
-    strip = jnp.where(token < part, strips[0], strips[1])
+    strip = token // part + strips[0]
+    if ends:
+        strip = jnp.where(token < part, strips[0], strips[1])
     at_row = strip * WIN + token % CELLS // WIN == iota((tokens, rows_total), 1)
     by_row = dot(one_hot(at_row), labels_ref[...].astype(F32).astype(BF16), NT)
     token = iota((tokens, breadth), 0)
@@ -408,7 +410,7 @@
     pairs = [(place, v, v) for v in range(VAR_DEV) for place in range(places)]
     results = swin_block(x, pairs, heads, channels, lambda v: bias_ref[v], *weights)
     for v in range(VAR_DEV):
-        for k in range(2):
+        for k in range(len(strips)):
             windows = []
             for w in range(count):
                 group = k * count + w
@@ -424,9 +426,13 @@
         left_ref[v] = side[0].astype(BF16)
         right_ref[v] = side[1].astype(BF16)
     if ends:
-        top_ref, bottom_ref = refs[8:10]
-        top_ref[...] = y_ref[:, :SHIFT]
-        bottom_ref[...] = y_ref[:, 2 * WIN - SHIFT :]
+        if len(refs) == 11:
+            refs[8][...] = jnp.where(
+                lax.axis_index("ty") == 0, y_ref[:, 2 * WIN - SHIFT :], y_ref[:, :SHIFT]
+            )
+        else:
+            refs[8][...] = y_ref[:, :SHIFT]
+            refs[9][...] = y_ref[:, 2 * WIN - SHIFT :]
 
 
 def place_rows(store, ends_ref, middle_ref, v):
@@ -547,41 +553,23 @@
 
     lax.fori_loop(0, slots // group, border, 0)
 
-    acc[...] = jnp.zeros_like(acc)
+    weights = w_recon[...].reshape(VAR_DEV * lanes, 3 * lanes)
 
     def scatter(strip, windows):
-        total = None
-        for v in range(VAR_DEV):
-            part = dot(jnp.concatenate(windows(v), axis=0), w_recon[v])
-            total = part if total is None else total + part
+        tokens = [jnp.concatenate(windows(v), axis=0) for v in range(VAR_DEV)]
+        total = dot(jnp.concatenate(tokens, axis=1), weights)
         total = total.reshape(count, WIN, WIN, 3 * lanes)
         for e in range(3):
+            rows = slice(strip * WIN + 2 - e, (strip + 1) * WIN + 2 - e)
             for w in range(count):
-                acc[pl.ds(strip * WIN + 2 - e, WIN), w * WIN : (w + 1) * WIN] += total[
-                    w, :, :, e * lanes : (e + 1) * lanes
-                ]
-
-    def middle(strip, carry):
-        slot = 2 * count + 2 * (strip - 1)
-        first = (strip - 1) * (count - 2)
-        scatter(
-            strip,
-            lambda v: [
-                y_held[slot, v],
-                *[inner_ref[first + w, v] for w in range(count - 2)],
-                y_held[slot + 1, v],
-            ],
-        )
-        return carry
-
-    scatter(0, lambda v: [y_held[w, v] for w in range(count)])
-    lax.fori_loop(1, strips - 1, middle, 0)
-    scatter(strips - 1, lambda v: [y_held[count + w, v] for w in range(count)])
+                across = slice(w * WIN, (w + 1) * WIN)
+                part = total[w, :, :, e * lanes : (e + 1) * lanes]
+                acc[rows, across] = part if e == 0 else acc[rows, across] + part
 
     out_channels = out_ref.shape[1]
 
-    def finish(strip, carry):
-        rows = pl.ds(1 + SHIFT + strip * WIN, WIN)
+    def finish(strip):
+        rows = slice(1 + SHIFT + strip * WIN, 1 + SHIFT + (strip + 1) * WIN)
         centre = acc[rows, SHIFT : SHIFT + breadth, :LANES]
         centre = pltpu.roll(centre.reshape(WIN * breadth, LANES), LANES - out_channels, 1)
         result = (
@@ -590,17 +578,39 @@
             + acc[rows, SHIFT + 1 : SHIFT + 1 + breadth, LANES : 2 * LANES]
         )
         out_ref[strip] = windows_of(result).T[:out_channels].astype(BF16)
-        return carry
-
-    lax.fori_loop(0, height // WIN, finish, 0)
+
+    scatter(0, lambda v: [y_held[w, v] for w in range(count)])
+    for strip in range(1, strips):
+        if strip == strips - 1:
+            scatter(strip, lambda v: [y_held[count + w, v] for w in range(count)])
+        else:
+            slot = 2 * count + 2 * (strip - 1)
+            first = (strip - 1) * (count - 2)
+            scatter(
+                strip,
+                lambda v: [
+                    y_held[slot, v],
+                    *[inner_ref[first + w, v] for w in range(count - 2)],
+                    y_held[slot + 1, v],
+                ],
+            )
+        finish(strip - 1)
 
 
 def refine_kernel(
-    heads, first_mark, place_ref, parts_ref, marks_ref, bias_ref, w_qvt, w_key, w_projt, out_ref, final
+    heads, first_mark, parts_ref, marks_ref, bias_ref, w_qvt, w_key, w_projt, out_ref, spread_ref
 ):
     sources, strips, channels, strip_tokens = parts_ref.shape
     breadth = strip_tokens // WIN
     width = channels // heads
+
+    @pl.when(pl.program_id(0) == 0)
+    def _():
+        shape = spread_ref.shape
+        cell = iota(shape, 1) // SCALE
+        source = (cell % breadth // WIN) * CELLS + (cell // breadth) * WIN + cell % WIN
+        spread_ref[...] = one_hot(iota(shape, 0) == source)
+
     z = jnp.concatenate(
         [
             sum(parts_ref[s, strip].astype(F32) for s in range(sources))
@@ -642,10 +652,7 @@
     stacked = jnp.concatenate(
         [refined[:, s * strip_tokens : (s + 1) * strip_tokens] for s in range(strips)], axis=0
     )
-    shape = (strip_tokens, WIN * breadth * SCALE)
-    cell = iota(shape, 1) // SCALE
-    source = (cell % breadth // WIN) * CELLS + (cell // breadth) * WIN + cell % WIN
-    wide = dot(stacked, one_hot(iota(shape, 0) == source))
+    wide = dot(stacked, spread_ref[...])
     own = iota(wide.shape, 1) % SCALE == iota(wide.shape, 0) % SCALE
     wide = jnp.where(own, wide, 0.0).astype(BF16)
     shape = (wide.shape[0] // SCALE, wide.shape[0])
@@ -657,20 +664,21 @@
             first = (s * colours + c) * SCALE
             for y in range(WIN):
                 start = (s * WIN + y) * SCALE
-                final[c, start : start + SCALE] = folded[
+                out_ref[c, start : start + SCALE] = folded[
                     first : first + SCALE, y * row_lanes : (y + 1) * row_lanes
                 ]
-    out_ref[...] = final[...].astype(BF16)
 
 
 def exchanged(last, first, axis):
     count = lax.axis_size(axis)
     up = [(i, i + 1) for i in range(count - 1)]
     down = [(i + 1, i) for i in range(count - 1)]
-    if count != 2:
-        return lax.ppermute(last, axis, up), lax.ppermute(first, axis, down)
+    return lax.ppermute(last, axis, up), lax.ppermute(first, axis, down)
+
+
+def swapped(strip, axis):
     at_start = lax.axis_index(axis) == 0
-    received = lax.ppermute(jnp.where(at_start, last, first), axis, up + down)
+    received = lax.ppermute(strip, axis, [(0, 1), (1, 0)])
     zero = jnp.zeros_like(received)
     return jnp.where(at_start, zero, received), jnp.where(at_start, received, zero)
 
@@ -704,27 +712,11 @@
     refine_heads = refine_bias.shape[0]
     lanes = round_up(channels + MARKS, LANES)
     hidden = round_up(up_weight.shape[-1], LANES)
-    position = lax.axis_index("var")
-    codes = position * VAR_DEV + jnp.arange(VAR_DEV, dtype=jnp.int32)
-
-    def widen(weight, size):
-        return jnp.pad(weight, ((0, 0), (0, lanes - channels), (0, size - weight.shape[2])))
-
-    packed = jnp.concatenate(
-        [
-            *[
-                widen(qkv_weight[:, :, i * channels : (i + 1) * channels], lanes)
-                for i in range(3)
-            ],
-            widen(proj_weight, lanes),
-            widen(up_weight, hidden),
-            widen(jnp.swapaxes(down_weight, 1, 2), hidden),
-        ],
-        axis=2,
-    )
     operands = (
-        codes,
-        packed,
+        qkv_weight,
+        proj_weight,
+        up_weight,
+        jnp.swapaxes(down_weight, 1, 2),
         jnp.swapaxes(swin_bias, 0, 1),
         jnp.swapaxes(recon_weight, 1, 2),
         refine_qkv,
@@ -747,9 +739,9 @@
     ]
     shapes = [jax.ShapeDtypeStruct(*s) for s in shapes]
     prepared = pl.pallas_call(
-        functools.partial(prepare_kernel, heads, channels),
+        functools.partial(prepare_kernel, heads),
         grid=(1,),
-        in_specs=[pl.BlockSpec(memory_space=pltpu.SMEM)] + [whole(a) for a in operands[1:]],
+        in_specs=[whole(a) for a in operands],
         out_specs=[whole(s) for s in shapes],
         out_shape=shapes,
         scratch_shapes=[
@@ -776,52 +768,39 @@
     arrays, specs = block_specs(0)
     strips = height // WIN
     tokens = WIN * breadth
-    side_rows = 2 * WIN * SHIFT
     labels_across = labels.T
 
-    def block_one(ends):
-        steps = 1 if ends else strips // 2 - 1
-        first = (lambda i: 0) if ends else (lambda i: 2 * i + 1)
-        second = (lambda i: strips - 1) if ends else (lambda i: 2 * i + 2)
+    pair_axis = lax.axis_size("ty") == 2
+
+    def block_one(places, name):
+        rows = len(places) * WIN
         outs = [
-            ((VAR_DEV, steps * 2 * WIN, breadth, lanes), BF16),
-            ((VAR_DEV, steps * side_rows, lanes), BF16),
-            ((VAR_DEV, steps * side_rows, lanes), BF16),
+            ((VAR_DEV, rows, breadth, lanes), BF16),
+            ((VAR_DEV, rows * SHIFT, lanes), BF16),
+            ((VAR_DEV, rows * SHIFT, lanes), BF16),
         ]
-        out_specs = [
-            pl.BlockSpec((VAR_DEV, 2 * WIN, breadth, lanes), lambda i: (0, i, 0, 0)),
-            pl.BlockSpec((VAR_DEV, side_rows, lanes), lambda i: (0, i, 0)),
-            pl.BlockSpec((VAR_DEV, side_rows, lanes), lambda i: (0, i, 0)),
-        ]
-        if ends:
-            outs += [((VAR_DEV, SHIFT, breadth, lanes), BF16)] * 2
-            out_specs += [
-                pl.BlockSpec((VAR_DEV, SHIFT, breadth, lanes), lambda i: (0, 0, 0, 0))
-            ] * 2
+        if places[0] == 0:
+            outs += [((VAR_DEV, SHIFT, breadth, lanes), BF16)] * (1 if pair_axis else 2)
+        outs = [jax.ShapeDtypeStruct(*o) for o in outs]
         return pl.pallas_call(
-            functools.partial(first_kernel, heads, channels, ends),
-            grid=(steps,),
-            in_specs=[
-                pl.BlockSpec((WIN, breadth, channels), lambda i: (first(i), 0, 0)),
-                pl.BlockSpec((WIN, breadth, channels), lambda i: (second(i), 0, 0)),
-                whole(labels_across),
-                *specs,
-            ],
-            out_specs=out_specs,
-            out_shape=[jax.ShapeDtypeStruct(*o) for o in outs],
+            functools.partial(first_kernel, heads, channels, places),
+            grid=(1,),
+            in_specs=[whole(features), whole(labels_across), *specs],
+            out_specs=[whole(o) for o in outs],
+            out_shape=outs,
             scratch_shapes=[
-                pltpu.VMEM((2 * tokens, lanes), F32),
-                pltpu.VMEM((2, side_rows, lanes), F32),
+                pltpu.VMEM((len(places) * tokens, lanes), F32),
+                pltpu.VMEM((2, rows * SHIFT, lanes), F32),
             ],
             compiler_params=params(),
-            cost_estimate=cost(steps * breadth // WIN * 4),
-            name="block_one_ends" if ends else "block_one_middle",
-        )(features, features, labels_across, *arrays)
-
-    y_ends, left_ends, right_ends, top_own, bottom_own = block_one(True)
-    top, bottom = exchanged(bottom_own, top_own, "ty")
-    y_middle, left_middle, right_middle = block_one(False)
-    half = side_rows // 2
+            cost_estimate=cost(len(places) * breadth // WIN * VAR_DEV),
+            name=name,
+        )(features, labels_across, *arrays)
+
+    y_ends, left_ends, right_ends, *own_ends = block_one((0, strips - 1), "block_one_ends")
+    top, bottom = swapped(*own_ends, "ty") if pair_axis else exchanged(*own_ends[::-1], "ty")
+    y_middle, left_middle, right_middle = block_one(tuple(range(1, strips - 1)), "block_one_middle")
+    half = WIN * SHIFT
     strips_out = []
     for ends, middle, cut in (
         (right_ends, right_middle, slice(breadth - SHIFT, breadth)),
@@ -837,7 +816,7 @@
 
     arrays, specs = block_specs(1)
     inner_count = (strips - 1) * (breadth // WIN - 1)
-    group = next(g for g in range(7, 0, -1) if inner_count % g == 0)
+    group = next(g for g in range(24, 0, -1) if inner_count % g == 0)
     inner, marks = pl.pallas_call(
         functools.partial(inner_kernel, heads, channels, group),
         grid=(inner_count // group,),
@@ -861,7 +840,7 @@
 
     tall, wide = height + 2 * SHIFT, breadth + 2 * SHIFT
     slots = 2 * (tall + wide) // WIN - 4
-    group = next(g for g in range(8, 0, -1) if slots % g == 0)
+    group = next(g for g in range(24, 0, -1) if slots % g == 0)
     operands = (y_ends, y_middle, top, bottom, *sides, inner)
     partial_shape = jax.ShapeDtypeStruct((strips, out_channels, tokens), BF16)
     partial = pl.pallas_call(
@@ -881,34 +860,27 @@
         name="block_two_border",
     )(*operands, *arrays, recon)
 
-    sharers = lax.axis_size("var")
-    strips = strips // sharers
-    parts = lax.all_to_all(
-        partial.reshape(sharers, strips, out_channels, tokens), "var", 0, 0
-    )
+    parts = lax.all_gather(partial, "var", axis=0)
     colours = out_channels // (SCALE * SCALE)
-    final = (colours, strips * WIN * SCALE, breadth * SCALE)
+    chunk = next(c for c in (8, 4, 2, 1) if strips % c == 0)
     operands = (parts, marks, refine_grid, refine_qvt, refine_key, refine_projt)
-    in_specs = [
-        pl.BlockSpec(a.shape, lambda i, place, n=a.ndim: (0,) * n) for a in operands
-    ]
-    in_specs[1] = pl.BlockSpec((strips, tokens, LANES), lambda i, place: (place[0], 0, 0))
-    strip = pl.pallas_call(
+    in_specs = [whole(a) for a in operands]
+    in_specs[0] = pl.BlockSpec(
+        (parts.shape[0], chunk, out_channels, tokens), lambda i: (0, i, 0, 0)
+    )
+    in_specs[1] = pl.BlockSpec((chunk, tokens, LANES), lambda i: (i, 0, 0))
+    return pl.pallas_call(
         functools.partial(refine_kernel, refine_heads, channels % LANES),
-        grid_spec=pltpu.PrefetchScalarGridSpec(
-            num_scalar_prefetch=1,
-            grid=(1,),
-            in_specs=in_specs,
-            out_specs=pl.BlockSpec(final, lambda i, place: (0, 0, 0)),
-            scratch_shapes=[pltpu.VMEM(final, F32)],
+        grid=(strips // chunk,),
+        in_specs=in_specs,
+        out_specs=pl.BlockSpec(
+            (colours, chunk * WIN * SCALE, breadth * SCALE), lambda i: (0, i, 0)
         ),
-        out_shape=jax.ShapeDtypeStruct(final, BF16),
+        out_shape=jax.ShapeDtypeStruct((colours, height * SCALE, breadth * SCALE), F32),
+        scratch_shapes=[pltpu.VMEM((tokens, tokens * SCALE), BF16)],
         compiler_params=params(),
         name="refinement",
-    )(position[None], *operands)
-    gathered = lax.all_gather(strip, "var", axis=0)
-    picture = gathered.transpose(1, 0, 2, 3).reshape(colours, height * SCALE, breadth * SCALE)
-    return picture.astype(F32)
+    )(*operands)
 
 
 def solution(mesh):

time: 94.2 us -> 76.7 us (0.81)
  Pallas kernels: 59.8 us -> 48.9 us
  blocking collectives: 16.5 us -> 11.4 us
  other arithmetic: 1.51 us -> 0.02 us
    all_to_all x1 -> x0, blocking collectives: 10.2 us -> none  [local(): lax.all_to_all(partial.reshape(sharers, strips, out_channels, tokens), 'v...]
    pallas_call x1, Pallas kernels: 19.6 us -> 14.4 us  [local(): pl.pallas_call(functools.partial(outer_kernel, heads, channels, group), g...]
    all_gather x1, blocking collectives: 6.38 us -> 11.4 us  [local(): parts = lax.all_gather(partial, 'var', axis=0)]
    pallas_call x1, Pallas kernels: 13.8 us -> 9.67 us  [local(): pl.pallas_call(functools.partial(inner_kernel, heads, channels, group), g...]
    pallas_call x3, Pallas kernels: 23.4 us -> 20 us  [the longest x2 14.6 us: block_one(): pl.pallas_call(functools.partial(first_kernel, heads, channels, places),...]
    pallas_call x1, Pallas kernels: 2.95 us -> 4.88 us  [local(): pl.pallas_call(functools.partial(refine_kernel, refine_heads, channels %...]
    unnamed x34 -> x25, local copies, waits for them, and re-layouts: 6.34 us -> 7.97 us
  transfers between devices with their start and end apart: 3 -> 3, of which waited for: 0 -> 0; matrix products, arithmetic and copies ran while one was open for 0% -> 0% of each run, Pallas kernels for 28% -> 25%
where the time goes in v3:
time: 76.7 us; the launch traced here: 75.2 us
  Pallas kernels  48.9 us (64%)
  blocking collectives  11.4 us (15%)
  local copies, waits for them, and re-layouts  8.06 us (11%)
  starting transfers between devices  6.59 us (9%)
    pallas_call x2, Pallas kernels, block_one(): pl.pallas_call(functools.partial(first_kernel, heads, channels, places),...  14.6 us
    pallas_call x1, Pallas kernels, local(): pl.pallas_call(functools.partial(outer_kernel, heads, channels, group), g...  14.4 us
    all_gather x1, blocking collectives, local(): parts = lax.all_gather(partial, 'var', axis=0)  11.4 us
    pallas_call x1, Pallas kernels, local(): pl.pallas_call(functools.partial(inner_kernel, heads, channels, group), g...  9.67 us
    unnamed x25, local copies, waits for them, and re-layouts  7.97 us
    pallas_call x1, Pallas kernels, local(): pl.pallas_call(functools.partial(prepare_kernel, heads), grid=(1,), in_sp...  5.4 us
    ppermute x2, starting transfers between devices, exchanged(): return (lax.ppermute(last, axis, up), lax.ppermute(first, axis, down))  5.28 us
    pallas_call x1, Pallas kernels, local(): pl.pallas_call(functools.partial(refine_kernel, refine_heads, channels %...  4.88 us
  transfers between devices with their start and end apart: 3, of which 0 were waited for; matrix products, arithmetic and copies ran while one was open for 0% of the time, Pallas kernels for 25%

profile of v3, /device:TPU:9, one launch (start us, length us, event | category | flops | bytes accessed | tf_op | source)
XLA Modules:
  0.0 75.2 jit_solution(5024941438116484641)
XLA Ops:
  0.0 0.0 copy-start.2
  0.0 1.7 %copy.18.proj_ref = bf16[2,180,180]{2,1,0:T(8,128)(2,1)} copy(bf16[2,180,180]{2,0,1:T(2,128)(2,1)} %param.14) | data formatting | bytes 259200 | tf_op args[3]
  1.7 1.7 %copy.19.up_ref = bf16[2,180,360]{2,1,0:T(8,128)(2,1)} copy(bf16[2,180,360]{2,0,1:T(2,128)(2,1)} %param.15) | data formatting | bytes 518400 | tf_op args[4]
  3.4 1.7 %copy.21 = bf16[2,360,180]{1,2,0:T(8,128)(2,1)} copy(bf16[2,360,180]{1,0,2:T(2,128)(2,1)} %param.16) | data formatting | bytes 518400 | tf_op args[5]
  5.1 0.0 copy-done.2
  5.1 0.8 %copy.17.qkv_ref = bf16[2,180,540]{2,1,0:T(8,128)(2,1)} copy(bf16[2,180,540]{2,0,1:T(2,128)(2,1)S(1)} %copy-done.2) | data formatting | bytes 777600 | tf_op args[2]
  5.9 5.4 %prepare.1 = (bf16[2,400,256]{2,1,0:T(8,128)(2,1)}, bf16[2,256,256]{2,1,0:T(8,128)(2,1)}, bf16[2,256,256]{2,1,0:T(8,128)(2,1)}, bf16[2,256,384]{2,1,0:T(8,128)(2...) custom-call(bf16[2,180,540]{2,1,0:T(8,128)(2,1)} %copy.17.qkv_ref, ...), custom_call_target="tpu_custom_call" | custom-call | tf_op jit(solution)/shard_map/prepare/pallas_call | solution.py:741
  11.3 5.4 %block_one_ends.1 = (bf16[2,16,32,256]{3,2,1,0:T(8,128)(2,1)}, bf16[2,64,256]{2,1,0:T(8,128)(2,1)}, bf16[2,64,256]{2,1,0:T(8,128)(2,1)}, bf16[2,4,32,256]{3,2,1,0:T(8,128)(2,1)}) custom-call(bf16[64,32,180]{2,1,0:T(8,128)(2,1)} %x_ref.3, s32[32,64]{1,0:T(8,128)} %bitcast.11, f32[2,2,64,384]{3,2,1,0:T(8,128)} %get-tuple-element.25.bias_ref, ...), custom_call_target="tpu_custom_call" | custom-call | flops 6400000000 | bytes 3200000 | tf_op jit(solution)/shard_map/block_one_ends/pallas_call | solution.py:785
  16.7 0.0 copy-start.6
  16.7 0.0 copy-start.5
  16.7 1.3 %collective-permute-start = (bf16[2,4,32,256]{3,2,1,0:T(8,128)(2,1)}, bf16[2,4,32,256]{3,2,1,0:T(8,128)(2,1)S(1)}, u32[]{:S(2)}, u32[]{:S(2)}) collective-permute-start(bf16[2,4,32,256]{3,2,1,0:T(8,128)(2,1)} %get-tuple-element.33), channel_id=1, source_target_pairs={{0,4},{4,0},{1,5},{5,1},{2,6},{6,2},{3,7},{7,3},{8,12},{12,8},{9,1... | collective-permute-start | bytes 393224 | tf_op jit(solution)/shard_map/ppermute | solution.py:681
  18.0 9.2 %block_one_middle.1 = (bf16[2,48,32,256]{3,2,1,0:T(8,128)(2,1)}, bf16[2,192,256]{2,1,0:T(8,128)(2,1)}, bf16[2,192,256]{2,1,0:T(8,128)(2,1)}) custom-call(bf16[64,32,180]{2,1,0:T(8,128)(2,1)} %x_ref.3, s32[32,64]{1,0:T(8,128)} %bitcast.12, f32[2,2,64,384]{3,2,1,0:T(8,128)} %get-tuple-element.25.bias_ref, bf16[2,400,256]{2,1,0:T(8,128)(2,1)} %get-tuple-element.26.refs_0_, ...), custom_call_target="tpu_custom_call" | custom-call | flops 19200000000 | bytes 9600000 | tf_op jit(solution)/shard_map/block_one_middle/pallas_call | solution.py:785
  27.2 0.0 collective-permute-done
  27.2 0.0 copy-start
  27.2 0.2 copy-start.1
  27.6 0.0 copy-done.6
  27.6 0.0 copy-done.5
  27.6 1.1 %constant_dynamic-update-slice_fusion.1 = (bf16[2,288,256]{2,1,0:T(8,128)(2,1)S(1)}, bf16[2,288,256]{2,1,0:T(8,128)(2,1)S(1)}) fusion(bf16[2,288,256]{2,1,0:T(8,128)(2,1)S(1)} %slice_dynamic-update-slice_fusion.3, bf16[2,192,256]{2,1,0:T(8,128)(2,1)} %get-tuple-element.35, bf16[2,288,256]{2,1,0:T(8,128)(2,1)S(1)} %slice_dynamic-update-slice_fusion.1, ...), kind=kLoop, calls=%fused_computation.8 | loop fusion | bytes 786432
  28.7 2.1 %collective-permute-start.2 = (bf16[2,288,256]{2,1,0:T(8,128)(2,1)S(1)}, bf16[2,288,256]{2,1,0:T(8,128)(2,1)S(1)}, u32[]{:S(2)}, u32[]{:S(2)}) collective-permute-start(bf16[2,288,256]{2,1,0:T(8,128)(2,1)S(1)} %constant_dynamic-update-slice_fusion.3), channel_id=1, source_target_pairs={{1,0},{2,1},{3,2},{5,4},{6,5},{7,6},{9,8},{10,9},{11,10},{13,12},{... | collective-permute-start | bytes 884744 | tf_op jit(solution)/shard_map/ppermute | solution.py:676
  30.8 3.2 %collective-permute-start.1 = (bf16[2,288,256]{2,1,0:T(8,128)(2,1)S(1)}, bf16[2,288,256]{2,1,0:T(8,128)(2,1)S(1)}, u32[]{:S(2)}, u32[]{:S(2)}) collective-permute-start(bf16[2,288,256]{2,1,0:T(8,128)(2,1)S(1)} %constant_dynamic-update-slice_fusion), channel_id=1, source_target_pairs={{0,1},{1,2},{2,3},{4,5},{5,6},{6,7},{8,9},{9,10},{10,11},{12,13},{... | collective-permute-start | bytes 884744 | tf_op jit(solution)/shard_map/ppermute | solution.py:676
  34.0 9.7 %block_two_inner.1 = (bf16[21,2,64,256]{3,2,1,0:T(8,128)(2,1)}, bf16[8,256,128]{2,1,0:T(8,128)(2,1)}) custom-call(bf16[2,16,32,256]{3,2,1,0:T(8,128)(2,1)} %get-tuple-element.31.ends_ref, bf16[2,48,32,256]{3,2,1,0:T(8,128)(2,1)} %get-tuple-element.32.middle_ref, f32[2,2,64,384]{3,2,1,0:T(8,128)} %get-tuple-element.25.bias_ref, ...), custom_call_target="tpu_custom_call" | custom-call | flops 16800000000 | bytes 8400000 | tf_op jit(solution)/shard_map/block_two_inner/pallas_call | solution.py:820
  43.7 0.0 copy-done
  43.7 0.0 copy-done.1
  43.7 0.0 collective-permute-done.2.right_ref
  43.7 0.0 copy-start.3
  43.7 0.0 collective-permute-done.1.left_ref
  43.7 0.0 copy-start.4
  43.7 0.7 copy-done.3
  44.4 0.1 copy-done.4
  44.5 14.4 %block_two_border.1 = bf16[8,48,256]{2,1,0:T(8,128)(2,1)} custom-call(bf16[2,16,32,256]{3,2,1,0:T(8,128)(2,1)} %get-tuple-element.31.ends_ref, bf16[2,48,32,256]{3,2,1,0:T(8,128)(2,1)} %get-tuple-element.32.middle_ref, bf16[2,4,32,256]{3,2,1,0:T(8,128)(2,1)} %copy-done.1, bf16[2,4,32,256]{3,2,1,0:T(8,128)(2,1)} %copy-done, bf16[2,288,256]{2,1,0:T(8,128)(2,1)} %copy-done.4, ...), custom_call_target="tpu_custom_call" | custom-call | tf_op jit(solution)/shard_map/block_two_border/pallas_call | solution.py:846
  58.9 11.4 %all-gather = bf16[32,48,256]{2,1,0:T(8,128)(2,1)} all-gather(bf16[8,48,256]{2,1,0:T(8,128)(2,1)} %block_two_border.1), channel_id=2, replica_groups=mesh['var'=4,'ty'=2,'tx'=4] {'var'}, dimensions={0}, use_global_device_ids=true | all-gather | bytes 983040 | tf_op jit(solution)/shard_map/all_gather | solution.py:863
  70.3 4.9 %refinement.1 = f32[3,256,128]{2,1,0:T(8,128)} custom-call(bf16[4,8,48,256]{3,2,1,0:T(8,128)(2,1)} %bitcast.7, bf16[8,256,128]{2,1,0:T(8,128)(2,1)} %get-tuple-element.40.marks_ref, f32[64,128]{1,0:T(8,128)} %get-tuple-element.41.bias_ref, bf16[144,128]{1,0:T(8,128)(2,1)} %get-tuple-element.42.w_qvt, bf16[128,128]{1,0:T(8,128)(2,1)} %get-tuple-element.43.w_key, ...), custom_call_target="tpu_custom_call" | custom-call | tf_op jit(solution)/shard_map/refinement/pallas_call | solution.py:872
  (15 shorter events, 0.1 us)
Async XLA Ops:
  0.0 5.1 %copy-start.2 = (bf16[2,180,540]{2,0,1:T(2,128)(2,1)S(1)}, bf16[2,180,540]{2,0,1:T(2,128)(2,1)}, u32[]{:S(2)}) copy-start(bf16[2,180,540]{2,0,1:T(2,128)(2,1)} %param.13) | copy-start | bytes 1166404
  16.7 10.9 %copy-start.6 = (bf16[2,64,256]{2,1,0:T(8,128)(2,1)S(1)}, bf16[2,64,256]{2,1,0:T(8,128)(2,1)}, u32[]{:S(2)}) copy-start(bf16[2,64,256]{2,1,0:T(8,128)(2,1)} %get-tuple-element.34) | copy-start | bytes 196612
  16.7 10.9 %copy-start.5 = (bf16[2,64,256]{2,1,0:T(8,128)(2,1)S(1)}, bf16[2,64,256]{2,1,0:T(8,128)(2,1)}, u32[]{:S(2)}) copy-start(bf16[2,64,256]{2,1,0:T(8,128)(2,1)} %get-tuple-element.36) | copy-start | bytes 196612
  16.7 10.5 %collective-permute-start = (bf16[2,4,32,256]{3,2,1,0:T(8,128)(2,1)}, bf16[2,4,32,256]{3,2,1,0:T(8,128)(2,1)S(1)}, u32[]{:S(2)}, u32[]{:S(2)}) collective-permute-start(bf16[2,4,32,256]{3,2,1,0:T(8,128)(2,1)} %get-tuple-element.33), channel_id=1, source_target_pairs={{0,4},{4,0},{1,5},{5,1},{2,6},{6,2},{3,7},{7,3},{8,12},{12,8},{9,1... | collective-permute-start | bytes 393224 | tf_op jit(solution)/shard_map/ppermute | solution.py:681
  27.2 16.5 %copy-start = (bf16[2,4,32,256]{3,2,1,0:T(8,128)(2,1)}, bf16[2,4,32,256]{3,2,1,0:T(8,128)(2,1)S(1)}, u32[]{:S(2)}) copy-start(bf16[2,4,32,256]{3,2,1,0:T(8,128)(2,1)S(1)} %get-tuple-element.49.bottom_ref) | copy-start | bytes 393220
  27.2 16.4 %copy-start.1 = (bf16[2,4,32,256]{3,2,1,0:T(8,128)(2,1)}, bf16[2,4,32,256]{3,2,1,0:T(8,128)(2,1)S(1)}, u32[]{:S(2)}) copy-start(bf16[2,4,32,256]{3,2,1,0:T(8,128)(2,1)S(1)} %get-tuple-element.50.top_ref) | copy-start | bytes 393220
  28.7 15.0 %collective-permute-start.2 = (bf16[2,288,256]{2,1,0:T(8,128)(2,1)S(1)}, bf16[2,288,256]{2,1,0:T(8,128)(2,1)S(1)}, u32[]{:S(2)}, u32[]{:S(2)}) collective-permute-start(bf16[2,288,256]{2,1,0:T(8,128)(2,1)S(1)} %constant_dynamic-update-slice_fusion.3), channel_id=1, source_target_pairs={{1,0},{2,1},{3,2},{5,4},{6,5},{7,6},{9,8},{10,9},{11,10},{13,12},{... | collective-permute-start | bytes 884744 | tf_op jit(solution)/shard_map/ppermute | solution.py:676
  30.8 12.9 %collective-permute-start.1 = (bf16[2,288,256]{2,1,0:T(8,128)(2,1)S(1)}, bf16[2,288,256]{2,1,0:T(8,128)(2,1)S(1)}, u32[]{:S(2)}, u32[]{:S(2)}) collective-permute-start(bf16[2,288,256]{2,1,0:T(8,128)(2,1)S(1)} %constant_dynamic-update-slice_fusion), channel_id=1, source_target_pairs={{0,1},{1,2},{2,3},{4,5},{5,6},{6,7},{8,9},{9,10},{10,11},{12,13},{... | collective-permute-start | bytes 884744 | tf_op jit(solution)/shard_map/ppermute | solution.py:676
  43.7 0.7 copy-start.3
  43.7 0.8 %copy-start.4 = (bf16[2,288,256]{2,1,0:T(8,128)(2,1)}, bf16[2,288,256]{2,1,0:T(8,128)(2,1)S(1)}, u32[]{:S(2)}) copy-start(bf16[2,288,256]{2,1,0:T(8,128)(2,1)S(1)} %collective-permute-done.1.left_ref) | copy-start | bytes 884740

commit v4 on v3

--- a/solution.py
+++ b/solution.py
@@ -12,6 +12,7 @@
 SHIFT = 4
 SCALE = 4
 VAR_DEV = 2
+CODES = 8
 LANES = 128
 HEAD_ROWS = 32
 CLASSES = 4
@@ -378,7 +379,7 @@
 
 def first_kernel(heads, channels, strips, x_ref, labels_ref, bias_ref, *refs):
     ends = strips[0] == 0
-    *weights, y_ref, left_ref, right_ref = refs[:8]
+    *weights, y_ref, side_a_ref, side_b_ref = refs[:8]
     held, side = refs[-2:]
     breadth = x_ref.shape[1]
     count = breadth // WIN
@@ -423,16 +424,16 @@
                 rows = slice(at + r * SHIFT, at + (r + 1) * SHIFT)
                 side[0, rows] = windows[0][r, :SHIFT]
                 side[1, rows] = windows[-1][r, SHIFT:]
-        left_ref[v] = side[0].astype(BF16)
-        right_ref[v] = side[1].astype(BF16)
+        left, right = side[0].astype(BF16), side[1].astype(BF16)
+        even = is_even("tx")
+        side_a_ref[v] = jnp.where(even, right, left)
+        side_b_ref[v] = jnp.where(even, left, right)
     if ends:
-        if len(refs) == 11:
-            refs[8][...] = jnp.where(
-                lax.axis_index("ty") == 0, y_ref[:, 2 * WIN - SHIFT :], y_ref[:, :SHIFT]
-            )
-        else:
-            refs[8][...] = y_ref[:, :SHIFT]
-            refs[9][...] = y_ref[:, 2 * WIN - SHIFT :]
+        top, bottom = y_ref[:, :SHIFT], y_ref[:, 2 * WIN - SHIFT :]
+        even = is_even("ty")
+        refs[8][...] = jnp.where(even, bottom, top)
+        if len(refs) == 12:
+            refs[9][...] = jnp.where(even, top, bottom)
 
 
 def place_rows(store, ends_ref, middle_ref, v):
@@ -474,45 +475,71 @@
         y_ref[w] = results[w].astype(BF16).reshape(VAR_DEV, CELLS, lanes)
 
 
+def received(refs, axis, after, place):
+    value = refs[0][place].astype(F32)
+    other = refs[1][place].astype(F32) if len(refs) > 1 else 0.0
+    return jnp.where(is_even(axis) == after, value, other)
+
+
+def edge_kernel(swaps, *refs):
+    across, own, outs = refs[:swaps], refs[swaps : swaps + 4], refs[swaps + 4 :]
+    breadth = across[0].shape[2]
+    half = WIN * SHIFT
+    corner = SHIFT * SHIFT
+    for first in range(2):
+        ends, middle = own[2 * first : 2 * first + 2]
+        out = outs[first]
+        at_right = is_even("tx") == (first == 0)
+        last = out.shape[1] - corner
+        for v in range(VAR_DEV):
+            for start, after in ((0, False), (last, True)):
+                rows = received(across, "ty", after, v)
+                cells = jnp.where(at_right, rows[:, breadth - SHIFT :], rows[:, :SHIFT])
+                cells = jnp.concatenate([cells[r] for r in range(SHIFT)], axis=0)
+                out[v, start : start + corner] = cells.astype(BF16)
+            out[v, corner : corner + half] = ends[v, :half]
+            out[v, corner + half : last - half] = middle[v]
+            out[v, last - half : last] = ends[v, half:]
+
+
 def outer_kernel(
     heads,
     channels,
     group,
+    swaps,
     ends_ref,
     middle_ref,
-    top_ref,
-    bottom_ref,
-    left_ref,
-    right_ref,
-    inner_ref,
-    bias_ref,
     *refs,
 ):
-    *weights, w_recon, out_ref, rows_held, sides_held, x_held, y_held, acc = refs
+    across, sides, (inner_ref, bias_ref) = refs[:swaps], refs[swaps : swaps + 2], refs[swaps + 2 : swaps + 4]
+    refs = refs[swaps + 4 :]
+    *weights, w_recon, keep_ref, give_ref, rows_held, sides_held, x_held, y_held, acc = refs
     lanes = middle_ref.shape[3]
     height, breadth = middle_ref.shape[1] + 2 * WIN, middle_ref.shape[2]
     tall, wide = height + 2 * SHIFT, breadth + 2 * SHIFT
     strips, count = tall // WIN, wide // WIN
     always = iota((1, lanes), 1) == channels + CLASSES + 1
 
-    def marked(received):
-        return jnp.where(always, 1.0, received.astype(F32))
+    def marked(refs, axis, after, place):
+        return jnp.where(always, 1.0, received(refs, axis, after, place))
 
     for v in range(VAR_DEV):
         for end in range(2):
             outside, inside = (0, SHIFT) if end == 0 else (SHIFT, 0)
             corner = 0 if end == 0 else (tall - SHIFT) * SHIFT
-            received = top_ref if end == 0 else bottom_ref
             first = 0 if end == 0 else 2 * WIN - SHIFT
-            across = slice(SHIFT, SHIFT + breadth)
-            rows_held[outside : outside + SHIFT, across] = marked(received[v])
-            rows_held[inside : inside + SHIFT, across] = ends_ref[
+            between = slice(SHIFT, SHIFT + breadth)
+            rows_held[outside : outside + SHIFT, between] = marked(
+                across, "ty", end == 1, v
+            )
+            rows_held[inside : inside + SHIFT, between] = ends_ref[
                 v, first : first + SHIFT
             ].astype(F32)
             side_first = SHIFT * SHIFT if end == 0 else (tall - 2 * SHIFT) * SHIFT
-            for ref, at in ((left_ref, 0), (right_ref, wide - SHIFT)):
+            for side, at in ((0, 0), (1, wide - SHIFT)):
                 for rows, start in ((outside, corner), (inside, side_first)):
-                    piece = marked(ref[v, start : start + SHIFT * SHIFT])
+                    cut = (v, slice(start, start + SHIFT * SHIFT))
+                    piece = marked(sides, "tx", side == 1, cut)
                     rows_held[rows : rows + SHIFT, at : at + SHIFT] = piece.reshape(
                         SHIFT, SHIFT, lanes
                     )
@@ -530,8 +557,8 @@
             rows = slice(strip * WIN - SHIFT, (strip + 1) * WIN - SHIFT)
             cut = slice(strip * WIN * SHIFT, (strip + 1) * WIN * SHIFT)
             for end in range(2):
-                ref = left_ref if end == 0 else right_ref
-                piece = marked(ref[v, cut]).reshape(WIN, SHIFT, lanes)
+                piece = marked(sides, "tx", end == 1, (v, cut))
+                piece = piece.reshape(WIN, SHIFT, lanes)
                 at = 0 if end == 0 else WIN + SHIFT
                 own = sides_held[rows, at : at + SHIFT]
                 both = [piece, own] if end == 0 else [own, piece]
@@ -566,7 +593,7 @@
                 part = total[w, :, :, e * lanes : (e + 1) * lanes]
                 acc[rows, across] = part if e == 0 else acc[rows, across] + part
 
-    out_channels = out_ref.shape[1]
+    out_channels = keep_ref.shape[1]
 
     def finish(strip):
         rows = slice(1 + SHIFT + strip * WIN, 1 + SHIFT + (strip + 1) * WIN)
@@ -577,8 +604,9 @@
             + centre.reshape(WIN, breadth, LANES)
             + acc[rows, SHIFT + 1 : SHIFT + 1 + breadth, LANES : 2 * LANES]
         )
-        out_ref[strip] = windows_of(result).T[:out_channels].astype(BF16)
-
+        return windows_of(result).T[:out_channels].astype(BF16)
+
+    results = []
     scatter(0, lambda v: [y_held[w, v] for w in range(count)])
     for strip in range(1, strips):
         if strip == strips - 1:
@@ -594,36 +622,30 @@
                     y_held[slot + 1, v],
                 ],
             )
-        finish(strip - 1)
+        results.append(finish(strip - 1))
+    half = len(results) // 2
+    even = is_even("var")
+    for strip in range(half):
+        keep_ref[strip] = jnp.where(even, results[strip], results[strip + half])
+        give_ref[strip] = jnp.where(even, results[strip + half], results[strip])
 
 
 def refine_kernel(
-    heads, first_mark, parts_ref, marks_ref, bias_ref, w_qvt, w_key, w_projt, out_ref, spread_ref
+    heads, first_mark, mine_ref, other_ref, marks_ref, bias_ref, w_qvt, w_key, w_projt, out_ref, final
 ):
-    sources, strips, channels, strip_tokens = parts_ref.shape
+    strips, channels, strip_tokens = mine_ref.shape
     breadth = strip_tokens // WIN
     width = channels // heads
-
-    @pl.when(pl.program_id(0) == 0)
-    def _():
-        shape = spread_ref.shape
-        cell = iota(shape, 1) // SCALE
-        source = (cell % breadth // WIN) * CELLS + (cell // breadth) * WIN + cell % WIN
-        spread_ref[...] = one_hot(iota(shape, 0) == source)
-
     z = jnp.concatenate(
-        [
-            sum(parts_ref[s, strip].astype(F32) for s in range(sources))
-            for strip in range(strips)
-        ],
-        axis=1,
-    ) * (1.0 / (sources * VAR_DEV))
+        [mine_ref[s].astype(F32) + other_ref[s].astype(F32) for s in range(strips)], axis=1
+    ) * (1.0 / CODES)
     mean = jnp.sum(z, axis=0, keepdims=True) * (1.0 / channels)
     centred = z - mean
     spread = jnp.sum(centred * centred, axis=0, keepdims=True) * (1.0 / channels)
     normed = centred * lax.rsqrt(spread + EPSILON)
     tall = jnp.concatenate([normed, jnp.zeros((LANES - channels, normed.shape[1]), F32)], axis=0)
-    marks = jnp.concatenate([marks_ref[s].astype(F32) for s in range(strips)], axis=0)
+    first = lax.axis_index("var") % 2 * strips
+    marks = jnp.concatenate([marks_ref[first + s].astype(F32) for s in range(strips)], axis=0)
     lane = iota((1, LANES), 1)
     is_mark = (lane >= first_mark) & (lane < first_mark + MARKS)
     n = jnp.where(is_mark, marks, tall.T).astype(BF16)
@@ -652,7 +674,10 @@
     stacked = jnp.concatenate(
         [refined[:, s * strip_tokens : (s + 1) * strip_tokens] for s in range(strips)], axis=0
     )
-    wide = dot(stacked, spread_ref[...])
+    shape = (strip_tokens, WIN * breadth * SCALE)
+    cell = iota(shape, 1) // SCALE
+    source = (cell % breadth // WIN) * CELLS + (cell // breadth) * WIN + cell % WIN
+    wide = dot(stacked, one_hot(iota(shape, 0) == source))
     own = iota(wide.shape, 1) % SCALE == iota(wide.shape, 0) % SCALE
     wide = jnp.where(own, wide, 0.0).astype(BF16)
     shape = (wide.shape[0] // SCALE, wide.shape[0])
@@ -664,32 +689,34 @@
             first = (s * colours + c) * SCALE
             for y in range(WIN):
                 start = (s * WIN + y) * SCALE
-                out_ref[c, start : start + SCALE] = folded[
+                final[c, start : start + SCALE] = folded[
                     first : first + SCALE, y * row_lanes : (y + 1) * row_lanes
                 ]
-
-
-def exchanged(last, first, axis):
+    out_ref[...] = final[...].astype(BF16)
+
+
+def is_even(axis):
+    return lax.axis_index(axis) % 2 == 0
+
+
+def swap_pairs(strip, axis, first):
     count = lax.axis_size(axis)
-    up = [(i, i + 1) for i in range(count - 1)]
-    down = [(i + 1, i) for i in range(count - 1)]
-    return lax.ppermute(last, axis, up), lax.ppermute(first, axis, down)
-
-
-def swapped(strip, axis):
-    at_start = lax.axis_index(axis) == 0
-    received = lax.ppermute(strip, axis, [(0, 1), (1, 0)])
-    zero = jnp.zeros_like(received)
-    return jnp.where(at_start, zero, received), jnp.where(at_start, received, zero)
+    pairs = [(i, i + 1) for i in range(first, count - 1, 2)]
+    return lax.ppermute(strip, axis, pairs + [(j, i) for i, j in pairs])
+
+
+def whole_swap(a, bit):
+    count = lax.axis_size("var")
+    return lax.ppermute(a, "var", [(i, i ^ bit) for i in range(count)])
 
 
 def whole(a):
     return pl.BlockSpec(a.shape, lambda *i: (0,) * a.ndim)
 
 
-def params():
+def params(mebibytes):
     return pltpu.CompilerParams(
-        dimension_semantics=("arbitrary",), vmem_limit_bytes=56 * 1024 * 1024
+        dimension_semantics=("arbitrary",), vmem_limit_bytes=mebibytes * 1024 * 1024
     )
 
 
@@ -748,7 +775,7 @@
             pltpu.VMEM((heads, WIN, LANES), F32),
             pltpu.VMEM((round_up(2 * heads, 8), swin_bias.shape[2]), F32),
         ],
-        compiler_params=params(),
+        compiler_params=params(10),
         name="prepare",
     )(*operands)
     *swin, recon, bias, refine_qvt, refine_key, refine_projt, refine_grid = prepared
@@ -792,27 +819,26 @@
                 pltpu.VMEM((len(places) * tokens, lanes), F32),
                 pltpu.VMEM((2, rows * SHIFT, lanes), F32),
             ],
-            compiler_params=params(),
+            compiler_params=params(12 if places[0] == 0 else 18),
             cost_estimate=cost(len(places) * breadth // WIN * VAR_DEV),
             name=name,
         )(features, labels_across, *arrays)
 
-    y_ends, left_ends, right_ends, *own_ends = block_one((0, strips - 1), "block_one_ends")
-    top, bottom = swapped(*own_ends, "ty") if pair_axis else exchanged(*own_ends[::-1], "ty")
-    y_middle, left_middle, right_middle = block_one(tuple(range(1, strips - 1)), "block_one_middle")
-    half = WIN * SHIFT
-    strips_out = []
-    for ends, middle, cut in (
-        (right_ends, right_middle, slice(breadth - SHIFT, breadth)),
-        (left_ends, left_middle, slice(0, SHIFT)),
-    ):
-        corners = [a[:, :, cut].reshape(VAR_DEV, SHIFT * SHIFT, lanes) for a in (top, bottom)]
-        strips_out.append(
-            jnp.concatenate(
-                [corners[0], ends[:, :half], middle, ends[:, half:], corners[1]], axis=1
-            )
-        )
-    sides = exchanged(*strips_out, "tx")
+    y_ends, a_ends, b_ends, *own_ends = block_one((0, strips - 1), "block_one_ends")
+    across = [swap_pairs(own, "ty", first) for first, own in enumerate(own_ends)]
+    y_middle, a_middle, b_middle = block_one(tuple(range(1, strips - 1)), "block_one_middle")
+    operands = (*across, a_ends, a_middle, b_ends, b_middle)
+    strip_shape = jax.ShapeDtypeStruct((VAR_DEV, (height + 2 * SHIFT) * SHIFT, lanes), BF16)
+    strips_out = pl.pallas_call(
+        functools.partial(edge_kernel, len(across)),
+        grid=(1,),
+        in_specs=[whole(a) for a in operands],
+        out_specs=[whole(strip_shape)] * 2,
+        out_shape=[strip_shape] * 2,
+        compiler_params=params(6),
+        name="edges",
+    )(*operands)
+    sides = [swap_pairs(strip, "tx", first) for first, strip in enumerate(strips_out)]
 
     arrays, specs = block_specs(1)
     inner_count = (strips - 1) * (breadth // WIN - 1)
@@ -833,7 +859,7 @@
             pltpu.VMEM((height, breadth, lanes), F32),
             pltpu.VMEM((inner_count, VAR_DEV, CELLS, lanes), F32),
         ],
-        compiler_params=params(),
+        compiler_params=params(20),
         cost_estimate=cost(inner_count * VAR_DEV),
         name="block_two_inner",
     )(y_ends, y_middle, *arrays)
@@ -841,14 +867,14 @@
     tall, wide = height + 2 * SHIFT, breadth + 2 * SHIFT
     slots = 2 * (tall + wide) // WIN - 4
     group = next(g for g in range(24, 0, -1) if slots % g == 0)
-    operands = (y_ends, y_middle, top, bottom, *sides, inner)
-    partial_shape = jax.ShapeDtypeStruct((strips, out_channels, tokens), BF16)
-    partial = pl.pallas_call(
-        functools.partial(outer_kernel, heads, channels, group),
+    operands = (y_ends, y_middle, *across, *sides, inner)
+    half_shape = jax.ShapeDtypeStruct((strips // 2, out_channels, tokens), BF16)
+    keep, give = pl.pallas_call(
+        functools.partial(outer_kernel, heads, channels, group, len(across)),
         grid=(1,),
         in_specs=[*[whole(a) for a in operands], *specs, whole(recon)],
-        out_specs=whole(partial_shape),
-        out_shape=partial_shape,
+        out_specs=[whole(half_shape)] * 2,
+        out_shape=[half_shape] * 2,
         scratch_shapes=[
             pltpu.VMEM((WIN, wide, lanes), F32),
             pltpu.VMEM((height, 2 * WIN, lanes), F32),
@@ -856,31 +882,29 @@
             pltpu.VMEM((slots, VAR_DEV, CELLS, lanes), BF16),
             pltpu.VMEM((tall + WIN, wide, lanes), F32),
         ],
-        compiler_params=params(),
+        compiler_params=params(26),
         name="block_two_border",
     )(*operands, *arrays, recon)
 
-    parts = lax.all_gather(partial, "var", axis=0)
+    mine = (keep.astype(F32) + whole_swap(give, 1).astype(F32)).astype(BF16)
+    other = whole_swap(mine, 2)
     colours = out_channels // (SCALE * SCALE)
-    chunk = next(c for c in (8, 4, 2, 1) if strips % c == 0)
-    operands = (parts, marks, refine_grid, refine_qvt, refine_key, refine_projt)
-    in_specs = [whole(a) for a in operands]
-    in_specs[0] = pl.BlockSpec(
-        (parts.shape[0], chunk, out_channels, tokens), lambda i: (0, i, 0, 0)
-    )
-    in_specs[1] = pl.BlockSpec((chunk, tokens, LANES), lambda i: (i, 0, 0))
-    return pl.pallas_call(
+    operands = (mine, other, marks, refine_grid, refine_qvt, refine_key, refine_projt)
+    out_shape = (colours, height * SCALE // 2, breadth * SCALE)
+    refined = pl.pallas_call(
         functools.partial(refine_kernel, refine_heads, channels % LANES),
-        grid=(strips // chunk,),
-        in_specs=in_specs,
-        out_specs=pl.BlockSpec(
-            (colours, chunk * WIN * SCALE, breadth * SCALE), lambda i: (0, i, 0)
-        ),
-        out_shape=jax.ShapeDtypeStruct((colours, height * SCALE, breadth * SCALE), F32),
-        scratch_shapes=[pltpu.VMEM((tokens, tokens * SCALE), BF16)],
-        compiler_params=params(),
+        grid=(1,),
+        in_specs=[whole(a) for a in operands],
+        out_specs=pl.BlockSpec(out_shape, lambda i: (0, 0, 0)),
+        out_shape=jax.ShapeDtypeStruct(out_shape, BF16),
+        scratch_shapes=[pltpu.VMEM(out_shape, F32)],
+        compiler_params=params(8),
         name="refinement",
     )(*operands)
+    received = whole_swap(refined, 1)
+    even = is_even("var")
+    halves = jnp.where(even, refined, received), jnp.where(even, received, refined)
+    return jnp.concatenate(halves, axis=1).astype(F32)
 
 
 def solution(mesh):

time: 76.7 us -> 50.7 us (0.66); the launches traced: 75.2 us -> 50.5 us
  Pallas kernels: 48.9 us -> 31.4 us
  blocking collectives: 11.4 us -> 0 us
  local copies, waits for them, and re-layouts: 8.06 us -> 3.21 us
  waiting for transfers between devices: 0.01 us -> 4.71 us
  starting transfers between devices: 6.59 us -> 10.2 us
  other arithmetic: 0.02 us -> 0.82 us
    all_gather x1 -> x0, blocking collectives: 11.4 us -> none  [local(): parts = lax.all_gather(partial, 'var', axis=0)]
    pallas_call x2, Pallas kernels: 14.6 us -> 9.21 us  [block_one(): pl.pallas_call(functools.partial(first_kernel, heads, channels, places),...]
    unnamed x25 -> x20, local copies, waits for them, and re-layouts: 7.97 us -> 3.21 us
    ppermute x3 -> x6, waiting for transfers between devices: 0.01 us -> 4.71 us  [the longest x3 4.7 us: whole_swap(): return lax.ppermute(a, 'var', [(i, i ^ bit) for i in range(count)])]
    ppermute x3 -> x6, starting transfers between devices: 6.59 us -> 10.2 us  [the longest x3 6.04 us: swap_pairs(): return lax.ppermute(strip, axis, pairs + [(j, i) for i, j in pairs])]
    pallas_call x1 -> x2, Pallas kernels: 14.4 us -> 10.9 us  [the longest x1 10.9 us: local(): pl.pallas_call(functools.partial(outer_kernel, heads, channels, group, le...]
    pallas_call x1, Pallas kernels: 4.88 us -> 1.7 us  [local(): pl.pallas_call(functools.partial(refine_kernel, refine_heads, channels %...]
    pallas_call x1, Pallas kernels: 9.67 us -> 6.68 us  [local(): pl.pallas_call(functools.partial(inner_kernel, heads, channels, group), g...]
  transfers between devices with their start and end apart: 3 -> 6, of which waited for: 0 -> 3; matrix products, arithmetic and copies ran while one was open for 0% -> 0% of each run, Pallas kernels for 25% -> 26%
where the time goes in v4:
time: 50.7 us; the launch traced here: 50.5 us
  Pallas kernels  31.4 us (62%)
  starting transfers between devices  10.2 us (20%)
  waiting for transfers between devices  4.71 us (9%)
  local copies, waits for them, and re-layouts  3.21 us (6%)
  other arithmetic  0.82 us (2%)
    pallas_call x1, Pallas kernels, local(): pl.pallas_call(functools.partial(outer_kernel, heads, channels, group, le...  10.9 us
    pallas_call x2, Pallas kernels, block_one(): pl.pallas_call(functools.partial(first_kernel, heads, channels, places),...  9.21 us
    pallas_call x1, Pallas kernels, local(): pl.pallas_call(functools.partial(inner_kernel, heads, channels, group), g...  6.68 us
    ppermute x3, starting transfers between devices, swap_pairs(): return lax.ppermute(strip, axis, pairs + [(j, i) for i, j in pairs])  6.04 us
    ppermute x3, waiting for transfers between devices, whole_swap(): return lax.ppermute(a, 'var', [(i, i ^ bit) for i in range(count)])  4.7 us
    ppermute x3, starting transfers between devices, whole_swap(): return lax.ppermute(a, 'var', [(i, i ^ bit) for i in range(count)])  4.12 us
    unnamed x20, local copies, waits for them, and re-layouts  3.21 us
    pallas_call x1, Pallas kernels, local(): pl.pallas_call(functools.partial(prepare_kernel, heads), grid=(1,), in_sp...  2.84 us
  transfers between devices with their start and end apart: 6, of which 3 were waited for; matrix products, arithmetic and copies ran while one was open for 0% of the time, Pallas kernels for 26%

profile of v4, /device:TPU:9, one launch (start us, length us, event | category | flops | bytes accessed | tf_op | source)
XLA Modules:
  0.0 50.5 jit_solution(4634494865210913124)
XLA Ops:
  0.0 0.0 copy-start.7
  0.0 0.0 copy-start.2
  0.0 0.0 copy-start
  0.0 0.0 copy-start.1
  0.0 0.0 copy-start.3
  0.0 0.0 copy-start.4
  0.0 1.1 %copy.13.qkv_ref = bf16[2,180,540]{2,1,0:T(8,128)(2,1)S(1)} copy(bf16[2,180,540]{2,0,1:T(2,128)(2,1)} %param.13) | data formatting | bytes 777600 | tf_op args[2]
  1.2 0.0 copy-start.5
  1.2 0.0 copy-start.6
  1.2 1.0 %copy.14.proj_ref = bf16[2,180,180]{2,1,0:T(8,128)(2,1)S(1)} copy(bf16[2,180,180]{2,0,1:T(2,128)(2,1)} %param.14) | data formatting | bytes 259200 | tf_op args[3]
  2.2 1.0 %copy.15.up_ref = bf16[2,180,360]{2,1,0:T(8,128)(2,1)S(1)} copy(bf16[2,180,360]{2,0,1:T(2,128)(2,1)} %param.15) | data formatting | bytes 518400 | tf_op args[4]
  3.2 0.0 copy-done.7
  3.3 0.0 copy-done.2
  3.3 0.0 copy-done
  3.3 0.0 copy-done.1
  3.3 0.0 copy-done.3
  3.3 0.0 copy-done.4
  3.3 2.8 %prepare.1 = (bf16[2,400,256]{2,1,0:T(8,128)(2,1)S(1)}, bf16[2,256,256]{2,1,0:T(8,128)(2,1)S(1)}, bf16[2,256,256]{2,1,0:T(8,128)(2,1)S(1)}, bf16[2,256,384]{2,1,...) custom-call(bf16[2,180,540]{2,1,0:T(8,128)(2,1)S(1)} %copy.13.qkv_re, ...), custom_call_target="tpu_custom_call" | custom-call | tf_op jit(solution)/shard_map/prepare/pallas_call | solution.py:768
  6.2 0.0 copy-done.5
  6.2 0.0 copy-done.6
  6.2 2.9 %block_one_ends.1 = (bf16[2,16,32,256]{3,2,1,0:T(8,128)(2,1)S(1)}, bf16[2,64,256]{2,1,0:T(8,128)(2,1)S(1)}, bf16[2,64,256]{2,1,0:T(8,128)(2,1)S(1)}, bf16[2,4,32,256]{3,2,1,0:T(8,128)(2,1)S(1)}) custom-call(bf16[64,32,180]{2,1,0:T(8,128)(2,1)S(1)} %copy-done.5, s32[32,64]{1,0:T(8,128)S(1)} %bitcast.9, ...), custom_call_target="tpu_custom_call" | custom-call | flops 6400000000 | bytes 3200000 | tf_op jit(solution)/shard_map/block_one_ends/pallas_call | solution.py:812
  9.1 1.3 %collective-permute-start = (bf16[2,4,32,256]{3,2,1,0:T(8,128)(2,1)S(1)}, bf16[2,4,32,256]{3,2,1,0:T(8,128)(2,1)S(1)}, u32[]{:S(2)}, u32[]{:S(2)}) collective-permute-start(bf16[2,4,32,256]{3,2,1,0:T(8,128)(2,1)S(1)} %get-tuple-element.37), channel_id=1, source_target_pairs={{0,4},{4,0},{1,5},{5,1},{2,6},{6,2},{3,7},{7,3},{8,12},{12,8},{9,1... | collective-permute-start | bytes 393224 | tf_op jit(solution)/shard_map/ppermute | solution.py:705
  10.4 6.3 %block_one_middle.1 = (bf16[2,48,32,256]{3,2,1,0:T(8,128)(2,1)S(1)}, bf16[2,192,256]{2,1,0:T(8,128)(2,1)S(1)}, bf16[2,192,256]{2,1,0:T(8,128)(2,1)S(1)}) custom-call(bf16[64,32,180]{2,1,0:T(8,128)(2,1)S(1)} %copy-done.5, s32[32,64]{1,0:T(8,128)S(1)} %bitcast.10, f32[2,2,64,384]{3,2,1,0:T(8,128)S(1)} %get-tuple-element.29.bias_ref.refs_4_, ...), custom_call_target="tpu_custom_call" | custom-call | flops 19200000000 | bytes 9600000 | tf_op jit(solution)/shard_map/block_one_middle/pallas_call | solution.py:812
  16.7 0.0 collective-permute-done.refs_0_
  16.7 0.1 edges.1
  16.8 0.4 collective-permute-start.1
  17.2 4.3 %collective-permute-start.2 = (bf16[2,288,256]{2,1,0:T(8,128)(2,1)S(1)}, bf16[2,288,256]{2,1,0:T(8,128)(2,1)S(1)}, u32[]{:S(2)}, u32[]{:S(2)}) collective-permute-start(bf16[2,288,256]{2,1,0:T(8,128)(2,1)S(1)} %get-tuple-element.43), channel_id=1, source_target_pairs={{1,2},{2,1},{5,6},{6,5},{9,10},{10,9},{13,14},{14,13},{17,18},{18,... | collective-permute-start | bytes 884744 | tf_op jit(solution)/shard_map/ppermute | solution.py:705
  21.5 6.7 %block_two_inner.1 = (bf16[21,2,64,256]{3,2,1,0:T(8,128)(2,1)S(1)}, bf16[8,256,128]{2,1,0:T(8,128)(2,1)S(1)}) custom-call(bf16[2,16,32,256]{3,2,1,0:T(8,128)(2,1)S(1)} %get-tuple-element.35.ends_ref, bf16[2,48,32,256]{3,2,1,0:T(8,128)(2,1)S(1)} %get-tuple-element.36.middle_ref, f32[2,2,64,384]{3,2,1,0:T(8,128)S(1)} %get-tuple-element.29.bias_ref.refs_4_, ...), custom_call_target="tpu_custom_call" | custom-call | flops 16800000000 | bytes 8400000 | tf_op jit(solution)/shard_map/block_two_inner/pallas_call | solution.py:846
  28.2 0.0 collective-permute-done.1.refs_1_
  28.2 0.0 collective-permute-done.2.refs_2_
  28.2 10.9 %block_two_border.1 = (bf16[4,48,256]{2,1,0:T(8,128)(2,1)S(1)}, bf16[4,48,256]{2,1,0:T(8,128)(2,1)S(1)}) custom-call(bf16[2,16,32,256]{3,2,1,0:T(8,128)(2,1)S(1)} %get-tuple-element.35.ends_ref, bf16[2,48,32,256]{3,2,1,0:T(8,128)(2,1)S(1)} %get-tuple-element.36.middle_ref, bf16[2,4,32,256]{3,2,1,0:T(8,128)(2,1)S(1)} %collective-permute-done.refs_0_, ...), custom_call_target="tpu_custom_call" | custom-call | tf_op jit(solution)/shard_map/block_two_border/pallas_call | solution.py:872
  39.1 1.6 %collective-permute-start.3 = (bf16[4,48,256]{2,1,0:T(8,128)(2,1)S(1)}, bf16[4,48,256]{2,1,0:T(8,128)(2,1)S(1)}, u32[]{:S(2)}, u32[]{:S(2)}) collective-permute-start(bf16[4,48,256]{2,1,0:T(8,128)(2,1)S(1)} %get-tuple-element.47), channel_id=1, source_target_pairs={{0,8},{8,0},{16,24},{24,16},{1,9},{9,1},{17,25},{25,17},{2,10},{10... | collective-permute-start | bytes 294920 | tf_op jit(solution)/shard_map/ppermute | solution.py:710
  40.7 0.9 %collective-permute-done.3 = bf16[4,48,256]{2,1,0:T(8,128)(2,1)S(1)} collective-permute-done((bf16[4,48,256]{2,1,0:T(8,128)(2,1)S(1)}, bf16[4,48,256]{2,1,0:T(8,128)(2,1)S(1)}, u32[]{:S(2)}, u32[]{:S(2)}) %collective-permute-start.3) | collective-permute-done | bytes 98336 | tf_op jit(solution)/shard_map/ppermute | solution.py:710
  41.7 1.3 %collective-permute-start.4 = (bf16[4,48,256]{2,1,0:T(8,128)(2,1)S(1)}, bf16[4,48,256]{2,1,0:T(8,128)(2,1)S(1)}, u32[]{:S(2)}, u32[]{:S(2)}) collective-permute-start(bf16[4,48,256]{2,1,0:T(8,128)(2,1)S(1)} %add_convert_fusion.mine_ref), channel_id=1, source_target_pairs={{0,16},{8,24},{16,0},{24,8},{1,17},{9,25},{17,1},{25,9},{2,18},{10... | collective-permute-start | bytes 294920 | tf_op jit(solution)/shard_map/ppermute | solution.py:710
  43.0 2.8 %collective-permute-done.4.other_ref = bf16[4,48,256]{2,1,0:T(8,128)(2,1)S(1)} collective-permute-done((bf16[4,48,256]{2,1,0:T(8,128)(2,1)S(1)}, bf16[4,48,256]{2,1,0:T(8,128)(2,1)S(1)}, u32[]{:S(2)}, u32[]{:S(2)}) %collective-permute-start.4) | collective-permute-done | bytes 98336 | tf_op jit(solution)/shard_map/ppermute | solution.py:710
  45.8 1.7 %refinement.1 = bf16[3,128,128]{2,1,0:T(8,128)(2,1)S(1)} custom-call(bf16[4,48,256]{2,1,0:T(8,128)(2,1)S(1)} %add_convert_fusion.mine_ref, bf16[4,48,256]{2,1,0:T(8,128)(2,1)S(1)} %collective-permute-done.4.other_ref, bf16[8,256,128]{2,1,0:T(8,128)(2,1)S(1)} %get-tuple-element.48.marks_ref, f32[64,128]{1,0:T(8,128)S(1)} %get-tuple-element.49.bias_ref, ...), custom_call_target="tpu_custom_call" | custom-call | tf_op jit(solution)/shard_map/refinement/pallas_call | solution.py:894
  47.5 1.3 %collective-permute-start.5 = (bf16[3,128,128]{2,1,0:T(8,128)(2,1)S(1)}, bf16[3,128,128]{2,1,0:T(8,128)(2,1)S(1)}, u32[]{:S(2)}, u32[]{:S(2)}) collective-permute-start(bf16[3,128,128]{2,1,0:T(8,128)(2,1)S(1)} %refinement.1), channel_id=1, source_target_pairs={{0,8},{8,0},{16,24},{24,16},{1,9},{9,1},{17,25},{25,17},{2,10},{10... | collective-permute-start | bytes 294920 | tf_op jit(solution)/shard_map/ppermute | solution.py:710
  48.8 0.9 %collective-permute-done.5 = bf16[3,128,128]{2,1,0:T(8,128)(2,1)S(1)} collective-permute-done((bf16[3,128,128]{2,1,0:T(8,128)(2,1)S(1)}, bf16[3,128,128]{2,1,0:T(8,128)(2,1)S(1)}, u32[]{:S(2)}, u32[]{:S(2)}) %collective-permute-start.5) | collective-permute-done | bytes 98336 | tf_op jit(solution)/shard_map/ppermute | solution.py:710
  49.7 0.8 %maximum_convert_fusion = f32[3,256,128]{2,1,0:T(8,128)} fusion(bf16[3,128,128]{2,1,0:T(8,128)(2,1)S(1)} %get-tuple-element.54, bf16[3,128,128]{2,1,0:T(8,128)(2,1)S(1)} %get-tuple-element.53), kind=kLoop, calls=%fused_computation.1 | loop fusion | flops 393216 | bytes 589824 | tf_op jit(solution)/shard_map/convert_element_type | solution.py:907
  (3 shorter events, 0.1 us)
Async XLA Ops:
  0.0 3.2 %copy-start.7 = (bf16[2,360,180]{1,0,2:T(2,128)(2,1)S(1)}, bf16[2,360,180]{1,0,2:T(2,128)(2,1)}, u32[]{:S(2)}) copy-start(bf16[2,360,180]{1,0,2:T(2,128)(2,1)} %param.16) | copy-start | bytes 777604
  0.0 3.3 %copy-start.2 = (f32[2,6,225]{2,0,1:T(2,128)S(1)}, f32[2,6,225]{2,0,1:T(2,128)}, u32[]{:S(2)}) copy-start(f32[2,6,225]{2,0,1:T(2,128)} %param.17) | copy-start | bytes 32404
  0.0 3.3 %copy-start = (bf16[9,180,48]{1,2,0:T(8,128)(2,1)S(1)}, bf16[9,180,48]{1,2,0:T(8,128)(2,1)}, u32[]{:S(2)}) copy-start(bf16[9,180,48]{1,2,0:T(8,128)(2,1)} %param.18) | copy-start | bytes 466564
  0.0 3.3 %copy-start.1 = (bf16[48,144]{1,0:T(8,128)(2,1)S(1)}, bf16[48,144]{1,0:T(8,128)(2,1)}, u32[]{:S(2)}) copy-start(bf16[48,144]{1,0:T(8,128)(2,1)} %refine_qkv_ref.1) | copy-start | bytes 41476
  0.0 3.3 %copy-start.3 = (bf16[48,48]{1,0:T(8,128)(2,1)S(1)}, bf16[48,48]{1,0:T(8,128)(2,1)}, u32[]{:S(2)}) copy-start(bf16[48,48]{1,0:T(8,128)(2,1)} %refine_proj_ref.1) | copy-start | bytes 13828
  0.0 3.3 %copy-start.4 = (f32[2,225]{1,0:T(2,128)S(1)}, f32[2,225]{1,0:T(2,128)}, u32[]{:S(2)}) copy-start(f32[2,225]{1,0:T(2,128)} %refine_bias_ref.1) | copy-start | bytes 5404
  1.2 5.0 %copy-start.5 = (bf16[64,32,180]{2,1,0:T(8,128)(2,1)S(1)}, bf16[64,32,180]{2,1,0:T(8,128)(2,1)}, u32[]{:S(2)}) copy-start(bf16[64,32,180]{2,1,0:T(8,128)(2,1)} %x_ref.3) | copy-start | bytes 2211844
  1.2 5.0 %copy-start.6 = (s32[64,32]{0,1:T(8,128)S(1)}, s32[64,32]{0,1:T(8,128)}, u32[]{:S(2)}) copy-start(s32[64,32]{0,1:T(8,128)} %param.12) | copy-start | bytes 24580
  9.1 7.6 %collective-permute-start = (bf16[2,4,32,256]{3,2,1,0:T(8,128)(2,1)S(1)}, bf16[2,4,32,256]{3,2,1,0:T(8,128)(2,1)S(1)}, u32[]{:S(2)}, u32[]{:S(2)}) collective-permute-start(bf16[2,4,32,256]{3,2,1,0:T(8,128)(2,1)S(1)} %get-tuple-element.37), channel_id=1, source_target_pairs={{0,4},{4,0},{1,5},{5,1},{2,6},{6,2},{3,7},{7,3},{8,12},{12,8},{9,1... | collective-permute-start | bytes 393224 | tf_op jit(solution)/shard_map/ppermute | solution.py:705
  16.8 11.4 %collective-permute-start.1 = (bf16[2,288,256]{2,1,0:T(8,128)(2,1)S(1)}, bf16[2,288,256]{2,1,0:T(8,128)(2,1)S(1)}, u32[]{:S(2)}, u32[]{:S(2)}) collective-permute-start(bf16[2,288,256]{2,1,0:T(8,128)(2,1)S(1)} %get-tuple-element.42), channel_id=1, source_target_pairs={{0,1},{2,3},{1,0},{3,2},{4,5},{6,7},{5,4},{7,6},{8,9},{10,11},{9,8... | collective-permute-start | bytes 884744 | tf_op jit(solution)/shard_map/ppermute | solution.py:705
  17.2 11.0 %collective-permute-start.2 = (bf16[2,288,256]{2,1,0:T(8,128)(2,1)S(1)}, bf16[2,288,256]{2,1,0:T(8,128)(2,1)S(1)}, u32[]{:S(2)}, u32[]{:S(2)}) collective-permute-start(bf16[2,288,256]{2,1,0:T(8,128)(2,1)S(1)} %get-tuple-element.43), channel_id=1, source_target_pairs={{1,2},{2,1},{5,6},{6,5},{9,10},{10,9},{13,14},{14,13},{17,18},{18,... | collective-permute-start | bytes 884744 | tf_op jit(solution)/shard_map/ppermute | solution.py:705
  39.1 2.5 %collective-permute-start.3 = (bf16[4,48,256]{2,1,0:T(8,128)(2,1)S(1)}, bf16[4,48,256]{2,1,0:T(8,128)(2,1)S(1)}, u32[]{:S(2)}, u32[]{:S(2)}) collective-permute-start(bf16[4,48,256]{2,1,0:T(8,128)(2,1)S(1)} %get-tuple-element.47), channel_id=1, source_target_pairs={{0,8},{8,0},{16,24},{24,16},{1,9},{9,1},{17,25},{25,17},{2,10},{10... | collective-permute-start | bytes 294920 | tf_op jit(solution)/shard_map/ppermute | solution.py:710
  41.7 4.1 %collective-permute-start.4 = (bf16[4,48,256]{2,1,0:T(8,128)(2,1)S(1)}, bf16[4,48,256]{2,1,0:T(8,128)(2,1)S(1)}, u32[]{:S(2)}, u32[]{:S(2)}) collective-permute-start(bf16[4,48,256]{2,1,0:T(8,128)(2,1)S(1)} %add_convert_fusion.mine_ref), channel_id=1, source_target_pairs={{0,16},{8,24},{16,0},{24,8},{1,17},{9,25},{17,1},{25,9},{2,18},{10... | collective-permute-start | bytes 294920 | tf_op jit(solution)/shard_map/ppermute | solution.py:710
  47.5 2.2 %collective-permute-start.5 = (bf16[3,128,128]{2,1,0:T(8,128)(2,1)S(1)}, bf16[3,128,128]{2,1,0:T(8,128)(2,1)S(1)}, u32[]{:S(2)}, u32[]{:S(2)}) collective-permute-start(bf16[3,128,128]{2,1,0:T(8,128)(2,1)S(1)} %refinement.1), channel_id=1, source_target_pairs={{0,8},{8,0},{16,24},{24,16},{1,9},{9,1},{17,25},{25,17},{2,10},{10... | collective-permute-start | bytes 294920 | tf_op jit(solution)/shard_map/ppermute | solution.py:710

commit v5 on v4

--- a/solution.py
+++ b/solution.py
@@ -17,6 +17,7 @@
 HEAD_ROWS = 32
 CLASSES = 4
 MARKS = CLASSES + 2
+CONSTANT = -2.0
 SIDE = 2 * WIN - 1
 
 EPSILON = 1e-05
@@ -51,35 +52,49 @@
     return dot(a, b, dims).astype(BF16)
 
 
-def pad_matrix(rows, size):
-    return one_hot(iota((rows, size), 0) == iota((rows, size), 1))
-
-
-def head_matrix(rows, size, heads, width, first=0):
-    row = iota((rows, size), 0)
-    unit = row % HEAD_ROWS
-    source = first + row // HEAD_ROWS * width + unit
-    keep = (unit < width) & (row < heads * HEAD_ROWS)
-    return one_hot(keep & (iota((rows, size), 1) == source))
-
-
-def query_labels(rows, lanes, first_row, first_lane):
-    row = iota((rows, lanes), 0) - first_row
-    lane = iota((rows, lanes), 1) - first_lane
-    is_class = (row >= 0) & (row < CLASSES)
-    is_pad = row == CLASSES
-    same = is_class & (row == lane)
-    always = lane == CLASSES + 1
-    return jnp.where(same, BIG, 0.0) - jnp.where(always & (is_class | is_pad), BIG, 0.0)
-
-
-def key_labels(rows, lanes, first_row, first_lane):
-    row = iota((rows, lanes), 0) - first_row
-    lane = iota((rows, lanes), 1) - first_lane
+def pick_rows(source, size):
+    return one_hot(iota((1, size), 1) == source)
+
+
+def pick_columns(source, size):
+    return one_hot(iota((size, 1), 0) == source)
+
+
+def head_source(index, heads, width, first=0):
+    unit = index % HEAD_ROWS
+    keep = (unit < width) & (index < heads * HEAD_ROWS)
+    return jnp.where(keep, first + index // HEAD_ROWS * width + unit, -1)
+
+
+def query_value_source(heads, width, channels):
+    row = iota((2 * heads * HEAD_ROWS + 16, 1), 0)
+    values = row - heads * HEAD_ROWS - 16
+    return jnp.where(
+        values < 0,
+        head_source(row, heads, width),
+        head_source(jnp.maximum(values, 0), heads, width, 2 * channels),
+    )
+
+
+def query_value_marks(heads, width, lanes, first_lane):
+    row = iota((2 * heads * HEAD_ROWS + 16, 1), 0)
+    lane = iota((1, lanes), 1) - first_lane
+    mark = row - heads * HEAD_ROWS
+    is_class = (mark >= 0) & (mark < CLASSES)
+    differ = jnp.where(is_class | (mark == CLASSES), -BIG / CONSTANT, 0.0)
+    unit = (mark - 16) % HEAD_ROWS
+    ones = jnp.where((mark >= 16) & (unit == width), 1.0 / CONSTANT, 0.0)
+    same = jnp.where(is_class & (mark == lane), BIG, 0.0)
+    return same + jnp.where(lane == CLASSES + 1, differ + ones, 0.0)
+
+
+def key_marks(rows, lanes, first_row, first_lane):
+    row = iota((rows, 1), 0) - first_row
+    lane = iota((1, lanes), 1) - first_lane
     is_class = (lane >= 0) & (lane < CLASSES)
-    is_pad = lane == CLASSES
-    add = is_class & (row == lane) | is_pad & (row == CLASSES + 1)
-    return jnp.where(add, 1.0, 0.0) - jnp.where(is_pad & (row == CLASSES), 1.0, 0.0)
+    same = jnp.where(is_class & (row == lane), 1.0, 0.0)
+    pad = jnp.where(row == CLASSES, -1.0, jnp.where(row == CLASSES + 1, 1.0 / CONSTANT, 0.0))
+    return same + jnp.where(lane == CLASSES, pad, 0.0)
 
 
 def bias_rows(table, turn, flip_rows, flip_cols):
@@ -119,53 +134,108 @@
 
 def prepare_kernel(
     heads,
-    qkv_ref,
-    proj_ref,
-    up_ref,
-    down_ref,
-    swin_bias_ref,
-    recon_ref,
-    refine_qkv_ref,
-    refine_proj_ref,
-    refine_bias_ref,
-    qvt_out,
-    key_out,
-    proj_out,
-    up_out,
-    down_out,
-    recon_out,
-    bias_out,
-    refine_qvt_out,
-    refine_key_out,
-    refine_proj_out,
-    refine_bias_out,
-    rows_ref,
-    tables_ref,
+    features_ref,
+    labels_ref,
+    *refs,
 ):
-    blocks, channels, hidden = up_ref.shape
+    sources, outs, scratch = refs[:9], refs[9:22], refs[22:]
+    held, (rows_ref, tables_ref, semaphores) = scratch[:9], scratch[9:]
+    (
+        qvt_out,
+        key_out,
+        proj_out,
+        up_out,
+        down_out,
+        recon_out,
+        bias_out,
+        refine_qvt_out,
+        refine_key_out,
+        refine_proj_out,
+        refine_bias_out,
+        features_out,
+        labels_out,
+    ) = outs
+    arrivals = [
+        pltpu.make_async_copy(source, target, semaphores.at[i])
+        for i, (source, target) in enumerate(
+            zip(
+                (*sources, features_ref, labels_ref), (*held, features_out, labels_out)
+            )
+        )
+    ]
+    for arrival in arrivals:
+        arrival.start()
+    for arrival in arrivals[:9]:
+        arrival.wait()
+    (
+        qkv_ref,
+        proj_ref,
+        up_ref,
+        down_ref,
+        swin_bias_ref,
+        recon_ref,
+        refine_qkv_ref,
+        refine_proj_ref,
+        refine_bias_ref,
+    ) = held
+    channels, blocks, hidden = up_ref.shape
     width = channels // heads
     lanes = key_out.shape[1]
     head_rows = heads * HEAD_ROWS
-    mark_rows = head_rows + 16
     taps, out, _ = recon_ref.shape
     refine_heads = refine_bias_ref.shape[0]
     refine_width = out // refine_heads
     refine_rows = refine_heads * HEAD_ROWS
     mark = channels % LANES
-    pad = one_hot(iota((lanes, channels), 0) == iota((lanes, channels), 1))
-
+    both = blocks * channels
+    qkv, proj, up, down = (
+        ref[...].reshape(both, ref.shape[2]) for ref in (qkv_ref, proj_ref, up_ref, down_ref)
+    )
+
+    def block_source(index, i):
+        return jnp.where(index < channels, index * blocks + i, -1)
+
+    moved = exact(pick_rows(query_value_source(heads, width, channels), 3 * channels), qkv, NT)
+    keys = exact(
+        qkv, pick_columns(head_source(iota((1, lanes), 1), heads, width, channels), 3 * channels)
+    )
+    turned = exact(pick_rows(iota((down_out.shape[1], 1), 0), hidden), down, NT)
+    pad = pick_rows(iota((lanes, 1), 0), channels)
+    kernel = exact(pad, recon_ref[...].reshape(taps * out, channels), NT)
     for i in range(blocks):
         tables_ref[i * heads : (i + 1) * heads] = swin_bias_ref[:, i]
-    rows, moved = [], []
-    kernel = recon_ref[...].reshape(taps * out, channels)
+    rows = []
     for v in range(VAR_DEV):
         code = lax.axis_index("var") * VAR_DEV + v
         turn, flip_rows, flip_cols = code // 4 == 1, code // 2 % 2 == 1, code % 2 == 1
         rows.append(bias_rows(tables_ref[: blocks * heads], turn, flip_rows, flip_cols))
-        shape = (3 * lanes, 1)
-        row = iota(shape, 0)
-        row_step = row // lanes - 1
-        lane = row % lanes
+    never = lax.axis_index("var") < 0
+    refine_table = bias_rows(refine_bias_ref[...], never, never, never)
+    weight = refine_qkv_ref[...]
+    source = query_value_source(refine_heads, refine_width, out)
+    refine_moved = exact(pick_rows(source, 3 * out), weight, NT)
+    source = head_source(iota((1, LANES), 1), refine_heads, refine_width, out)
+    refine_keys = exact(weight, pick_columns(source, 3 * out))
+    refine_proj = []
+    for h in range(refine_heads):
+        row = iota((LANES, 1), 0)
+        source = jnp.where(row < refine_width, row + h * refine_width, -1)
+        refine_proj.append(exact(pick_rows(source, out), refine_proj_ref[...]))
+
+    row = iota((2 * LANES, 1), 0)
+    head, unit = row % LANES // HEAD_ROWS * 2 + row // LANES, row % HEAD_ROWS
+    proj_source = jnp.where((head < heads) & (unit < width), head * width + unit, channels)
+    for i in range(blocks):
+        for ref in (proj_out, up_out):
+            ref[i] = jnp.zeros(ref.shape[1:], BF16)
+        proj_out[i, :, :channels] = exact(pick_rows(block_source(proj_source, i), both), proj)
+        up_out[i, :, :hidden] = exact(pick_rows(block_source(iota((lanes, 1), 0), i), both), up)
+    for v in range(VAR_DEV):
+        code = lax.axis_index("var") * VAR_DEV + v
+        turn, flip_rows, flip_cols = code // 4 == 1, code // 2 % 2 == 1, code % 2 == 1
+        lane = iota((1, 3 * lanes), 1)
+        row_step = lane // lanes - 1
+        lane = lane % lanes
         col_step = jnp.where(lane >= LANES, 1, jnp.where(lane >= out, 0, -1))
         channel = jnp.where(lane >= LANES, lane - LANES, jnp.where(lane >= out, lane - out, lane))
         row_step = jnp.where(flip_rows, -row_step, row_step)
@@ -180,60 +250,28 @@
         source = source + jnp.where(turn, sub_col, sub_row) * SCALE
         source = tap * out + source + jnp.where(turn, sub_row, sub_col)
         source = jnp.where(channel < out, source, -1)
-        moved.append(exact(one_hot(iota((3 * lanes, taps * out), 1) == source), kernel))
-    never = lax.axis_index("var") < 0
-    refine_table = bias_rows(refine_bias_ref[...], never, never, never)
-    keys = [
-        exact(qkv_ref[i], head_matrix(lanes, 3 * channels, heads, width, channels), NT)
-        for i in range(blocks)
-    ]
-    weight = refine_qkv_ref[...]
-    refine_queries = exact(
-        head_matrix(refine_rows + 16, 3 * out, refine_heads, refine_width), weight, NT
-    )
-    refine_values = exact(
-        head_matrix(refine_rows, 3 * out, refine_heads, refine_width, 2 * out), weight, NT
-    )
-    refine_keys = exact(head_matrix(LANES, 3 * out, refine_heads, refine_width, out), weight, NT)
-    refine_proj = []
-    for h in range(refine_heads):
-        shape = (LANES, out)
-        row = iota(shape, 0)
-        pick = one_hot((row < refine_width) & (iota(shape, 1) == row + h * refine_width))
-        refine_proj.append(exact(pick, refine_proj_ref[...]))
-
-    queries = head_matrix(mark_rows, 3 * channels, heads, width)
-    values = head_matrix(head_rows, 3 * channels, heads, width, 2 * channels)
-    query_add = query_labels(mark_rows, lanes, head_rows, channels).astype(BF16)
-    key_add = key_labels(lanes, lanes, channels, head_rows)
-    shape = (2 * LANES, channels)
-    row = iota(shape, 0)
-    head, unit = row % LANES // HEAD_ROWS * 2 + row // LANES, row % HEAD_ROWS
-    proj_rows = one_hot((head < heads) & (unit < width) & (iota(shape, 1) == head * width + unit))
-    shape = (down_out.shape[1], hidden)
-    down_rows = one_hot(iota(shape, 0) == iota(shape, 1))
+        recon_out[v] = exact(kernel, pick_columns(source, taps * out))
+
+    row = iota((2 * head_rows + 16, 1), 0)
+    scale = jnp.where(row < head_rows, width**-0.5 * LOG2E, 1.0)
+    query_add = query_value_marks(heads, width, lanes, channels)
+    key_add = key_marks(lanes, lanes, channels, head_rows)
     for i in range(blocks):
-        for ref in (qvt_out, proj_out, up_out, down_out):
-            ref[i] = jnp.zeros(ref.shape[1:], BF16)
-        qvt_out[i, :mark_rows] = query_add
-        qvt_out[i, :mark_rows, :channels] = exact(queries, qkv_ref[i], NT)
-        qvt_out[i, mark_rows:, :channels] = exact(values, qkv_ref[i], NT)
-        proj_out[i, :, :channels] = exact(proj_rows, proj_ref[i])
-        up_out[i, :, :hidden] = exact(pad, up_ref[i])
-        down_out[i, :, :channels] = exact(down_rows, down_ref[i], NT)
-
-    for i in range(blocks):
-        key_out[i] = (dot(pad, keys[i]) + key_add).astype(BF16)
-    for v in range(VAR_DEV):
-        recon_out[v] = exact(pad, moved[v], NT)
-    out_pad = one_hot(iota((LANES, out), 0) == iota((LANES, out), 1))
-    refine_qvt_out[: refine_rows + 16] = (
-        dot(refine_queries, out_pad, NT)
-        + query_labels(refine_rows + 16, LANES, refine_rows, mark)
+        columns = pick_columns(block_source(iota((1, lanes), 1), i), both)
+        qvt_out[i] = (dot(moved, columns) * scale + query_add).astype(BF16)
+        down_out[i] = (dot(turned, columns) * 0.5).astype(BF16)
+        key_out[i] = (
+            dot(pick_rows(block_source(iota((lanes, 1), 0), i), both), keys) + key_add
+        ).astype(BF16)
+    row = iota((2 * refine_rows + 16, 1), 0)
+    scale = jnp.where(row < refine_rows, refine_width**-0.5 * LOG2E, 1.0)
+    out_pad = pick_rows(iota((LANES, 1), 0), out)
+    refine_qvt_out[...] = (
+        dot(refine_moved, out_pad, NT) * scale
+        + query_value_marks(refine_heads, refine_width, LANES, mark)
     ).astype(BF16)
-    refine_qvt_out[refine_rows + 16 :] = exact(refine_values, out_pad, NT)
     refine_key_out[...] = (
-        dot(out_pad, refine_keys, NT) + key_labels(LANES, LANES, mark, refine_rows)
+        dot(out_pad, refine_keys) + key_marks(LANES, LANES, mark, refine_rows)
     ).astype(BF16)
     for h in range(refine_heads):
         square = dot(refine_proj[h], out_pad, NT)
@@ -251,23 +289,31 @@
         refine_bias_out[key_row * WIN : (key_row + 1) * WIN] = value
 
     bias_grid(refine_table, rows_ref, store_refine)
-
-
-def gelu(x):
+    for arrival in arrivals[9:]:
+        arrival.wait()
+
+
+def twice_gelu(x):
     x = x.astype(BF16)
     square = jnp.minimum(x * x, BF16(REACH))
     first, second, third = (BF16(factor) for factor in ERF_TANH)
     series = (square * third + second) * square + first
-    half = BF16(0.5) * x
-    return half + half * jnp.tanh(x * series)
-
-
-def normalize(x, channels):
-    inside = iota((1, x.shape[1]), 1) < channels
-    mean = jnp.sum(jnp.where(inside, x, 0.0), axis=1, keepdims=True) * (1.0 / channels)
-    centred = jnp.where(inside, x - mean, 0.0)
-    spread = jnp.sum(centred * centred, axis=1, keepdims=True) * (1.0 / channels)
-    return jnp.where(inside, centred * lax.rsqrt(spread + EPSILON), x).astype(BF16)
+    return x + x * jnp.tanh(x * series)
+
+
+def normalize(x, channels, keep_marks):
+    tiles = [x[:, i : i + LANES] for i in range(0, x.shape[1], LANES)]
+    inside = iota((1, LANES), 1) < channels - (len(tiles) - 1) * LANES
+    mean = jnp.sum(sum(tiles[1:], tiles[0]), axis=1, keepdims=True) * (1.0 / channels)
+    centred = [tile - mean for tile in tiles]
+    centred[-1] = jnp.where(inside, centred[-1], 0.0)
+    squares = [tile * tile for tile in centred]
+    spread = jnp.sum(sum(squares[1:], squares[0]), axis=1, keepdims=True) * (1.0 / channels)
+    scale = lax.rsqrt(spread + EPSILON)
+    result = [tile * scale for tile in centred]
+    if keep_marks:
+        result[-1] = jnp.where(inside, result[-1], tiles[-1])
+    return jnp.concatenate(result, axis=1).astype(BF16)
 
 
 def split_queries(queries, heads):
@@ -294,14 +340,11 @@
     return results
 
 
-def heads_of(n, scale, heads, width, w_qvt, w_key):
+def heads_of(n, heads, w_qvt, w_key):
     mark_rows = heads * HEAD_ROWS + 16
     both = dot(w_qvt, n, NT)
-    row = iota((mark_rows, 1), 0)
-    queries = both[:mark_rows] * jnp.where(row < heads * HEAD_ROWS, scale, 1.0)
-    values = both[mark_rows:]
-    row = iota((heads * HEAD_ROWS, 1), 0) % HEAD_ROWS
-    values = jnp.where(row == width, 1.0, values).astype(BF16)
+    queries = both[:mark_rows]
+    values = both[mark_rows:].astype(BF16)
     keys = dot(n, w_key).astype(BF16)
     scores = []
     for place in range(n.shape[0] // LANES):
@@ -338,9 +381,8 @@
 
 def swin_block(x, pairs, heads, channels, bias, w_qvt, w_key, w_proj, w_up, w_down):
     width = channels // heads
-    n = normalize(x, channels)
-    scale = width**-0.5 * LOG2E
-    scores, values = heads_of(n, scale, heads, width, w_qvt[...], w_key[...])
+    n = normalize(x, channels, True)
+    scores, values = heads_of(n, heads, w_qvt[...], w_key[...])
     pad = jnp.zeros((LANES - heads // 2 * HEAD_ROWS, 2 * LANES), F32)
     weights = [
         (soft(scores[2 * place] + bias(a)), soft(scores[2 * place + 1] + bias(b)))
@@ -361,7 +403,7 @@
     if places != list(range(x.shape[0] // LANES)):
         x = jnp.concatenate([x[place * LANES : (place + 1) * LANES] for place in places], axis=0)
     h = (x + dot(outputs, w_proj[...])).astype(BF16).astype(F32)
-    hidden = gelu(dot(normalize(h, channels), w_up[...]))
+    hidden = twice_gelu(dot(normalize(h, channels, False), w_up[...]))
     y = h + dot(hidden, w_down[...])
     return [y[i * LANES : (i + 1) * LANES] for i in range(len(pairs))]
 
@@ -389,23 +431,18 @@
     for k, strip in enumerate(strips):
         rows = x_ref[strip * WIN : (strip + 1) * WIN].astype(F32)
         held[k * part : (k + 1) * part, :channels] = windows_of(rows)
-    token = iota((tokens, rows_total), 0)
-    strip = token // part + strips[0]
-    if ends:
-        strip = jnp.where(token < part, strips[0], strips[1])
-    at_row = strip * WIN + token % CELLS // WIN == iota((tokens, rows_total), 1)
-    by_row = dot(one_hot(at_row), labels_ref[...].astype(F32).astype(BF16), NT)
-    token = iota((tokens, breadth), 0)
-    at_col = token % part // CELLS * WIN + token % WIN == iota((tokens, breadth), 1)
-    label = dot(jnp.where(at_col, by_row, 0.0).astype(BF16), jnp.ones((breadth, LANES), BF16))
-    lane = iota((tokens, LANES), 1) - channels % LANES
-    marks = jnp.where(
-        (label == (lane + 1).astype(F32)) & (lane < CLASSES)
-        | (lane >= CLASSES) & (lane < MARKS),
-        1.0,
-        0.0,
+    labels = labels_ref[...].astype(F32).astype(BF16)
+    row_gap = iota((CELLS, rows_total), 1) - iota((CELLS, rows_total), 0) // WIN
+    col_gap = iota((CELLS, breadth), 1) - iota((CELLS, breadth), 0) % WIN
+    by_row = [dot(one_hot(row_gap == strip * WIN), labels, NT) for strip in strips]
+    cells = [jnp.where(col_gap == w * WIN, rows, 0.0) for rows in by_row for w in range(count)]
+    label = dot(
+        jnp.concatenate(cells, axis=0).astype(BF16), jnp.ones((breadth, LANES), BF16)
     )
-    tail = jnp.where(lane < 0, held[:, lanes - LANES :], marks)
+    lane = iota((1, LANES), 1) - channels % LANES
+    wanted = jnp.where((lane >= 0) & (lane < CLASSES), lane + 1, -1).astype(F32)
+    fixed = jnp.where(lane == CLASSES, 1.0, jnp.where(lane == CLASSES + 1, CONSTANT, 0.0))
+    tail = jnp.where(lane < 0, held[:, lanes - LANES :], jnp.where(label == wanted, 1.0, fixed))
     x = jnp.concatenate([held[:, : lanes - LANES], tail], axis=1)
     places = tokens // LANES
     pairs = [(place, v, v) for v in range(VAR_DEV) for place in range(places)]
@@ -521,7 +558,7 @@
     always = iota((1, lanes), 1) == channels + CLASSES + 1
 
     def marked(refs, axis, after, place):
-        return jnp.where(always, 1.0, received(refs, axis, after, place))
+        return jnp.where(always, CONSTANT, received(refs, axis, after, place))
 
     for v in range(VAR_DEV):
         for end in range(2):
@@ -649,9 +686,7 @@
     lane = iota((1, LANES), 1)
     is_mark = (lane >= first_mark) & (lane < first_mark + MARKS)
     n = jnp.where(is_mark, marks, tall.T).astype(BF16)
-    scores, values = heads_of(
-        n, width**-0.5 * LOG2E, heads, width, w_qvt[...], w_key[...]
-    )
+    scores, values = heads_of(n, heads, w_qvt[...], w_key[...])
     probabilities = [soft(s + bias_ref[...]) for s in scores]
     lane = iota((channels, LANES), 1)
     branches = []
@@ -740,10 +775,12 @@
     lanes = round_up(channels + MARKS, LANES)
     hidden = round_up(up_weight.shape[-1], LANES)
     operands = (
-        qkv_weight,
-        proj_weight,
-        up_weight,
-        jnp.swapaxes(down_weight, 1, 2),
+        features,
+        labels.T,
+        jnp.swapaxes(qkv_weight, 0, 1),
+        jnp.swapaxes(proj_weight, 0, 1),
+        jnp.swapaxes(up_weight, 0, 1),
+        down_weight.transpose(2, 0, 1),
         jnp.swapaxes(swin_bias, 0, 1),
         jnp.swapaxes(recon_weight, 1, 2),
         refine_qkv,
@@ -763,22 +800,27 @@
         ((LANES, LANES), BF16),
         ((refine_heads * out_channels, LANES), BF16),
         ((CELLS, refine_heads * CELLS), F32),
+        (features.shape, BF16),
+        (operands[1].shape, jnp.int32),
     ]
     shapes = [jax.ShapeDtypeStruct(*s) for s in shapes]
     prepared = pl.pallas_call(
         functools.partial(prepare_kernel, heads),
         grid=(1,),
-        in_specs=[whole(a) for a in operands],
+        in_specs=[pl.BlockSpec(memory_space=pltpu.HBM)] * len(operands),
         out_specs=[whole(s) for s in shapes],
         out_shape=shapes,
         scratch_shapes=[
+            *[pltpu.VMEM(a.shape, a.dtype) for a in operands[2:]],
             pltpu.VMEM((heads, WIN, LANES), F32),
             pltpu.VMEM((round_up(2 * heads, 8), swin_bias.shape[2]), F32),
+            pltpu.SemaphoreType.DMA((len(operands),)),
         ],
-        compiler_params=params(10),
+        compiler_params=params(12),
         name="prepare",
-    )(*operands)
-    *swin, recon, bias, refine_qvt, refine_key, refine_projt, refine_grid = prepared
+    )(*[pltpu.with_memory_space_constraint(a, pltpu.HBM) for a in operands])
+    *swin, recon, bias, refine_qvt, refine_key, refine_projt, refine_grid = prepared[:-2]
+    features, labels_across = prepared[-2:]
 
     def block_specs(i):
         arrays = (bias, *swin)
@@ -795,7 +837,6 @@
     arrays, specs = block_specs(0)
     strips = height // WIN
     tokens = WIN * breadth
-    labels_across = labels.T
 
     pair_axis = lax.axis_size("ty") == 2
 

time: 50.7 us -> 48.5 us (0.957)
  local copies, waits for them, and re-layouts: 3.21 us -> 0 us
  Pallas kernels: 31.4 us -> 32.6 us
    unnamed x20 -> x0, local copies, waits for them, and re-layouts: 3.21 us -> none
    pallas_call x1, Pallas kernels: 2.84 us -> 4.68 us  [local(): pl.pallas_call(functools.partial(prepare_kernel, heads), grid=(1,), in_sp...]
where the time goes in v5:
time: 48.5 us; the launch traced here: 48.3 us
  Pallas kernels  32.6 us (67%)
  starting transfers between devices  10.1 us (21%)
  waiting for transfers between devices  4.71 us (10%)
  other arithmetic  0.82 us (2%)
    pallas_call x1, Pallas kernels, local(): pl.pallas_call(functools.partial(outer_kernel, heads, channels, group, le...  10.8 us
    pallas_call x2, Pallas kernels, block_one(): pl.pallas_call(functools.partial(first_kernel, heads, channels, places),...  8.86 us
    pallas_call x1, Pallas kernels, local(): pl.pallas_call(functools.partial(inner_kernel, heads, channels, group), g...  6.49 us
    ppermute x3, starting transfers between devices, swap_pairs(): return lax.ppermute(strip, axis, pairs + [(j, i) for i, j in pairs])  6.04 us
    ppermute x3, waiting for transfers between devices, whole_swap(): return lax.ppermute(a, 'var', [(i, i ^ bit) for i in range(count)])  4.7 us
    pallas_call x1, Pallas kernels, local(): pl.pallas_call(functools.partial(prepare_kernel, heads), grid=(1,), in_sp...  4.68 us
    ppermute x3, starting transfers between devices, whole_swap(): return lax.ppermute(a, 'var', [(i, i ^ bit) for i in range(count)])  4.11 us
    pallas_call x1, Pallas kernels, local(): pl.pallas_call(functools.partial(refine_kernel, refine_heads, channels %...  1.71 us
  transfers between devices with their start and end apart: 6, of which 3 were waited for; matrix products, arithmetic and copies ran while one was open for 0% of the time, Pallas kernels for 26%

profile of v5, /device:TPU:9, one launch (start us, length us, event | category | flops | bytes accessed | tf_op | source)
XLA Modules:
  0.0 48.3 jit_solution(5450574647114252373)
XLA Ops:
  0.0 4.7 %prepare.1 = (bf16[2,400,256]{2,1,0:T(8,128)(2,1)S(1)}, bf16[2,256,256]{2,1,0:T(8,128)(2,1)S(1)}, bf16[2,256,256]{2,1,0:T(8,128)(2,1)S(1)}, bf16[2,256,384]{2,1,...) custom-call(bf16[64,32,180]{2,1,0:T(8,128)(2,1)} %features_ref.1, ...), custom_call_target="tpu_custom_call" | custom-call | tf_op jit(solution)/shard_map/prepare/pallas_call | solution.py:807
  4.7 2.8 %block_one_ends.1 = (bf16[2,16,32,256]{3,2,1,0:T(8,128)(2,1)S(1)}, bf16[2,64,256]{2,1,0:T(8,128)(2,1)S(1)}, bf16[2,64,256]{2,1,0:T(8,128)(2,1)S(1)}, bf16[2,4,32,256]{3,2,1,0:T(8,128)(2,1)S(1)}) custom-call(bf16[64,32,180]{2,1,0:T(8,128)(2,1)S(1)} %get-tuple-element.31.x_ref, s32[32,64]{1,0:T(8,128)S(1)} %get-tuple-element.32.labels_ref, ...), custom_call_target="tpu_custom_call" | custom-call | flops 6400000000 | bytes 3200000 | tf_op jit(solution)/shard_map/block_one_ends/pallas_call | solution.py:853
  7.5 1.3 %collective-permute-start = (bf16[2,4,32,256]{3,2,1,0:T(8,128)(2,1)S(1)}, bf16[2,4,32,256]{3,2,1,0:T(8,128)(2,1)S(1)}, u32[]{:S(2)}, u32[]{:S(2)}) collective-permute-start(bf16[2,4,32,256]{3,2,1,0:T(8,128)(2,1)S(1)} %get-tuple-element.41), channel_id=1, source_target_pairs={{0,4},{4,0},{1,5},{5,1},{2,6},{6,2},{3,7},{7,3},{8,12},{12,8},{9,1... | collective-permute-start | bytes 393224 | tf_op jit(solution)/shard_map/ppermute | solution.py:740
  8.8 6.0 %block_one_middle.1 = (bf16[2,48,32,256]{3,2,1,0:T(8,128)(2,1)S(1)}, bf16[2,192,256]{2,1,0:T(8,128)(2,1)S(1)}, bf16[2,192,256]{2,1,0:T(8,128)(2,1)S(1)}) custom-call(bf16[64,32,180]{2,1,0:T(8,128)(2,1)S(1)} %get-tuple-element.31.x_ref, s32[32,64]{1,0:T(8,128)S(1)} %get-tuple-element.32.labels_ref, f32[2,2,64,384]{3,2,1,0:T(8,128)S(1)} %get-tuple-element.33.bias_ref.refs_4_, ...), custom_call_target="tpu_custom_call" | custom-call | flops 19200000000 | bytes 9600000 | tf_op jit(solution)/shard_map/block_one_middle/pallas_call | solution.py:853
  14.9 0.0 collective-permute-done.refs_0_
  14.9 0.1 edges.1
  15.0 0.2 collective-permute-start.1
  15.2 4.5 %collective-permute-start.2 = (bf16[2,288,256]{2,1,0:T(8,128)(2,1)S(1)}, bf16[2,288,256]{2,1,0:T(8,128)(2,1)S(1)}, u32[]{:S(2)}, u32[]{:S(2)}) collective-permute-start(bf16[2,288,256]{2,1,0:T(8,128)(2,1)S(1)} %get-tuple-element.47), channel_id=1, source_target_pairs={{1,2},{2,1},{5,6},{6,5},{9,10},{10,9},{13,14},{14,13},{17,18},{18,... | collective-permute-start | bytes 884744 | tf_op jit(solution)/shard_map/ppermute | solution.py:740
  19.7 6.5 %block_two_inner.1 = (bf16[21,2,64,256]{3,2,1,0:T(8,128)(2,1)S(1)}, bf16[8,256,128]{2,1,0:T(8,128)(2,1)S(1)}) custom-call(bf16[2,16,32,256]{3,2,1,0:T(8,128)(2,1)S(1)} %get-tuple-element.39.ends_ref, bf16[2,48,32,256]{3,2,1,0:T(8,128)(2,1)S(1)} %get-tuple-element.40.middle_ref, f32[2,2,64,384]{3,2,1,0:T(8,128)S(1)} %get-tuple-element.33.bias_ref.refs_4_, ...), custom_call_target="tpu_custom_call" | custom-call | flops 16800000000 | bytes 8400000 | tf_op jit(solution)/shard_map/block_two_inner/pallas_call | solution.py:887
  26.2 0.0 collective-permute-done.1.refs_1_
  26.2 0.0 collective-permute-done.2.refs_2_
  26.2 10.8 %block_two_border.1 = (bf16[4,48,256]{2,1,0:T(8,128)(2,1)S(1)}, bf16[4,48,256]{2,1,0:T(8,128)(2,1)S(1)}) custom-call(bf16[2,16,32,256]{3,2,1,0:T(8,128)(2,1)S(1)} %get-tuple-element.39.ends_ref, bf16[2,48,32,256]{3,2,1,0:T(8,128)(2,1)S(1)} %get-tuple-element.40.middle_ref, bf16[2,4,32,256]{3,2,1,0:T(8,128)(2,1)S(1)} %collective-permute-done.refs_0_, ...), custom_call_target="tpu_custom_call" | custom-call | tf_op jit(solution)/shard_map/block_two_border/pallas_call | solution.py:913
  37.0 1.6 %collective-permute-start.3 = (bf16[4,48,256]{2,1,0:T(8,128)(2,1)S(1)}, bf16[4,48,256]{2,1,0:T(8,128)(2,1)S(1)}, u32[]{:S(2)}, u32[]{:S(2)}) collective-permute-start(bf16[4,48,256]{2,1,0:T(8,128)(2,1)S(1)} %get-tuple-element.51), channel_id=1, source_target_pairs={{0,8},{8,0},{16,24},{24,16},{1,9},{9,1},{17,25},{25,17},{2,10},{10... | collective-permute-start | bytes 294920 | tf_op jit(solution)/shard_map/ppermute | solution.py:745
  38.6 0.9 %collective-permute-done.3 = bf16[4,48,256]{2,1,0:T(8,128)(2,1)S(1)} collective-permute-done((bf16[4,48,256]{2,1,0:T(8,128)(2,1)S(1)}, bf16[4,48,256]{2,1,0:T(8,128)(2,1)S(1)}, u32[]{:S(2)}, u32[]{:S(2)}) %collective-permute-start.3) | collective-permute-done | bytes 98336 | tf_op jit(solution)/shard_map/ppermute | solution.py:745
  39.5 1.3 %collective-permute-start.4 = (bf16[4,48,256]{2,1,0:T(8,128)(2,1)S(1)}, bf16[4,48,256]{2,1,0:T(8,128)(2,1)S(1)}, u32[]{:S(2)}, u32[]{:S(2)}) collective-permute-start(bf16[4,48,256]{2,1,0:T(8,128)(2,1)S(1)} %add_convert_fusion.mine_ref), channel_id=1, source_target_pairs={{0,16},{8,24},{16,0},{24,8},{1,17},{9,25},{17,1},{25,9},{2,18},{10... | collective-permute-start | bytes 294920 | tf_op jit(solution)/shard_map/ppermute | solution.py:745
  40.8 2.8 %collective-permute-done.4.other_ref = bf16[4,48,256]{2,1,0:T(8,128)(2,1)S(1)} collective-permute-done((bf16[4,48,256]{2,1,0:T(8,128)(2,1)S(1)}, bf16[4,48,256]{2,1,0:T(8,128)(2,1)S(1)}, u32[]{:S(2)}, u32[]{:S(2)}) %collective-permute-start.4) | collective-permute-done | bytes 98336 | tf_op jit(solution)/shard_map/ppermute | solution.py:745
  43.6 1.7 %refinement.1 = bf16[3,128,128]{2,1,0:T(8,128)(2,1)S(1)} custom-call(bf16[4,48,256]{2,1,0:T(8,128)(2,1)S(1)} %add_convert_fusion.mine_ref, bf16[4,48,256]{2,1,0:T(8,128)(2,1)S(1)} %collective-permute-done.4.other_ref, bf16[8,256,128]{2,1,0:T(8,128)(2,1)S(1)} %get-tuple-element.52.marks_ref, f32[64,128]{1,0:T(8,128)S(1)} %get-tuple-element.53.bias_ref, ...), custom_call_target="tpu_custom_call" | custom-call | tf_op jit(solution)/shard_map/refinement/pallas_call | solution.py:935
  45.3 1.3 %collective-permute-start.5 = (bf16[3,128,128]{2,1,0:T(8,128)(2,1)S(1)}, bf16[3,128,128]{2,1,0:T(8,128)(2,1)S(1)}, u32[]{:S(2)}, u32[]{:S(2)}) collective-permute-start(bf16[3,128,128]{2,1,0:T(8,128)(2,1)S(1)} %refinement.1), channel_id=1, source_target_pairs={{0,8},{8,0},{16,24},{24,16},{1,9},{9,1},{17,25},{25,17},{2,10},{10... | collective-permute-start | bytes 294920 | tf_op jit(solution)/shard_map/ppermute | solution.py:745
  46.6 0.9 %collective-permute-done.5 = bf16[3,128,128]{2,1,0:T(8,128)(2,1)S(1)} collective-permute-done((bf16[3,128,128]{2,1,0:T(8,128)(2,1)S(1)}, bf16[3,128,128]{2,1,0:T(8,128)(2,1)S(1)}, u32[]{:S(2)}, u32[]{:S(2)}) %collective-permute-start.5) | collective-permute-done | bytes 98336 | tf_op jit(solution)/shard_map/ppermute | solution.py:745
  47.6 0.8 %maximum_convert_fusion = f32[3,256,128]{2,1,0:T(8,128)} fusion(bf16[3,128,128]{2,1,0:T(8,128)(2,1)S(1)} %get-tuple-element.58, bf16[3,128,128]{2,1,0:T(8,128)(2,1)S(1)} %get-tuple-element.57), kind=kLoop, calls=%fused_computation | loop fusion | flops 393216 | bytes 589824 | tf_op jit(solution)/shard_map/convert_element_type | solution.py:948
  (2 shorter events, 0.0 us)
Async XLA Ops:
  7.5 7.4 %collective-permute-start = (bf16[2,4,32,256]{3,2,1,0:T(8,128)(2,1)S(1)}, bf16[2,4,32,256]{3,2,1,0:T(8,128)(2,1)S(1)}, u32[]{:S(2)}, u32[]{:S(2)}) collective-permute-start(bf16[2,4,32,256]{3,2,1,0:T(8,128)(2,1)S(1)} %get-tuple-element.41), channel_id=1, source_target_pairs={{0,4},{4,0},{1,5},{5,1},{2,6},{6,2},{3,7},{7,3},{8,12},{12,8},{9,1... | collective-permute-start | bytes 393224 | tf_op jit(solution)/shard_map/ppermute | solution.py:740
  15.0 11.2 %collective-permute-start.1 = (bf16[2,288,256]{2,1,0:T(8,128)(2,1)S(1)}, bf16[2,288,256]{2,1,0:T(8,128)(2,1)S(1)}, u32[]{:S(2)}, u32[]{:S(2)}) collective-permute-start(bf16[2,288,256]{2,1,0:T(8,128)(2,1)S(1)} %get-tuple-element.46), channel_id=1, source_target_pairs={{0,1},{2,3},{1,0},{3,2},{4,5},{6,7},{5,4},{7,6},{8,9},{10,11},{9,8... | collective-permute-start | bytes 884744 | tf_op jit(solution)/shard_map/ppermute | solution.py:740
  15.2 11.0 %collective-permute-start.2 = (bf16[2,288,256]{2,1,0:T(8,128)(2,1)S(1)}, bf16[2,288,256]{2,1,0:T(8,128)(2,1)S(1)}, u32[]{:S(2)}, u32[]{:S(2)}) collective-permute-start(bf16[2,288,256]{2,1,0:T(8,128)(2,1)S(1)} %get-tuple-element.47), channel_id=1, source_target_pairs={{1,2},{2,1},{5,6},{6,5},{9,10},{10,9},{13,14},{14,13},{17,18},{18,... | collective-permute-start | bytes 884744 | tf_op jit(solution)/shard_map/ppermute | solution.py:740
  37.0 2.5 %collective-permute-start.3 = (bf16[4,48,256]{2,1,0:T(8,128)(2,1)S(1)}, bf16[4,48,256]{2,1,0:T(8,128)(2,1)S(1)}, u32[]{:S(2)}, u32[]{:S(2)}) collective-permute-start(bf16[4,48,256]{2,1,0:T(8,128)(2,1)S(1)} %get-tuple-element.51), channel_id=1, source_target_pairs={{0,8},{8,0},{16,24},{24,16},{1,9},{9,1},{17,25},{25,17},{2,10},{10... | collective-permute-start | bytes 294920 | tf_op jit(solution)/shard_map/ppermute | solution.py:745
  39.5 4.1 %collective-permute-start.4 = (bf16[4,48,256]{2,1,0:T(8,128)(2,1)S(1)}, bf16[4,48,256]{2,1,0:T(8,128)(2,1)S(1)}, u32[]{:S(2)}, u32[]{:S(2)}) collective-permute-start(bf16[4,48,256]{2,1,0:T(8,128)(2,1)S(1)} %add_convert_fusion.mine_ref), channel_id=1, source_target_pairs={{0,16},{8,24},{16,0},{24,8},{1,17},{9,25},{17,1},{25,9},{2,18},{10... | collective-permute-start | bytes 294920 | tf_op jit(solution)/shard_map/ppermute | solution.py:745
  45.3 2.2 %collective-permute-start.5 = (bf16[3,128,128]{2,1,0:T(8,128)(2,1)S(1)}, bf16[3,128,128]{2,1,0:T(8,128)(2,1)S(1)}, u32[]{:S(2)}, u32[]{:S(2)}) collective-permute-start(bf16[3,128,128]{2,1,0:T(8,128)(2,1)S(1)} %refinement.1), channel_id=1, source_target_pairs={{0,8},{8,0},{16,24},{24,16},{1,9},{9,1},{17,25},{25,17},{2,10},{10... | collective-permute-start | bytes 294920 | tf_op jit(solution)/shard_map/ppermute | solution.py:745

commit v6 on v5

--- a/solution.py
+++ b/solution.py
@@ -165,8 +165,6 @@
     ]
     for arrival in arrivals:
         arrival.start()
-    for arrival in arrivals[:9]:
-        arrival.wait()
     (
         qkv_ref,
         proj_ref,
@@ -188,20 +186,9 @@
     refine_rows = refine_heads * HEAD_ROWS
     mark = channels % LANES
     both = blocks * channels
-    qkv, proj, up, down = (
-        ref[...].reshape(both, ref.shape[2]) for ref in (qkv_ref, proj_ref, up_ref, down_ref)
-    )
-
-    def block_source(index, i):
-        return jnp.where(index < channels, index * blocks + i, -1)
-
-    moved = exact(pick_rows(query_value_source(heads, width, channels), 3 * channels), qkv, NT)
-    keys = exact(
-        qkv, pick_columns(head_source(iota((1, lanes), 1), heads, width, channels), 3 * channels)
-    )
-    turned = exact(pick_rows(iota((down_out.shape[1], 1), 0), hidden), down, NT)
-    pad = pick_rows(iota((lanes, 1), 0), channels)
-    kernel = exact(pad, recon_ref[...].reshape(taps * out, channels), NT)
+
+    for arrival in (arrivals[4], arrivals[8]):
+        arrival.wait()
     for i in range(blocks):
         tables_ref[i * heads : (i + 1) * heads] = swin_bias_ref[:, i]
     rows = []
@@ -211,6 +198,22 @@
         rows.append(bias_rows(tables_ref[: blocks * heads], turn, flip_rows, flip_cols))
     never = lax.axis_index("var") < 0
     refine_table = bias_rows(refine_bias_ref[...], never, never, never)
+    for arrival in (*arrivals[:4], *arrivals[5:8]):
+        arrival.wait()
+    qkv, proj, up, down = (
+        ref[...].reshape(both, ref.shape[2]) for ref in (qkv_ref, proj_ref, up_ref, down_ref)
+    )
+
+    def block_source(index, i):
+        return jnp.where(index < channels, index * blocks + i, -1)
+
+    moved = exact(pick_rows(query_value_source(heads, width, channels), 3 * channels), qkv, NT)
+    keys = exact(
+        qkv, pick_columns(head_source(iota((1, lanes), 1), heads, width, channels), 3 * channels)
+    )
+    turned = exact(pick_rows(iota((down_out.shape[1], 1), 0), hidden), down, NT)
+    pad = pick_rows(iota((lanes, 1), 0), channels)
+    kernel = exact(pad, recon_ref[...].reshape(taps * out, channels), NT)
     weight = refine_qkv_ref[...]
     source = query_value_source(refine_heads, refine_width, out)
     refine_moved = exact(pick_rows(source, 3 * out), weight, NT)
@@ -379,33 +382,76 @@
     return mixed
 
 
-def swin_block(x, pairs, heads, channels, bias, w_qvt, w_key, w_proj, w_up, w_down):
+def swin_unit(x, pairs, results, heads, channels, bias, w_qvt, w_key, w_proj, w_up, w_down):
     width = channels // heads
+    mark_rows = heads * HEAD_ROWS + 16
     n = normalize(x, channels, True)
-    scores, values = heads_of(n, heads, w_qvt[...], w_key[...])
-    pad = jnp.zeros((LANES - heads // 2 * HEAD_ROWS, 2 * LANES), F32)
+    yield
+    both = dot(w_qvt[...], n, NT)
+    queries = both[:mark_rows]
+    values = both[mark_rows:].astype(BF16)
+    keys = dot(n, w_key[...]).astype(BF16)
+    yield
+    scores = []
+    for place in range(x.shape[0] // LANES):
+        cut = slice(place * LANES, (place + 1) * LANES)
+        for half, stationary in enumerate(split_queries(queries[:, cut], heads)):
+            at = place * LANES + half * CELLS
+            scores.append(dot(keys[at : at + CELLS], stationary))
+    yield
     weights = [
         (soft(scores[2 * place] + bias(a)), soft(scores[2 * place + 1] + bias(b)))
         for place, a, b in pairs
     ]
+    yield
+    pad = jnp.zeros((LANES - heads // 2 * HEAD_ROWS, 2 * LANES), F32)
     blocks = []
     for (place, _, _), (first, second) in zip(pairs, weights):
         cut = slice(place * LANES, (place + 1) * LANES)
         mixed = mix_pair(values[:, cut], first, second, heads, width)
         blocks.append(jnp.concatenate(mixed + [pad], axis=0).astype(BF16))
+    yield
     outputs = []
     for block in blocks:
         for half in range(2):
             turned = block[:, half * LANES : (half + 1) * LANES].T
             outputs.append(jnp.concatenate([turned[:CELLS], turned[CELLS:]], axis=1))
     outputs = jnp.concatenate(outputs, axis=0)
-    places = [place for place, _, _ in pairs]
-    if places != list(range(x.shape[0] // LANES)):
-        x = jnp.concatenate([x[place * LANES : (place + 1) * LANES] for place in places], axis=0)
-    h = (x + dot(outputs, w_proj[...])).astype(BF16).astype(F32)
-    hidden = twice_gelu(dot(normalize(h, channels, False), w_up[...]))
+    yield
+    x = jnp.concatenate([x[place * LANES : (place + 1) * LANES] for place, _, _ in pairs], axis=0)
+    h = x + dot(outputs, w_proj[...])
+    yield
+    n = normalize(h, channels, False)
+    yield
+    hidden = dot(n, w_up[...])
+    yield
+    hidden = twice_gelu(hidden)
+    yield
     y = h + dot(hidden, w_down[...])
-    return [y[i * LANES : (i + 1) * LANES] for i in range(len(pairs))]
+    results.extend(y[i * LANES : (i + 1) * LANES] for i in range(len(pairs)))
+
+
+def swin_block(x, pairs, unit, *args):
+    places = x.shape[0] // LANES
+    units = []
+    for low in range(0, places, unit):
+        high = min(low + unit, places)
+        picked = [i for i, pair in enumerate(pairs) if low <= pair[0] < high]
+        moved = [(pairs[i][0] - low, *pairs[i][1:]) for i in picked]
+        found = []
+        units.append((picked, found, swin_unit(x[low * LANES : high * LANES], moved, found, *args)))
+    running = dict(enumerate(units))
+    tick = 0
+    while running:
+        for number in sorted(running):
+            if tick >= number and next(running[number][2], StopIteration) is StopIteration:
+                del running[number]
+        tick += 1
+    results = [None] * len(pairs)
+    for picked, found, _ in units:
+        for i, result in zip(picked, found):
+            results[i] = result
+    return results
 
 
 def windows_of(grid):
@@ -446,7 +492,7 @@
     x = jnp.concatenate([held[:, : lanes - LANES], tail], axis=1)
     places = tokens // LANES
     pairs = [(place, v, v) for v in range(VAR_DEV) for place in range(places)]
-    results = swin_block(x, pairs, heads, channels, lambda v: bias_ref[v], *weights)
+    results = swin_block(x, pairs, x.shape[0], heads, channels, lambda v: bias_ref[v], *weights)
     for v in range(VAR_DEV):
         for k in range(len(strips)):
             windows = []
@@ -455,7 +501,7 @@
                 block = results[v * places + group // 2]
                 at = group % 2 * CELLS
                 windows.append(block[at : at + CELLS].reshape(WIN, WIN, lanes))
-            y_ref[v, k * WIN : (k + 1) * WIN] = jnp.concatenate(windows, axis=1).astype(BF16)
+            y_ref[v, k * WIN : (k + 1) * WIN] = jnp.concatenate(windows, axis=1)
             at = k * WIN * SHIFT
             for r in range(WIN):
                 rows = slice(at + r * SHIFT, at + (r + 1) * SHIFT)
@@ -466,50 +512,57 @@
         side_a_ref[v] = jnp.where(even, right, left)
         side_b_ref[v] = jnp.where(even, left, right)
     if ends:
-        top, bottom = y_ref[:, :SHIFT], y_ref[:, 2 * WIN - SHIFT :]
+        top, bottom = y_ref[:, :SHIFT].astype(BF16), y_ref[:, 2 * WIN - SHIFT :].astype(BF16)
         even = is_even("ty")
         refs[8][...] = jnp.where(even, bottom, top)
         if len(refs) == 12:
             refs[9][...] = jnp.where(even, top, bottom)
 
 
-def place_rows(store, ends_ref, middle_ref, v):
-    store(0, ends_ref[v, :WIN])
-    for r in range(0, middle_ref.shape[1], WIN):
-        store(WIN + r, middle_ref[v, r : r + WIN])
-    store(WIN + middle_ref.shape[1], ends_ref[v, WIN:])
-
-
-def inner_kernel(
-    heads, channels, group, ends_ref, middle_ref, bias_ref, *refs
-):
-    *weights, y_ref, marks_ref, held, x_held = refs
-    height, breadth, lanes = held.shape
+def tile_rows(ends_ref, middle_ref, v, first, count, columns):
+    height = middle_ref.shape[1] + 2 * WIN
+    pieces = []
+    while count > 0:
+        if first < WIN:
+            ref, at, limit = ends_ref, first, WIN - first
+        elif first < height - WIN:
+            ref, at, limit = middle_ref, first - WIN, height - WIN - first
+        else:
+            ref, at, limit = ends_ref, first - height + 2 * WIN, height - first
+        taken = min(count, limit)
+        pieces.append(ref[v, at : at + taken, columns])
+        first, count = first + taken, count - taken
+    return pieces[0] if len(pieces) == 1 else jnp.concatenate(pieces, axis=0)
+
+
+def inner_kernel(heads, channels, ends_ref, middle_ref, bias_ref, *refs):
+    *weights, y_ref, marks_ref = refs
+    breadth, lanes = middle_ref.shape[2:]
+    strips = middle_ref.shape[1] // WIN + 2
     count = breadth // WIN - 1
-
-    @pl.when(pl.program_id(0) == 0)
-    def _():
-        for v in range(VAR_DEV):
-
-            def store(first, rows):
-                rows = rows.astype(F32)
-                held[first : first + WIN] = rows
-                if v == 0:
-                    marks_ref[first // WIN] = windows_of(rows[:, :, lanes - LANES :]).astype(BF16)
-
-            place_rows(store, ends_ref, middle_ref, v)
-            for strip in range(height // WIN - 1):
-                rows = slice(strip * WIN + SHIFT, (strip + 1) * WIN + SHIFT)
-                for w in range(count):
-                    at = SHIFT + w * WIN
-                    x_held[strip * count + w, v] = held[rows, at : at + WIN].reshape(CELLS, lanes)
-
-    base = pl.program_id(0) * group
-    x = x_held[pl.ds(base, group)].reshape(group * VAR_DEV * CELLS, lanes)
-    pairs = [(w, 0, 1) for w in range(group)]
-    results = swin_block(x, pairs, heads, channels, lambda v: bias_ref[v], *weights)
-    for w in range(group):
-        y_ref[w] = results[w].astype(BF16).reshape(VAR_DEV, CELLS, lanes)
+    for strip in range(strips):
+        rows = tile_rows(ends_ref, middle_ref, 0, strip * WIN, WIN, slice(None))
+        marks_ref[strip] = windows_of(rows[:, :, lanes - LANES :]).astype(BF16)
+    x = jnp.concatenate(
+        [
+            tile_rows(
+                ends_ref,
+                middle_ref,
+                v,
+                strip * WIN + SHIFT,
+                WIN,
+                slice(SHIFT + w * WIN, SHIFT + (w + 1) * WIN),
+            ).reshape(CELLS, lanes)
+            for strip in range(strips - 1)
+            for w in range(count)
+            for v in range(VAR_DEV)
+        ],
+        axis=0,
+    )
+    pairs = [(w, 0, 1) for w in range((strips - 1) * count)]
+    results = swin_block(x, pairs, 4, heads, channels, lambda v: bias_ref[v], *weights)
+    for w, result in enumerate(results):
+        y_ref[w] = result.astype(BF16).reshape(VAR_DEV, CELLS, lanes)
 
 
 def received(refs, axis, after, place):
@@ -542,7 +595,6 @@
 def outer_kernel(
     heads,
     channels,
-    group,
     swaps,
     ends_ref,
     middle_ref,
@@ -550,7 +602,7 @@
 ):
     across, sides, (inner_ref, bias_ref) = refs[:swaps], refs[swaps : swaps + 2], refs[swaps + 2 : swaps + 4]
     refs = refs[swaps + 4 :]
-    *weights, w_recon, keep_ref, give_ref, rows_held, sides_held, x_held, y_held, acc = refs
+    *weights, w_recon, keep_ref, give_ref, rows_held, x_held, y_held, acc = refs
     lanes = middle_ref.shape[3]
     height, breadth = middle_ref.shape[1] + 2 * WIN, middle_ref.shape[2]
     tall, wide = height + 2 * SHIFT, breadth + 2 * SHIFT
@@ -569,9 +621,7 @@
             rows_held[outside : outside + SHIFT, between] = marked(
                 across, "ty", end == 1, v
             )
-            rows_held[inside : inside + SHIFT, between] = ends_ref[
-                v, first : first + SHIFT
-            ].astype(F32)
+            rows_held[inside : inside + SHIFT, between] = ends_ref[v, first : first + SHIFT]
             side_first = SHIFT * SHIFT if end == 0 else (tall - 2 * SHIFT) * SHIFT
             for side, at in ((0, 0), (1, wide - SHIFT)):
                 for rows, start in ((outside, corner), (inside, side_first)):
@@ -584,38 +634,26 @@
                 x_held[end * count + w, v] = rows_held[:, w * WIN : (w + 1) * WIN].reshape(
                     CELLS, lanes
                 )
-
-        def store(first, rows):
-            sides_held[first : first + WIN, :WIN] = rows[:, :WIN].astype(F32)
-            sides_held[first : first + WIN, WIN:] = rows[:, breadth - WIN :].astype(F32)
-
-        place_rows(store, ends_ref, middle_ref, v)
         for strip in range(1, strips - 1):
-            rows = slice(strip * WIN - SHIFT, (strip + 1) * WIN - SHIFT)
             cut = slice(strip * WIN * SHIFT, (strip + 1) * WIN * SHIFT)
             for end in range(2):
                 piece = marked(sides, "tx", end == 1, (v, cut))
                 piece = piece.reshape(WIN, SHIFT, lanes)
-                at = 0 if end == 0 else WIN + SHIFT
-                own = sides_held[rows, at : at + SHIFT]
+                at = 0 if end == 0 else breadth - SHIFT
+                near = slice(at, at + SHIFT)
+                own = tile_rows(ends_ref, middle_ref, v, strip * WIN - SHIFT, WIN, near)
                 both = [piece, own] if end == 0 else [own, piece]
                 slot = 2 * count + 2 * (strip - 1) + end
                 x_held[slot, v] = jnp.concatenate(both, axis=1).reshape(CELLS, lanes)
 
     slots = x_held.shape[0]
-
-    def border(step, carry):
-        x = x_held[pl.ds(step * group, group)].reshape(group * VAR_DEV * CELLS, lanes)
-        pairs = [(w, 0, 1) for w in range(group)]
-        results = swin_block(x, pairs, heads, channels, lambda v: bias_ref[v], *weights)
-        at = channels + CLASSES
-        for w in range(group):
-            block = x[w * LANES : (w + 1) * LANES]
-            y = results[w] * block[:, at : at + 1]
-            y_held[step * group + w] = y.astype(BF16).reshape(VAR_DEV, CELLS, lanes)
-        return carry
-
-    lax.fori_loop(0, slots // group, border, 0)
+    x = x_held[...].reshape(slots * VAR_DEV * CELLS, lanes)
+    pairs = [(w, 0, 1) for w in range(slots)]
+    results = swin_block(x, pairs, 6, heads, channels, lambda v: bias_ref[v], *weights)
+    at = channels + CLASSES
+    for w in range(slots):
+        valid = x[w * LANES : (w + 1) * LANES, at : at + 1]
+        y_held[w] = (results[w] * valid).astype(BF16).reshape(VAR_DEV, CELLS, lanes)
 
     weights = w_recon[...].reshape(VAR_DEV * lanes, 3 * lanes)
 
@@ -843,7 +881,7 @@
     def block_one(places, name):
         rows = len(places) * WIN
         outs = [
-            ((VAR_DEV, rows, breadth, lanes), BF16),
+            ((VAR_DEV, rows, breadth, lanes), F32),
             ((VAR_DEV, rows * SHIFT, lanes), BF16),
             ((VAR_DEV, rows * SHIFT, lanes), BF16),
         ]
@@ -883,23 +921,16 @@
 
     arrays, specs = block_specs(1)
     inner_count = (strips - 1) * (breadth // WIN - 1)
-    group = next(g for g in range(24, 0, -1) if inner_count % g == 0)
+    outs = [
+        jax.ShapeDtypeStruct((inner_count, VAR_DEV, CELLS, lanes), BF16),
+        jax.ShapeDtypeStruct((strips, tokens, LANES), BF16),
+    ]
     inner, marks = pl.pallas_call(
-        functools.partial(inner_kernel, heads, channels, group),
-        grid=(inner_count // group,),
+        functools.partial(inner_kernel, heads, channels),
+        grid=(1,),
         in_specs=[whole(y_ends), whole(y_middle), *specs],
-        out_specs=[
-            pl.BlockSpec((group, VAR_DEV, CELLS, lanes), lambda i: (i, 0, 0, 0)),
-            pl.BlockSpec((strips, tokens, LANES), lambda i: (0, 0, 0)),
-        ],
-        out_shape=[
-            jax.ShapeDtypeStruct((inner_count, VAR_DEV, CELLS, lanes), BF16),
-            jax.ShapeDtypeStruct((strips, tokens, LANES), BF16),
-        ],
-        scratch_shapes=[
-            pltpu.VMEM((height, breadth, lanes), F32),
-            pltpu.VMEM((inner_count, VAR_DEV, CELLS, lanes), F32),
-        ],
+        out_specs=[whole(o) for o in outs],
+        out_shape=outs,
         compiler_params=params(20),
         cost_estimate=cost(inner_count * VAR_DEV),
         name="block_two_inner",
@@ -907,18 +938,16 @@
 
     tall, wide = height + 2 * SHIFT, breadth + 2 * SHIFT
     slots = 2 * (tall + wide) // WIN - 4
-    group = next(g for g in range(24, 0, -1) if slots % g == 0)
     operands = (y_ends, y_middle, *across, *sides, inner)
     half_shape = jax.ShapeDtypeStruct((strips // 2, out_channels, tokens), BF16)
     keep, give = pl.pallas_call(
-        functools.partial(outer_kernel, heads, channels, group, len(across)),
+        functools.partial(outer_kernel, heads, channels, len(across)),
         grid=(1,),
         in_specs=[*[whole(a) for a in operands], *specs, whole(recon)],
         out_specs=[whole(half_shape)] * 2,
         out_shape=[half_shape] * 2,
         scratch_shapes=[
             pltpu.VMEM((WIN, wide, lanes), F32),
-            pltpu.VMEM((height, 2 * WIN, lanes), F32),
             pltpu.VMEM((slots, VAR_DEV, CELLS, lanes), F32),
             pltpu.VMEM((slots, VAR_DEV, CELLS, lanes), BF16),
             pltpu.VMEM((tall + WIN, wide, lanes), F32),

time: 48.5 us -> 47 us (0.969)
  Pallas kernels: 32.6 us -> 30.6 us
    pallas_call x2, Pallas kernels: 17.3 us -> 15.6 us  [the longest x1 9.72 us: local(): pl.pallas_call(functools.partial(outer_kernel, heads, channels, len(acros...]
  transfers between devices with their start and end apart: 6 -> 6, of which waited for: 3 -> 3; matrix products, arithmetic and copies ran while one was open for 0% -> 0% of each run, Pallas kernels for 26% -> 25%
where the time goes in v6:
time: 47 us; the launch traced here: 46.7 us
  Pallas kernels  30.6 us (65%)
  starting transfers between devices  10.5 us (22%)
  waiting for transfers between devices  4.72 us (10%)
  other arithmetic  0.82 us (2%)
    pallas_call x1, Pallas kernels, local(): pl.pallas_call(functools.partial(outer_kernel, heads, channels, len(acros...  9.72 us
    pallas_call x2, Pallas kernels, block_one(): pl.pallas_call(functools.partial(first_kernel, heads, channels, places),...  8.83 us
    ppermute x3, starting transfers between devices, swap_pairs(): return lax.ppermute(strip, axis, pairs + [(j, i) for i, j in pairs])  6.04 us
    pallas_call x1, Pallas kernels, local(): pl.pallas_call(functools.partial(inner_kernel, heads, channels), grid=(1,...  5.89 us
    ppermute x3, waiting for transfers between devices, whole_swap(): return lax.ppermute(a, 'var', [(i, i ^ bit) for i in range(count)])  4.71 us
    ppermute x3, starting transfers between devices, whole_swap(): return lax.ppermute(a, 'var', [(i, i ^ bit) for i in range(count)])  4.43 us
    pallas_call x1, Pallas kernels, local(): pl.pallas_call(functools.partial(prepare_kernel, heads), grid=(1,), in_sp...  4.42 us
    pallas_call x1, Pallas kernels, local(): pl.pallas_call(functools.partial(refine_kernel, refine_heads, channels %...  1.71 us
  transfers between devices with their start and end apart: 6, of which 3 were waited for; matrix products, arithmetic and copies ran while one was open for 0% of the time, Pallas kernels for 25%

profile of v6, /device:TPU:9, one launch (start us, length us, event | category | flops | bytes accessed | tf_op | source)
XLA Modules:
  0.0 46.7 jit_solution(9884066565324709834)
XLA Ops:
  0.0 4.4 %prepare.1 = (bf16[2,400,256]{2,1,0:T(8,128)(2,1)S(1)}, bf16[2,256,256]{2,1,0:T(8,128)(2,1)S(1)}, bf16[2,256,256]{2,1,0:T(8,128)(2,1)S(1)}, bf16[2,256,384]{2,1,...) custom-call(bf16[64,32,180]{2,1,0:T(8,128)(2,1)} %features_ref.1, ...), custom_call_target="tpu_custom_call" | custom-call | tf_op jit(solution)/shard_map/prepare/pallas_call | solution.py:845
  4.4 2.8 %block_one_ends.1 = (f32[2,16,32,256]{3,2,1,0:T(8,128)S(1)}, bf16[2,64,256]{2,1,0:T(8,128)(2,1)S(1)}, bf16[2,64,256]{2,1,0:T(8,128)(2,1)S(1)}, bf16[2,4,32,256]{3,2,1,0:T(8,128)(2,1)S(1)}) custom-call(bf16[64,32,180]{2,1,0:T(8,128)(2,1)S(1)} %get-tuple-element.31.x_ref, s32[32,64]{1,0:T(8,128)S(1)} %get-tuple-element.32.labels_ref, ...), custom_call_target="tpu_custom_call" | custom-call | flops 6400000000 | bytes 3200000 | tf_op jit(solution)/shard_map/block_one_ends/pallas_call | solution.py:891
  7.2 1.3 %collective-permute-start = (bf16[2,4,32,256]{3,2,1,0:T(8,128)(2,1)S(1)}, bf16[2,4,32,256]{3,2,1,0:T(8,128)(2,1)S(1)}, u32[]{:S(2)}, u32[]{:S(2)}) collective-permute-start(bf16[2,4,32,256]{3,2,1,0:T(8,128)(2,1)S(1)} %get-tuple-element.41), channel_id=1, source_target_pairs={{0,4},{4,0},{1,5},{5,1},{2,6},{6,2},{3,7},{7,3},{8,12},{12,8},{9,1... | collective-permute-start | bytes 393224 | tf_op jit(solution)/shard_map/ppermute | solution.py:778
  8.6 6.0 %block_one_middle.1 = (f32[2,48,32,256]{3,2,1,0:T(8,128)S(1)}, bf16[2,192,256]{2,1,0:T(8,128)(2,1)S(1)}, bf16[2,192,256]{2,1,0:T(8,128)(2,1)S(1)}) custom-call(bf16[64,32,180]{2,1,0:T(8,128)(2,1)S(1)} %get-tuple-element.31.x_ref, s32[32,64]{1,0:T(8,128)S(1)} %get-tuple-element.32.labels_ref, f32[2,2,64,384]{3,2,1,0:T(8,128)S(1)} %get-tuple-element.33.bias_ref.refs_4_, ...), custom_call_target="tpu_custom_call" | custom-call | flops 19200000000 | bytes 9600000 | tf_op jit(solution)/shard_map/block_one_middle/pallas_call | solution.py:891
  14.6 0.0 collective-permute-done.refs_0_
  14.6 0.1 edges.1
  14.7 0.2 collective-permute-start.1
  14.9 4.5 %collective-permute-start.2 = (bf16[2,288,256]{2,1,0:T(8,128)(2,1)S(1)}, bf16[2,288,256]{2,1,0:T(8,128)(2,1)S(1)}, u32[]{:S(2)}, u32[]{:S(2)}) collective-permute-start(bf16[2,288,256]{2,1,0:T(8,128)(2,1)S(1)} %get-tuple-element.47), channel_id=1, source_target_pairs={{1,2},{2,1},{5,6},{6,5},{9,10},{10,9},{13,14},{14,13},{17,18},{18,... | collective-permute-start | bytes 884744 | tf_op jit(solution)/shard_map/ppermute | solution.py:778
  19.4 5.9 %block_two_inner.1 = (bf16[21,2,64,256]{3,2,1,0:T(8,128)(2,1)S(1)}, bf16[8,256,128]{2,1,0:T(8,128)(2,1)S(1)}) custom-call(f32[2,16,32,256]{3,2,1,0:T(8,128)S(1)} %get-tuple-element.39.ends_ref, f32[2,48,32,256]{3,2,1,0:T(8,128)S(1)} %get-tuple-element.40.middle_ref, f32[2,2,64,384]{3,2,1,0:T(8,128)S(1)} %get-tuple-element.33.bias_ref.refs_4_, ...), custom_call_target="tpu_custom_call" | custom-call | flops 16800000000 | bytes 8400000 | tf_op jit(solution)/shard_map/block_two_inner/pallas_call | solution.py:928
  25.3 0.0 collective-permute-done.1.refs_1_
  25.3 0.0 collective-permute-done.2.refs_2_
  25.3 9.7 %block_two_border.1 = (bf16[4,48,256]{2,1,0:T(8,128)(2,1)S(1)}, bf16[4,48,256]{2,1,0:T(8,128)(2,1)S(1)}) custom-call(f32[2,16,32,256]{3,2,1,0:T(8,128)S(1)} %get-tuple-element.39.ends_ref, f32[2,48,32,256]{3,2,1,0:T(8,128)S(1)} %get-tuple-element.40.middle_ref, bf16[2,4,32,256]{3,2,1,0:T(8,128)(2,1)S(1)} %collective-permute-done.refs_0_, ...), custom_call_target="tpu_custom_call" | custom-call | tf_op jit(solution)/shard_map/block_two_border/pallas_call | solution.py:943
  35.1 1.9 %collective-permute-start.3 = (bf16[4,48,256]{2,1,0:T(8,128)(2,1)S(1)}, bf16[4,48,256]{2,1,0:T(8,128)(2,1)S(1)}, u32[]{:S(2)}, u32[]{:S(2)}) collective-permute-start(bf16[4,48,256]{2,1,0:T(8,128)(2,1)S(1)} %get-tuple-element.51), channel_id=1, source_target_pairs={{0,8},{8,0},{16,24},{24,16},{1,9},{9,1},{17,25},{25,17},{2,10},{10... | collective-permute-start | bytes 294920 | tf_op jit(solution)/shard_map/ppermute | solution.py:783
  37.0 0.9 %collective-permute-done.3 = bf16[4,48,256]{2,1,0:T(8,128)(2,1)S(1)} collective-permute-done((bf16[4,48,256]{2,1,0:T(8,128)(2,1)S(1)}, bf16[4,48,256]{2,1,0:T(8,128)(2,1)S(1)}, u32[]{:S(2)}, u32[]{:S(2)}) %collective-permute-start.3) | collective-permute-done | bytes 98336 | tf_op jit(solution)/shard_map/ppermute | solution.py:783
  37.9 1.3 %collective-permute-start.4 = (bf16[4,48,256]{2,1,0:T(8,128)(2,1)S(1)}, bf16[4,48,256]{2,1,0:T(8,128)(2,1)S(1)}, u32[]{:S(2)}, u32[]{:S(2)}) collective-permute-start(bf16[4,48,256]{2,1,0:T(8,128)(2,1)S(1)} %add_convert_fusion.mine_ref), channel_id=1, source_target_pairs={{0,16},{8,24},{16,0},{24,8},{1,17},{9,25},{17,1},{25,9},{2,18},{10... | collective-permute-start | bytes 294920 | tf_op jit(solution)/shard_map/ppermute | solution.py:783
  39.2 2.8 %collective-permute-done.4.other_ref = bf16[4,48,256]{2,1,0:T(8,128)(2,1)S(1)} collective-permute-done((bf16[4,48,256]{2,1,0:T(8,128)(2,1)S(1)}, bf16[4,48,256]{2,1,0:T(8,128)(2,1)S(1)}, u32[]{:S(2)}, u32[]{:S(2)}) %collective-permute-start.4) | collective-permute-done | bytes 98336 | tf_op jit(solution)/shard_map/ppermute | solution.py:783
  42.0 1.7 %refinement.1 = bf16[3,128,128]{2,1,0:T(8,128)(2,1)S(1)} custom-call(bf16[4,48,256]{2,1,0:T(8,128)(2,1)S(1)} %add_convert_fusion.mine_ref, bf16[4,48,256]{2,1,0:T(8,128)(2,1)S(1)} %collective-permute-done.4.other_ref, bf16[8,256,128]{2,1,0:T(8,128)(2,1)S(1)} %get-tuple-element.52.marks_ref, f32[64,128]{1,0:T(8,128)S(1)} %get-tuple-element.53.bias_ref, ...), custom_call_target="tpu_custom_call" | custom-call | tf_op jit(solution)/shard_map/refinement/pallas_call | solution.py:964
  43.8 1.2 %collective-permute-start.5 = (bf16[3,128,128]{2,1,0:T(8,128)(2,1)S(1)}, bf16[3,128,128]{2,1,0:T(8,128)(2,1)S(1)}, u32[]{:S(2)}, u32[]{:S(2)}) collective-permute-start(bf16[3,128,128]{2,1,0:T(8,128)(2,1)S(1)} %refinement.1), channel_id=1, source_target_pairs={{0,8},{8,0},{16,24},{24,16},{1,9},{9,1},{17,25},{25,17},{2,10},{10... | collective-permute-start | bytes 294920 | tf_op jit(solution)/shard_map/ppermute | solution.py:783
  45.0 0.9 %collective-permute-done.5 = bf16[3,128,128]{2,1,0:T(8,128)(2,1)S(1)} collective-permute-done((bf16[3,128,128]{2,1,0:T(8,128)(2,1)S(1)}, bf16[3,128,128]{2,1,0:T(8,128)(2,1)S(1)}, u32[]{:S(2)}, u32[]{:S(2)}) %collective-permute-start.5) | collective-permute-done | bytes 98336 | tf_op jit(solution)/shard_map/ppermute | solution.py:783
  46.0 0.8 %maximum_convert_fusion = f32[3,256,128]{2,1,0:T(8,128)} fusion(bf16[3,128,128]{2,1,0:T(8,128)(2,1)S(1)} %get-tuple-element.58, bf16[3,128,128]{2,1,0:T(8,128)(2,1)S(1)} %get-tuple-element.57), kind=kLoop, calls=%fused_computation | loop fusion | flops 393216 | bytes 589824 | tf_op jit(solution)/shard_map/convert_element_type | solution.py:977
  (2 shorter events, 0.0 us)
Async XLA Ops:
  7.2 7.3 %collective-permute-start = (bf16[2,4,32,256]{3,2,1,0:T(8,128)(2,1)S(1)}, bf16[2,4,32,256]{3,2,1,0:T(8,128)(2,1)S(1)}, u32[]{:S(2)}, u32[]{:S(2)}) collective-permute-start(bf16[2,4,32,256]{3,2,1,0:T(8,128)(2,1)S(1)} %get-tuple-element.41), channel_id=1, source_target_pairs={{0,4},{4,0},{1,5},{5,1},{2,6},{6,2},{3,7},{7,3},{8,12},{12,8},{9,1... | collective-permute-start | bytes 393224 | tf_op jit(solution)/shard_map/ppermute | solution.py:778
  14.7 10.6 %collective-permute-start.1 = (bf16[2,288,256]{2,1,0:T(8,128)(2,1)S(1)}, bf16[2,288,256]{2,1,0:T(8,128)(2,1)S(1)}, u32[]{:S(2)}, u32[]{:S(2)}) collective-permute-start(bf16[2,288,256]{2,1,0:T(8,128)(2,1)S(1)} %get-tuple-element.46), channel_id=1, source_target_pairs={{0,1},{2,3},{1,0},{3,2},{4,5},{6,7},{5,4},{7,6},{8,9},{10,11},{9,8... | collective-permute-start | bytes 884744 | tf_op jit(solution)/shard_map/ppermute | solution.py:778
  14.9 10.4 %collective-permute-start.2 = (bf16[2,288,256]{2,1,0:T(8,128)(2,1)S(1)}, bf16[2,288,256]{2,1,0:T(8,128)(2,1)S(1)}, u32[]{:S(2)}, u32[]{:S(2)}) collective-permute-start(bf16[2,288,256]{2,1,0:T(8,128)(2,1)S(1)} %get-tuple-element.47), channel_id=1, source_target_pairs={{1,2},{2,1},{5,6},{6,5},{9,10},{10,9},{13,14},{14,13},{17,18},{18,... | collective-permute-start | bytes 884744 | tf_op jit(solution)/shard_map/ppermute | solution.py:778
  35.1 2.9 %collective-permute-start.3 = (bf16[4,48,256]{2,1,0:T(8,128)(2,1)S(1)}, bf16[4,48,256]{2,1,0:T(8,128)(2,1)S(1)}, u32[]{:S(2)}, u32[]{:S(2)}) collective-permute-start(bf16[4,48,256]{2,1,0:T(8,128)(2,1)S(1)} %get-tuple-element.51), channel_id=1, source_target_pairs={{0,8},{8,0},{16,24},{24,16},{1,9},{9,1},{17,25},{25,17},{2,10},{10... | collective-permute-start | bytes 294920 | tf_op jit(solution)/shard_map/ppermute | solution.py:783
  37.9 4.1 %collective-permute-start.4 = (bf16[4,48,256]{2,1,0:T(8,128)(2,1)S(1)}, bf16[4,48,256]{2,1,0:T(8,128)(2,1)S(1)}, u32[]{:S(2)}, u32[]{:S(2)}) collective-permute-start(bf16[4,48,256]{2,1,0:T(8,128)(2,1)S(1)} %add_convert_fusion.mine_ref), channel_id=1, source_target_pairs={{0,16},{8,24},{16,0},{24,8},{1,17},{9,25},{17,1},{25,9},{2,18},{10... | collective-permute-start | bytes 294920 | tf_op jit(solution)/shard_map/ppermute | solution.py:783
  43.8 2.2 %collective-permute-start.5 = (bf16[3,128,128]{2,1,0:T(8,128)(2,1)S(1)}, bf16[3,128,128]{2,1,0:T(8,128)(2,1)S(1)}, u32[]{:S(2)}, u32[]{:S(2)}) collective-permute-start(bf16[3,128,128]{2,1,0:T(8,128)(2,1)S(1)} %refinement.1), channel_id=1, source_target_pairs={{0,8},{8,0},{16,24},{24,16},{1,9},{9,1},{17,25},{25,17},{2,10},{10... | collective-permute-start | bytes 294920 | tf_op jit(solution)/shard_map/ppermute | solution.py:783

commit v7 on v6

--- a/solution.py
+++ b/solution.py
@@ -138,8 +138,8 @@
     labels_ref,
     *refs,
 ):
-    sources, outs, scratch = refs[:9], refs[9:22], refs[22:]
-    held, (rows_ref, tables_ref, semaphores) = scratch[:9], scratch[9:]
+    sources, outs, scratch = refs[:6], refs[6:15], refs[15:]
+    held, spreads, (rows_ref, tables_ref, semaphores) = scratch[:6], scratch[6:10], scratch[10:]
     (
         qvt_out,
         key_out,
@@ -148,10 +148,6 @@
         down_out,
         recon_out,
         bias_out,
-        refine_qvt_out,
-        refine_key_out,
-        refine_proj_out,
-        refine_bias_out,
         features_out,
         labels_out,
     ) = outs
@@ -172,23 +168,15 @@
         down_ref,
         swin_bias_ref,
         recon_ref,
-        refine_qkv_ref,
-        refine_proj_ref,
-        refine_bias_ref,
     ) = held
     channels, blocks, hidden = up_ref.shape
     width = channels // heads
     lanes = key_out.shape[1]
     head_rows = heads * HEAD_ROWS
     taps, out, _ = recon_ref.shape
-    refine_heads = refine_bias_ref.shape[0]
-    refine_width = out // refine_heads
-    refine_rows = refine_heads * HEAD_ROWS
-    mark = channels % LANES
     both = blocks * channels
 
-    for arrival in (arrivals[4], arrivals[8]):
-        arrival.wait()
+    arrivals[4].wait()
     for i in range(blocks):
         tables_ref[i * heads : (i + 1) * heads] = swin_bias_ref[:, i]
     rows = []
@@ -196,51 +184,61 @@
         code = lax.axis_index("var") * VAR_DEV + v
         turn, flip_rows, flip_cols = code // 4 == 1, code // 2 % 2 == 1, code % 2 == 1
         rows.append(bias_rows(tables_ref[: blocks * heads], turn, flip_rows, flip_cols))
-    never = lax.axis_index("var") < 0
-    refine_table = bias_rows(refine_bias_ref[...], never, never, never)
-    for arrival in (*arrivals[:4], *arrivals[5:8]):
+    row = iota((2 * LANES, 1), 0)
+    head, unit = row % LANES // HEAD_ROWS * 2 + row // LANES, row % HEAD_ROWS
+    proj_source = jnp.where((head < heads) & (unit < width), head * width + unit, -1)
+    query_values = pick_rows(query_value_source(heads, width, channels), 3 * channels)
+    keys = pick_columns(head_source(iota((1, lanes), 1), heads, width, channels), 3 * channels)
+    hidden_rows = pick_rows(iota((down_out.shape[1], 1), 0), hidden)
+    proj_rows = pick_rows(proj_source, lanes)
+    for arrival in (*arrivals[:4], arrivals[5]):
         arrival.wait()
+
+    def block_rows(ref, spread_ref):
+        size = ref.shape[2]
+        rows = ref[...].reshape(both, size).astype(F32)
+        pieces = [[] for _ in range(blocks)]
+        for at in range(0, size, LANES):
+            used = min(LANES, size - at)
+            place = at // LANES
+            spread_ref[place, :both, :used] = rows[:, at : at + used]
+            spread_ref[place, both:] = jnp.zeros((blocks * lanes - both, LANES), F32)
+            for i in range(blocks):
+                piece = spread_ref[place, pl.ds(i, lanes, stride=blocks), :]
+                pieces[i].append(piece[:, :used].astype(BF16))
+        return [jnp.concatenate(piece, axis=1) for piece in pieces]
+
     qkv, proj, up, down = (
-        ref[...].reshape(both, ref.shape[2]) for ref in (qkv_ref, proj_ref, up_ref, down_ref)
+        block_rows(ref, spread)
+        for ref, spread in zip((qkv_ref, proj_ref, up_ref, down_ref), spreads)
     )
 
-    def block_source(index, i):
-        return jnp.where(index < channels, index * blocks + i, -1)
-
-    moved = exact(pick_rows(query_value_source(heads, width, channels), 3 * channels), qkv, NT)
-    keys = exact(
-        qkv, pick_columns(head_source(iota((1, lanes), 1), heads, width, channels), 3 * channels)
-    )
-    turned = exact(pick_rows(iota((down_out.shape[1], 1), 0), hidden), down, NT)
     pad = pick_rows(iota((lanes, 1), 0), channels)
     kernel = exact(pad, recon_ref[...].reshape(taps * out, channels), NT)
-    weight = refine_qkv_ref[...]
-    source = query_value_source(refine_heads, refine_width, out)
-    refine_moved = exact(pick_rows(source, 3 * out), weight, NT)
-    source = head_source(iota((1, LANES), 1), refine_heads, refine_width, out)
-    refine_keys = exact(weight, pick_columns(source, 3 * out))
-    refine_proj = []
-    for h in range(refine_heads):
-        row = iota((LANES, 1), 0)
-        source = jnp.where(row < refine_width, row + h * refine_width, -1)
-        refine_proj.append(exact(pick_rows(source, out), refine_proj_ref[...]))
-
-    row = iota((2 * LANES, 1), 0)
-    head, unit = row % LANES // HEAD_ROWS * 2 + row // LANES, row % HEAD_ROWS
-    proj_source = jnp.where((head < heads) & (unit < width), head * width + unit, channels)
+    row = iota((2 * head_rows + 16, 1), 0)
+    scale = jnp.where(row < head_rows, width**-0.5 * LOG2E, 1.0)
+    query_add = query_value_marks(heads, width, lanes, channels)
+    key_add = key_marks(lanes, lanes, channels, head_rows)
     for i in range(blocks):
-        for ref in (proj_out, up_out):
-            ref[i] = jnp.zeros(ref.shape[1:], BF16)
-        proj_out[i, :, :channels] = exact(pick_rows(block_source(proj_source, i), both), proj)
-        up_out[i, :, :hidden] = exact(pick_rows(block_source(iota((lanes, 1), 0), i), both), up)
+        qvt_out[i] = (dot(query_values, qkv[i], NT) * scale + query_add).astype(BF16)
+        key_out[i] = (dot(qkv[i], keys) + key_add).astype(BF16)
+        proj_out[i] = jnp.zeros(proj_out.shape[1:], BF16)
+        proj_out[i, :, :channels] = exact(proj_rows, proj[i])
+        up_out[i] = jnp.zeros(up_out.shape[1:], BF16)
+        up_out[i, :, :hidden] = up[i]
+        down_out[i] = (dot(hidden_rows, down[i], NT) * 0.5).astype(BF16)
     for v in range(VAR_DEV):
         code = lax.axis_index("var") * VAR_DEV + v
         turn, flip_rows, flip_cols = code // 4 == 1, code // 2 % 2 == 1, code % 2 == 1
-        lane = iota((1, 3 * lanes), 1)
-        row_step = lane // lanes - 1
-        lane = lane % lanes
-        col_step = jnp.where(lane >= LANES, 1, jnp.where(lane >= out, 0, -1))
-        channel = jnp.where(lane >= LANES, lane - LANES, jnp.where(lane >= out, lane - out, lane))
+        lane = iota((1, 4 * LANES), 1)
+        tile, lane = lane // LANES, lane % LANES
+        part = jnp.where(lane >= 2 * out, 2, jnp.where(lane >= out, 1, 0))
+        is_last = tile == 3
+        is_left = (tile == 0) & (part == 2)
+        row_step = jnp.where(is_last, part, jnp.where(is_left, 2, tile)) - 1
+        col_step = jnp.where(is_last | is_left, 2, part) - 1
+        channel = lane - part * out + jnp.where(is_left, LANES - 2 * out, 0)
+        used = (channel < out) & (is_last | is_left | (part < 2))
         row_step = jnp.where(flip_rows, -row_step, row_step)
         col_step = jnp.where(flip_cols, -col_step, col_step)
         tap = (jnp.where(turn, col_step, row_step) + 1) * 3
@@ -252,20 +250,54 @@
         source = channel // (SCALE * SCALE) * SCALE * SCALE
         source = source + jnp.where(turn, sub_col, sub_row) * SCALE
         source = tap * out + source + jnp.where(turn, sub_row, sub_col)
-        source = jnp.where(channel < out, source, -1)
+        source = jnp.where(used, source, -1)
         recon_out[v] = exact(kernel, pick_columns(source, taps * out))
 
-    row = iota((2 * head_rows + 16, 1), 0)
-    scale = jnp.where(row < head_rows, width**-0.5 * LOG2E, 1.0)
-    query_add = query_value_marks(heads, width, lanes, channels)
-    key_add = key_marks(lanes, lanes, channels, head_rows)
-    for i in range(blocks):
-        columns = pick_columns(block_source(iota((1, lanes), 1), i), both)
-        qvt_out[i] = (dot(moved, columns) * scale + query_add).astype(BF16)
-        down_out[i] = (dot(turned, columns) * 0.5).astype(BF16)
-        key_out[i] = (
-            dot(pick_rows(block_source(iota((lanes, 1), 0), i), both), keys) + key_add
-        ).astype(BF16)
+    for v in range(VAR_DEV):
+        for i in range(blocks):
+
+            def store(key_row, pair, value):
+                at = slice(key_row * WIN, (key_row + 1) * WIN)
+                bias_out[i, v, at, pair * LANES : (pair + 1) * LANES] = value
+
+            bias_grid(rows[v][i * heads : (i + 1) * heads], rows_ref, store)
+
+    for arrival in arrivals[6:]:
+        arrival.wait()
+
+
+def prepare_refine_kernel(
+    mark, after_ref, qkv_source, proj_source, bias_source, *refs
+):
+    refine_qvt_out, refine_key_out, refine_proj_out, refine_bias_out = refs[:4]
+    refine_qkv_ref, refine_proj_ref, refine_bias_ref, rows_ref, semaphores = refs[4:]
+    arrivals = [
+        pltpu.make_async_copy(source, target, semaphores.at[i])
+        for i, (source, target) in enumerate(
+            zip((qkv_source, proj_source, bias_source), refs[4:7])
+        )
+    ]
+    for arrival in arrivals:
+        arrival.start()
+    for arrival in arrivals:
+        arrival.wait()
+    out = refine_proj_ref.shape[0]
+    refine_heads = refine_bias_ref.shape[0]
+    refine_width = out // refine_heads
+    refine_rows = refine_heads * HEAD_ROWS
+    never = lax.axis_index("var") < 0
+    refine_table = bias_rows(refine_bias_ref[...], never, never, never)
+    weight = refine_qkv_ref[...]
+    source = query_value_source(refine_heads, refine_width, out)
+    refine_moved = exact(pick_rows(source, 3 * out), weight, NT)
+    source = head_source(iota((1, LANES), 1), refine_heads, refine_width, out)
+    refine_keys = exact(weight, pick_columns(source, 3 * out))
+    refine_proj = []
+    for h in range(refine_heads):
+        row = iota((LANES, 1), 0)
+        source = jnp.where(row < refine_width, row + h * refine_width, -1)
+        refine_proj.append(exact(pick_rows(source, out), refine_proj_ref[...]))
+
     row = iota((2 * refine_rows + 16, 1), 0)
     scale = jnp.where(row < refine_rows, refine_width**-0.5 * LOG2E, 1.0)
     out_pad = pick_rows(iota((LANES, 1), 0), out)
@@ -279,21 +311,10 @@
     for h in range(refine_heads):
         square = dot(refine_proj[h], out_pad, NT)
         refine_proj_out[h * out : (h + 1) * out] = square.T[:out].astype(BF16)
-    for v in range(VAR_DEV):
-        for i in range(blocks):
-
-            def store(key_row, pair, value):
-                at = slice(key_row * WIN, (key_row + 1) * WIN)
-                bias_out[i, v, at, pair * LANES : (pair + 1) * LANES] = value
-
-            bias_grid(rows[v][i * heads : (i + 1) * heads], rows_ref, store)
-
     def store_refine(key_row, pair, value):
         refine_bias_out[key_row * WIN : (key_row + 1) * WIN] = value
 
     bias_grid(refine_table, rows_ref, store_refine)
-    for arrival in arrivals[9:]:
-        arrival.wait()
 
 
 def twice_gelu(x):
@@ -431,7 +452,7 @@
     results.extend(y[i * LANES : (i + 1) * LANES] for i in range(len(pairs)))
 
 
-def swin_block(x, pairs, unit, *args):
+def swin_block(x, pairs, unit, lag, *args):
     places = x.shape[0] // LANES
     units = []
     for low in range(0, places, unit):
@@ -444,7 +465,7 @@
     tick = 0
     while running:
         for number in sorted(running):
-            if tick >= number and next(running[number][2], StopIteration) is StopIteration:
+            if tick >= number * lag and next(running[number][2], StopIteration) is StopIteration:
                 del running[number]
         tick += 1
     results = [None] * len(pairs)
@@ -492,7 +513,7 @@
     x = jnp.concatenate([held[:, : lanes - LANES], tail], axis=1)
     places = tokens // LANES
     pairs = [(place, v, v) for v in range(VAR_DEV) for place in range(places)]
-    results = swin_block(x, pairs, x.shape[0], heads, channels, lambda v: bias_ref[v], *weights)
+    results = swin_block(x, pairs, x.shape[0], 1, heads, channels, lambda v: bias_ref[v], *weights)
     for v in range(VAR_DEV):
         for k in range(len(strips)):
             windows = []
@@ -560,7 +581,7 @@
         axis=0,
     )
     pairs = [(w, 0, 1) for w in range((strips - 1) * count)]
-    results = swin_block(x, pairs, 4, heads, channels, lambda v: bias_ref[v], *weights)
+    results = swin_block(x, pairs, 4, 1, heads, channels, lambda v: bias_ref[v], *weights)
     for w, result in enumerate(results):
         y_ref[w] = result.astype(BF16).reshape(VAR_DEV, CELLS, lanes)
 
@@ -649,26 +670,34 @@
     slots = x_held.shape[0]
     x = x_held[...].reshape(slots * VAR_DEV * CELLS, lanes)
     pairs = [(w, 0, 1) for w in range(slots)]
-    results = swin_block(x, pairs, 6, heads, channels, lambda v: bias_ref[v], *weights)
+    results = swin_block(x, pairs, 6, 3, heads, channels, lambda v: bias_ref[v], *weights)
     at = channels + CLASSES
     for w in range(slots):
         valid = x[w * LANES : (w + 1) * LANES, at : at + 1]
         y_held[w] = (results[w] * valid).astype(BF16).reshape(VAR_DEV, CELLS, lanes)
 
-    weights = w_recon[...].reshape(VAR_DEV * lanes, 3 * lanes)
+    weights = w_recon[...].reshape(VAR_DEV * lanes, w_recon.shape[2])
+    out_channels = keep_ref.shape[1]
 
     def scatter(strip, windows):
         tokens = [jnp.concatenate(windows(v), axis=0) for v in range(VAR_DEV)]
         total = dot(jnp.concatenate(tokens, axis=1), weights)
-        total = total.reshape(count, WIN, WIN, 3 * lanes)
+        tiles = [total[:, i : i + LANES] for i in range(0, total.shape[1], LANES)]
+        spare = LANES - 2 * out_channels
+        lane = iota((1, LANES), 1)
+        last = jnp.where(
+            lane < spare,
+            pltpu.roll(tiles[3], spare, 1),
+            pltpu.roll(tiles[0], 2 * spare, 1),
+        )
+        after = [tiles[3], pltpu.roll(tiles[3], LANES - out_channels, 1), last]
         for e in range(3):
             rows = slice(strip * WIN + 2 - e, (strip + 1) * WIN + 2 - e)
-            for w in range(count):
-                across = slice(w * WIN, (w + 1) * WIN)
-                part = total[w, :, :, e * lanes : (e + 1) * lanes]
-                acc[rows, across] = part if e == 0 else acc[rows, across] + part
-
-    out_channels = keep_ref.shape[1]
+            for at, tile in ((0, tiles[e]), (LANES, after[e])):
+                tile = tile.reshape(count, WIN, WIN, LANES)
+                for w in range(count):
+                    place = (rows, slice(w * WIN, (w + 1) * WIN), slice(at, at + LANES))
+                    acc[place] = tile[w] if e == 0 else acc[place] + tile[w]
 
     def finish(strip):
         rows = slice(1 + SHIFT + strip * WIN, 1 + SHIFT + (strip + 1) * WIN)
@@ -821,9 +850,6 @@
         down_weight.transpose(2, 0, 1),
         jnp.swapaxes(swin_bias, 0, 1),
         jnp.swapaxes(recon_weight, 1, 2),
-        refine_qkv,
-        refine_proj,
-        refine_bias,
     )
     head_rows, refine_rows = heads * HEAD_ROWS, refine_heads * HEAD_ROWS
     shapes = [
@@ -832,12 +858,8 @@
         ((2, 2 * LANES, lanes), BF16),
         ((2, lanes, hidden), BF16),
         ((2, hidden, lanes), BF16),
-        ((VAR_DEV, lanes, 3 * lanes), BF16),
+        ((VAR_DEV, lanes, 4 * LANES), BF16),
         ((2, VAR_DEV, CELLS, heads * CELLS), F32),
-        ((2 * refine_rows + 16, LANES), BF16),
-        ((LANES, LANES), BF16),
-        ((refine_heads * out_channels, LANES), BF16),
-        ((CELLS, refine_heads * CELLS), F32),
         (features.shape, BF16),
         (operands[1].shape, jnp.int32),
     ]
@@ -850,15 +872,18 @@
         out_shape=shapes,
         scratch_shapes=[
             *[pltpu.VMEM(a.shape, a.dtype) for a in operands[2:]],
+            *[
+                pltpu.VMEM((round_up(a.shape[2], LANES) // LANES, 2 * lanes, LANES), F32)
+                for a in operands[2:6]
+            ],
             pltpu.VMEM((heads, WIN, LANES), F32),
             pltpu.VMEM((round_up(2 * heads, 8), swin_bias.shape[2]), F32),
             pltpu.SemaphoreType.DMA((len(operands),)),
         ],
-        compiler_params=params(12),
+        compiler_params=params(16),
         name="prepare",
     )(*[pltpu.with_memory_space_constraint(a, pltpu.HBM) for a in operands])
-    *swin, recon, bias, refine_qvt, refine_key, refine_projt, refine_grid = prepared[:-2]
-    features, labels_across = prepared[-2:]
+    *swin, recon, bias, features, labels_across = prepared
 
     def block_specs(i):
         arrays = (bias, *swin)
@@ -950,7 +975,7 @@
             pltpu.VMEM((WIN, wide, lanes), F32),
             pltpu.VMEM((slots, VAR_DEV, CELLS, lanes), F32),
             pltpu.VMEM((slots, VAR_DEV, CELLS, lanes), BF16),
-            pltpu.VMEM((tall + WIN, wide, lanes), F32),
+            pltpu.VMEM((tall + WIN, wide, 2 * LANES), F32),
         ],
         compiler_params=params(26),
         name="block_two_border",
@@ -958,6 +983,29 @@
 
     mine = (keep.astype(F32) + whole_swap(give, 1).astype(F32)).astype(BF16)
     other = whole_swap(mine, 2)
+    shapes = [
+        ((2 * refine_rows + 16, LANES), BF16),
+        ((LANES, LANES), BF16),
+        ((refine_heads * out_channels, LANES), BF16),
+        ((CELLS, refine_heads * CELLS), F32),
+    ]
+    shapes = [jax.ShapeDtypeStruct(*s) for s in shapes]
+    operands = (mine, refine_qkv, refine_proj, refine_bias)
+    refine_qvt, refine_key, refine_projt, refine_grid = pl.pallas_call(
+        functools.partial(prepare_refine_kernel, channels % LANES),
+        grid=(1,),
+        in_specs=[pl.BlockSpec(memory_space=pl.ANY)]
+        + [pl.BlockSpec(memory_space=pltpu.HBM)] * 3,
+        out_specs=[whole(s) for s in shapes],
+        out_shape=shapes,
+        scratch_shapes=[
+            *[pltpu.VMEM(a.shape, a.dtype) for a in operands[1:]],
+            pltpu.VMEM((refine_heads, WIN, LANES), F32),
+            pltpu.SemaphoreType.DMA((3,)),
+        ],
+        compiler_params=params(6),
+        name="prepare_refine",
+    )(mine, *[pltpu.with_memory_space_constraint(a, pltpu.HBM) for a in operands[1:]])
     colours = out_channels // (SCALE * SCALE)
     operands = (mine, other, marks, refine_grid, refine_qvt, refine_key, refine_projt)
     out_shape = (colours, height * SCALE // 2, breadth * SCALE)

time: 47 us -> 46.1 us (0.981)
  waiting for transfers between devices: 4.72 us -> 3.41 us
    ppermute x3, waiting for transfers between devices: 4.71 us -> 3.4 us  [whole_swap(): return lax.ppermute(a, 'var', [(i, i ^ bit) for i in range(count)])]
    pallas_call x0 -> x1, Pallas kernels: none -> 1.28 us  [local(): pl.pallas_call(functools.partial(prepare_refine_kernel, channels % LANES)...]
    pallas_call x1, Pallas kernels: 9.72 us -> 9.03 us  [local(): pl.pallas_call(functools.partial(outer_kernel, heads, channels, len(acros...]
  transfers between devices with their start and end apart: 6 -> 6, of which waited for: 3 -> 3; matrix products, arithmetic and copies ran while one was open for 0% -> 0% of each run, Pallas kernels for 25% -> 29%
where the time goes in v7:
time: 46.1 us; the launch traced here: 45.7 us
  Pallas kernels  30.9 us (67%)
  starting transfers between devices  10.5 us (23%)
  waiting for transfers between devices  3.41 us (7%)
  other arithmetic  0.82 us (2%)
    pallas_call x1, Pallas kernels, local(): pl.pallas_call(functools.partial(outer_kernel, heads, channels, len(acros...  9.03 us
    pallas_call x2, Pallas kernels, block_one(): pl.pallas_call(functools.partial(first_kernel, heads, channels, places),...  8.84 us
    ppermute x3, starting transfers between devices, swap_pairs(): return lax.ppermute(strip, axis, pairs + [(j, i) for i, j in pairs])  6.03 us
    pallas_call x1, Pallas kernels, local(): pl.pallas_call(functools.partial(inner_kernel, heads, channels), grid=(1,...  5.89 us
    ppermute x3, starting transfers between devices, whole_swap(): return lax.ppermute(a, 'var', [(i, i ^ bit) for i in range(count)])  4.45 us
    pallas_call x1, Pallas kernels, local(): pl.pallas_call(functools.partial(prepare_kernel, heads), grid=(1,), in_sp...  4.07 us
    ppermute x3, waiting for transfers between devices, whole_swap(): return lax.ppermute(a, 'var', [(i, i ^ bit) for i in range(count)])  3.4 us
    pallas_call x1, Pallas kernels, local(): pl.pallas_call(functools.partial(refine_kernel, refine_heads, channels %...  1.71 us
  transfers between devices with their start and end apart: 6, of which 3 were waited for; matrix products, arithmetic and copies ran while one was open for 0% of the time, Pallas kernels for 29%

profile of v7, /device:TPU:9, one launch (start us, length us, event | category | flops | bytes accessed | tf_op | source)
XLA Modules:
  0.0 45.7 jit_solution(6568614065286550640)
XLA Ops:
  0.0 4.1 %prepare.1 = (bf16[2,400,256]{2,1,0:T(8,128)(2,1)S(1)}, bf16[2,256,256]{2,1,0:T(8,128)(2,1)S(1)}, bf16[2,256,256]{2,1,0:T(8,128)(2,1)S(1)}, bf16[2,256,384]{2,1,...) custom-call(bf16[64,32,180]{2,1,0:T(8,128)(2,1)} %features_ref.1, ...), custom_call_target="tpu_custom_call" | custom-call | tf_op jit(solution)/shard_map/prepare/pallas_call | solution.py:867
  4.1 2.8 %block_one_ends.1 = (f32[2,16,32,256]{3,2,1,0:T(8,128)S(1)}, bf16[2,64,256]{2,1,0:T(8,128)(2,1)S(1)}, bf16[2,64,256]{2,1,0:T(8,128)(2,1)S(1)}, bf16[2,4,32,256]{3,2,1,0:T(8,128)(2,1)S(1)}) custom-call(bf16[64,32,180]{2,1,0:T(8,128)(2,1)S(1)} %get-tuple-element.31.x_ref, s32[32,64]{1,0:T(8,128)S(1)} %get-tuple-element.32.labels_ref, ...), custom_call_target="tpu_custom_call" | custom-call | flops 6400000000 | bytes 3200000 | tf_op jit(solution)/shard_map/block_one_ends/pallas_call | solution.py:916
  6.9 1.3 %collective-permute-start = (bf16[2,4,32,256]{3,2,1,0:T(8,128)(2,1)S(1)}, bf16[2,4,32,256]{3,2,1,0:T(8,128)(2,1)S(1)}, u32[]{:S(2)}, u32[]{:S(2)}) collective-permute-start(bf16[2,4,32,256]{3,2,1,0:T(8,128)(2,1)S(1)} %get-tuple-element.41), channel_id=1, source_target_pairs={{0,4},{4,0},{1,5},{5,1},{2,6},{6,2},{3,7},{7,3},{8,12},{12,8},{9,1... | collective-permute-start | bytes 393224 | tf_op jit(solution)/shard_map/ppermute | solution.py:807
  8.2 6.0 %block_one_middle.1 = (f32[2,48,32,256]{3,2,1,0:T(8,128)S(1)}, bf16[2,192,256]{2,1,0:T(8,128)(2,1)S(1)}, bf16[2,192,256]{2,1,0:T(8,128)(2,1)S(1)}) custom-call(bf16[64,32,180]{2,1,0:T(8,128)(2,1)S(1)} %get-tuple-element.31.x_ref, s32[32,64]{1,0:T(8,128)S(1)} %get-tuple-element.32.labels_ref, f32[2,2,64,384]{3,2,1,0:T(8,128)S(1)} %get-tuple-element.33.bias_ref.refs_4_, ...), custom_call_target="tpu_custom_call" | custom-call | flops 19200000000 | bytes 9600000 | tf_op jit(solution)/shard_map/block_one_middle/pallas_call | solution.py:916
  14.2 0.0 collective-permute-done.refs_0_
  14.2 0.1 edges.1
  14.3 0.2 collective-permute-start.1
  14.6 4.5 %collective-permute-start.2 = (bf16[2,288,256]{2,1,0:T(8,128)(2,1)S(1)}, bf16[2,288,256]{2,1,0:T(8,128)(2,1)S(1)}, u32[]{:S(2)}, u32[]{:S(2)}) collective-permute-start(bf16[2,288,256]{2,1,0:T(8,128)(2,1)S(1)} %get-tuple-element.47), channel_id=1, source_target_pairs={{1,2},{2,1},{5,6},{6,5},{9,10},{10,9},{13,14},{14,13},{17,18},{18,... | collective-permute-start | bytes 884744 | tf_op jit(solution)/shard_map/ppermute | solution.py:807
  19.1 5.9 %block_two_inner.1 = (bf16[21,2,64,256]{3,2,1,0:T(8,128)(2,1)S(1)}, bf16[8,256,128]{2,1,0:T(8,128)(2,1)S(1)}) custom-call(f32[2,16,32,256]{3,2,1,0:T(8,128)S(1)} %get-tuple-element.39.ends_ref, f32[2,48,32,256]{3,2,1,0:T(8,128)S(1)} %get-tuple-element.40.middle_ref, f32[2,2,64,384]{3,2,1,0:T(8,128)S(1)} %get-tuple-element.33.bias_ref.refs_4_, ...), custom_call_target="tpu_custom_call" | custom-call | flops 16800000000 | bytes 8400000 | tf_op jit(solution)/shard_map/block_two_inner/pallas_call | solution.py:953
  25.0 0.0 collective-permute-done.1.refs_1_
  25.0 0.0 collective-permute-done.2.refs_2_
  25.0 9.0 %block_two_border.1 = (bf16[4,48,256]{2,1,0:T(8,128)(2,1)S(1)}, bf16[4,48,256]{2,1,0:T(8,128)(2,1)S(1)}) custom-call(f32[2,16,32,256]{3,2,1,0:T(8,128)S(1)} %get-tuple-element.39.ends_ref, f32[2,48,32,256]{3,2,1,0:T(8,128)S(1)} %get-tuple-element.40.middle_ref, bf16[2,4,32,256]{3,2,1,0:T(8,128)(2,1)S(1)} %collective-permute-done.refs_0_, ...), custom_call_target="tpu_custom_call" | custom-call | tf_op jit(solution)/shard_map/block_two_border/pallas_call | solution.py:968
  34.0 1.9 %collective-permute-start.3 = (bf16[4,48,256]{2,1,0:T(8,128)(2,1)S(1)}, bf16[4,48,256]{2,1,0:T(8,128)(2,1)S(1)}, u32[]{:S(2)}, u32[]{:S(2)}) collective-permute-start(bf16[4,48,256]{2,1,0:T(8,128)(2,1)S(1)} %get-tuple-element.51), channel_id=1, source_target_pairs={{0,8},{8,0},{16,24},{24,16},{1,9},{9,1},{17,25},{25,17},{2,10},{10... | collective-permute-start | bytes 294920 | tf_op jit(solution)/shard_map/ppermute | solution.py:812
  35.9 0.9 %collective-permute-done.3 = bf16[4,48,256]{2,1,0:T(8,128)(2,1)S(1)} collective-permute-done((bf16[4,48,256]{2,1,0:T(8,128)(2,1)S(1)}, bf16[4,48,256]{2,1,0:T(8,128)(2,1)S(1)}, u32[]{:S(2)}, u32[]{:S(2)}) %collective-permute-start.3) | collective-permute-done | bytes 98336 | tf_op jit(solution)/shard_map/ppermute | solution.py:812
  36.9 1.3 %collective-permute-start.4 = (bf16[4,48,256]{2,1,0:T(8,128)(2,1)S(1)}, bf16[4,48,256]{2,1,0:T(8,128)(2,1)S(1)}, u32[]{:S(2)}, u32[]{:S(2)}) collective-permute-start(bf16[4,48,256]{2,1,0:T(8,128)(2,1)S(1)} %add_convert_fusion.after_ref.mine_ref), channel_id=1, source_target_pairs={{0,16},{8,24},{16,0},{24,8},{1,17},{9,25},{17,1},{25,9},{2,18},{10... | collective-permute-start | bytes 294920 | tf_op jit(solution)/shard_map/ppermute | solution.py:812
  38.2 1.3 %prepare_refine.1 = (bf16[144,128]{1,0:T(8,128)(2,1)S(1)}, bf16[128,128]{1,0:T(8,128)(2,1)S(1)}, bf16[96,128]{1,0:T(8,128)(2,1)S(1)}, f32[64,128]{1,0:T(8,128)S(1)}) custom-call(bf16[4,48,256]{2,1,0:T(8,128)(2,1)S(1)} %add_convert_fusion.after_ref.mine_ref, bf16[48,144]{1,0:T(8,128)(2,1)} %qkv_source.1, bf16[48,48]{1,0:T(8,128)(2,1)} %proj_source.1, ...), custom_call_target="tpu_custom_call" | custom-call | tf_op jit(solution)/shard_map/prepare_refine/pallas_call | solution.py:994
  39.5 1.5 %collective-permute-done.4.other_ref = bf16[4,48,256]{2,1,0:T(8,128)(2,1)S(1)} collective-permute-done((bf16[4,48,256]{2,1,0:T(8,128)(2,1)S(1)}, bf16[4,48,256]{2,1,0:T(8,128)(2,1)S(1)}, u32[]{:S(2)}, u32[]{:S(2)}) %collective-permute-start.4) | collective-permute-done | bytes 98336 | tf_op jit(solution)/shard_map/ppermute | solution.py:812
  41.0 1.7 %refinement.1 = bf16[3,128,128]{2,1,0:T(8,128)(2,1)S(1)} custom-call(bf16[4,48,256]{2,1,0:T(8,128)(2,1)S(1)} %add_convert_fusion.after_ref.mine_ref, bf16[4,48,256]{2,1,0:T(8,128)(2,1)S(1)} %collective-permute-done.4.other_ref, bf16[8,256,128]{2,1,0:T(8,128)(2,1)S(1)} %get-tuple-element.52.marks_ref, f32[64,128]{1,0:T(8,128)S(1)} %get-tuple-element.53.bias_ref, ...), custom_call_target="tpu_custom_call" | custom-call | tf_op jit(solution)/shard_map/refinement/pallas_call | solution.py:1012
  42.7 1.3 %collective-permute-start.5 = (bf16[3,128,128]{2,1,0:T(8,128)(2,1)S(1)}, bf16[3,128,128]{2,1,0:T(8,128)(2,1)S(1)}, u32[]{:S(2)}, u32[]{:S(2)}) collective-permute-start(bf16[3,128,128]{2,1,0:T(8,128)(2,1)S(1)} %refinement.1), channel_id=1, source_target_pairs={{0,8},{8,0},{16,24},{24,16},{1,9},{9,1},{17,25},{25,17},{2,10},{10... | collective-permute-start | bytes 294920 | tf_op jit(solution)/shard_map/ppermute | solution.py:812
  44.0 0.9 %collective-permute-done.5 = bf16[3,128,128]{2,1,0:T(8,128)(2,1)S(1)} collective-permute-done((bf16[3,128,128]{2,1,0:T(8,128)(2,1)S(1)}, bf16[3,128,128]{2,1,0:T(8,128)(2,1)S(1)}, u32[]{:S(2)}, u32[]{:S(2)}) %collective-permute-start.5) | collective-permute-done | bytes 98336 | tf_op jit(solution)/shard_map/ppermute | solution.py:812
  44.9 0.8 %maximum_convert_fusion = f32[3,256,128]{2,1,0:T(8,128)} fusion(bf16[3,128,128]{2,1,0:T(8,128)(2,1)S(1)} %get-tuple-element.58, bf16[3,128,128]{2,1,0:T(8,128)(2,1)S(1)} %get-tuple-element.57), kind=kLoop, calls=%fused_computation | loop fusion | flops 393216 | bytes 589824 | tf_op jit(solution)/shard_map/convert_element_type | solution.py:1025
  (2 shorter events, 0.0 us)
Async XLA Ops:
  6.9 7.3 %collective-permute-start = (bf16[2,4,32,256]{3,2,1,0:T(8,128)(2,1)S(1)}, bf16[2,4,32,256]{3,2,1,0:T(8,128)(2,1)S(1)}, u32[]{:S(2)}, u32[]{:S(2)}) collective-permute-start(bf16[2,4,32,256]{3,2,1,0:T(8,128)(2,1)S(1)} %get-tuple-element.41), channel_id=1, source_target_pairs={{0,4},{4,0},{1,5},{5,1},{2,6},{6,2},{3,7},{7,3},{8,12},{12,8},{9,1... | collective-permute-start | bytes 393224 | tf_op jit(solution)/shard_map/ppermute | solution.py:807
  14.3 10.6 %collective-permute-start.1 = (bf16[2,288,256]{2,1,0:T(8,128)(2,1)S(1)}, bf16[2,288,256]{2,1,0:T(8,128)(2,1)S(1)}, u32[]{:S(2)}, u32[]{:S(2)}) collective-permute-start(bf16[2,288,256]{2,1,0:T(8,128)(2,1)S(1)} %get-tuple-element.46), channel_id=1, source_target_pairs={{0,1},{2,3},{1,0},{3,2},{4,5},{6,7},{5,4},{7,6},{8,9},{10,11},{9,8... | collective-permute-start | bytes 884744 | tf_op jit(solution)/shard_map/ppermute | solution.py:807
  14.6 10.4 %collective-permute-start.2 = (bf16[2,288,256]{2,1,0:T(8,128)(2,1)S(1)}, bf16[2,288,256]{2,1,0:T(8,128)(2,1)S(1)}, u32[]{:S(2)}, u32[]{:S(2)}) collective-permute-start(bf16[2,288,256]{2,1,0:T(8,128)(2,1)S(1)} %get-tuple-element.47), channel_id=1, source_target_pairs={{1,2},{2,1},{5,6},{6,5},{9,10},{10,9},{13,14},{14,13},{17,18},{18,... | collective-permute-start | bytes 884744 | tf_op jit(solution)/shard_map/ppermute | solution.py:807
  34.0 2.9 %collective-permute-start.3 = (bf16[4,48,256]{2,1,0:T(8,128)(2,1)S(1)}, bf16[4,48,256]{2,1,0:T(8,128)(2,1)S(1)}, u32[]{:S(2)}, u32[]{:S(2)}) collective-permute-start(bf16[4,48,256]{2,1,0:T(8,128)(2,1)S(1)} %get-tuple-element.51), channel_id=1, source_target_pairs={{0,8},{8,0},{16,24},{24,16},{1,9},{9,1},{17,25},{25,17},{2,10},{10... | collective-permute-start | bytes 294920 | tf_op jit(solution)/shard_map/ppermute | solution.py:812
  36.9 4.1 %collective-permute-start.4 = (bf16[4,48,256]{2,1,0:T(8,128)(2,1)S(1)}, bf16[4,48,256]{2,1,0:T(8,128)(2,1)S(1)}, u32[]{:S(2)}, u32[]{:S(2)}) collective-permute-start(bf16[4,48,256]{2,1,0:T(8,128)(2,1)S(1)} %add_convert_fusion.after_ref.mine_ref), channel_id=1, source_target_pairs={{0,16},{8,24},{16,0},{24,8},{1,17},{9,25},{17,1},{25,9},{2,18},{10... | collective-permute-start | bytes 294920 | tf_op jit(solution)/shard_map/ppermute | solution.py:812
  42.7 2.2 %collective-permute-start.5 = (bf16[3,128,128]{2,1,0:T(8,128)(2,1)S(1)}, bf16[3,128,128]{2,1,0:T(8,128)(2,1)S(1)}, u32[]{:S(2)}, u32[]{:S(2)}) collective-permute-start(bf16[3,128,128]{2,1,0:T(8,128)(2,1)S(1)} %refinement.1), channel_id=1, source_target_pairs={{0,8},{8,0},{16,24},{24,16},{1,9},{9,1},{17,25},{25,17},{2,10},{10... | collective-permute-start | bytes 294920 | tf_op jit(solution)/shard_map/ppermute | solution.py:812

commit v8 on v7

--- a/solution.py
+++ b/solution.py
@@ -346,7 +346,6 @@
     left = iota((1, LANES), 1) < CELLS
     turned = pltpu.roll(queries, CELLS, 1).astype(BF16)
     queries = queries.astype(BF16)
-    depth = round_up(queries.shape[0], LANES)
     zero = jnp.zeros((HEAD_ROWS, LANES), BF16)
     results = []
     for even, odd in ((queries, turned), (turned, queries)):
@@ -358,7 +357,6 @@
             rows[2 * pair] = jnp.where(left, even[at : at + HEAD_ROWS], zero)
             rows[2 * pair + 1] = jnp.where(left, zero, odd[at + HEAD_ROWS : at + 2 * HEAD_ROWS])
             rows.append(marks)
-            rows.append(jnp.zeros((depth - queries.shape[0], LANES), BF16))
             columns.append(jnp.concatenate(rows, axis=0))
         results.append(jnp.concatenate(columns, axis=1) if pairs > 1 else columns[0])
     return results
@@ -375,7 +373,7 @@
         cut = slice(place * LANES, (place + 1) * LANES)
         for half, stationary in enumerate(split_queries(queries[:, cut], heads)):
             at = place * LANES + half * CELLS
-            scores.append(dot(keys[at : at + CELLS], stationary))
+            scores.append(dot(keys[at : at + CELLS, : stationary.shape[0]], stationary))
     return scores, values
 
 
@@ -418,7 +416,7 @@
         cut = slice(place * LANES, (place + 1) * LANES)
         for half, stationary in enumerate(split_queries(queries[:, cut], heads)):
             at = place * LANES + half * CELLS
-            scores.append(dot(keys[at : at + CELLS], stationary))
+            scores.append(dot(keys[at : at + CELLS, : stationary.shape[0]], stationary))
     yield
     weights = [
         (soft(scores[2 * place] + bias(a)), soft(scores[2 * place + 1] + bias(b)))

time: 46.1 us -> 46.1 us (level)
  no operation moved by 1% of the time
where the time goes in v8:
time: 46.1 us; the launch traced here: 45.7 us
  Pallas kernels  30.9 us (67%)
  starting transfers between devices  10.5 us (23%)
  waiting for transfers between devices  3.41 us (7%)
  other arithmetic  0.82 us (2%)
    pallas_call x1, Pallas kernels, local(): pl.pallas_call(functools.partial(outer_kernel, heads, channels, len(acros...  9.05 us
    pallas_call x2, Pallas kernels, block_one(): pl.pallas_call(functools.partial(first_kernel, heads, channels, places),...  8.83 us
    ppermute x3, starting transfers between devices, swap_pairs(): return lax.ppermute(strip, axis, pairs + [(j, i) for i, j in pairs])  6.04 us
    pallas_call x1, Pallas kernels, local(): pl.pallas_call(functools.partial(inner_kernel, heads, channels), grid=(1,...  5.9 us
    ppermute x3, starting transfers between devices, whole_swap(): return lax.ppermute(a, 'var', [(i, i ^ bit) for i in range(count)])  4.44 us
    pallas_call x1, Pallas kernels, local(): pl.pallas_call(functools.partial(prepare_kernel, heads), grid=(1,), in_sp...  4.07 us
    ppermute x3, waiting for transfers between devices, whole_swap(): return lax.ppermute(a, 'var', [(i, i ^ bit) for i in range(count)])  3.4 us
    pallas_call x1, Pallas kernels, local(): pl.pallas_call(functools.partial(refine_kernel, refine_heads, channels %...  1.71 us
  transfers between devices with their start and end apart: 6, of which 3 were waited for; matrix products, arithmetic and copies ran while one was open for 0% of the time, Pallas kernels for 29%

profile of v8, /device:TPU:9, one launch (start us, length us, event | category | flops | bytes accessed | tf_op | source)
XLA Modules:
  0.0 45.7 jit_solution(14122486129848862708)
XLA Ops:
  0.0 4.1 %prepare.1 = (bf16[2,400,256]{2,1,0:T(8,128)(2,1)S(1)}, bf16[2,256,256]{2,1,0:T(8,128)(2,1)S(1)}, bf16[2,256,256]{2,1,0:T(8,128)(2,1)S(1)}, bf16[2,256,384]{2,1,...) custom-call(bf16[64,32,180]{2,1,0:T(8,128)(2,1)} %features_ref.1, ...), custom_call_target="tpu_custom_call" | custom-call | tf_op jit(solution)/shard_map/prepare/pallas_call | solution.py:865
  4.1 2.8 %block_one_ends.1 = (f32[2,16,32,256]{3,2,1,0:T(8,128)S(1)}, bf16[2,64,256]{2,1,0:T(8,128)(2,1)S(1)}, bf16[2,64,256]{2,1,0:T(8,128)(2,1)S(1)}, bf16[2,4,32,256]{3,2,1,0:T(8,128)(2,1)S(1)}) custom-call(bf16[64,32,180]{2,1,0:T(8,128)(2,1)S(1)} %get-tuple-element.31.x_ref, s32[32,64]{1,0:T(8,128)S(1)} %get-tuple-element.32.labels_ref, ...), custom_call_target="tpu_custom_call" | custom-call | flops 6400000000 | bytes 3200000 | tf_op jit(solution)/shard_map/block_one_ends/pallas_call | solution.py:914
  6.9 1.3 %collective-permute-start = (bf16[2,4,32,256]{3,2,1,0:T(8,128)(2,1)S(1)}, bf16[2,4,32,256]{3,2,1,0:T(8,128)(2,1)S(1)}, u32[]{:S(2)}, u32[]{:S(2)}) collective-permute-start(bf16[2,4,32,256]{3,2,1,0:T(8,128)(2,1)S(1)} %get-tuple-element.41), channel_id=1, source_target_pairs={{0,4},{4,0},{1,5},{5,1},{2,6},{6,2},{3,7},{7,3},{8,12},{12,8},{9,1... | collective-permute-start | bytes 393224 | tf_op jit(solution)/shard_map/ppermute | solution.py:805
  8.2 6.0 %block_one_middle.1 = (f32[2,48,32,256]{3,2,1,0:T(8,128)S(1)}, bf16[2,192,256]{2,1,0:T(8,128)(2,1)S(1)}, bf16[2,192,256]{2,1,0:T(8,128)(2,1)S(1)}) custom-call(bf16[64,32,180]{2,1,0:T(8,128)(2,1)S(1)} %get-tuple-element.31.x_ref, s32[32,64]{1,0:T(8,128)S(1)} %get-tuple-element.32.labels_ref, f32[2,2,64,384]{3,2,1,0:T(8,128)S(1)} %get-tuple-element.33.bias_ref.refs_4_, ...), custom_call_target="tpu_custom_call" | custom-call | flops 19200000000 | bytes 9600000 | tf_op jit(solution)/shard_map/block_one_middle/pallas_call | solution.py:914
  14.2 0.0 collective-permute-done.refs_0_
  14.2 0.1 edges.1
  14.3 0.2 collective-permute-start.1
  14.6 4.5 %collective-permute-start.2 = (bf16[2,288,256]{2,1,0:T(8,128)(2,1)S(1)}, bf16[2,288,256]{2,1,0:T(8,128)(2,1)S(1)}, u32[]{:S(2)}, u32[]{:S(2)}) collective-permute-start(bf16[2,288,256]{2,1,0:T(8,128)(2,1)S(1)} %get-tuple-element.47), channel_id=1, source_target_pairs={{1,2},{2,1},{5,6},{6,5},{9,10},{10,9},{13,14},{14,13},{17,18},{18,... | collective-permute-start | bytes 884744 | tf_op jit(solution)/shard_map/ppermute | solution.py:805
  19.1 5.9 %block_two_inner.1 = (bf16[21,2,64,256]{3,2,1,0:T(8,128)(2,1)S(1)}, bf16[8,256,128]{2,1,0:T(8,128)(2,1)S(1)}) custom-call(f32[2,16,32,256]{3,2,1,0:T(8,128)S(1)} %get-tuple-element.39.ends_ref, f32[2,48,32,256]{3,2,1,0:T(8,128)S(1)} %get-tuple-element.40.middle_ref, f32[2,2,64,384]{3,2,1,0:T(8,128)S(1)} %get-tuple-element.33.bias_ref.refs_4_, ...), custom_call_target="tpu_custom_call" | custom-call | flops 16800000000 | bytes 8400000 | tf_op jit(solution)/shard_map/block_two_inner/pallas_call | solution.py:951
  25.0 0.0 collective-permute-done.1.refs_1_
  25.0 0.0 collective-permute-done.2.refs_2_
  25.0 9.0 %block_two_border.1 = (bf16[4,48,256]{2,1,0:T(8,128)(2,1)S(1)}, bf16[4,48,256]{2,1,0:T(8,128)(2,1)S(1)}) custom-call(f32[2,16,32,256]{3,2,1,0:T(8,128)S(1)} %get-tuple-element.39.ends_ref, f32[2,48,32,256]{3,2,1,0:T(8,128)S(1)} %get-tuple-element.40.middle_ref, bf16[2,4,32,256]{3,2,1,0:T(8,128)(2,1)S(1)} %collective-permute-done.refs_0_, ...), custom_call_target="tpu_custom_call" | custom-call | tf_op jit(solution)/shard_map/block_two_border/pallas_call | solution.py:966
  34.0 1.9 %collective-permute-start.3 = (bf16[4,48,256]{2,1,0:T(8,128)(2,1)S(1)}, bf16[4,48,256]{2,1,0:T(8,128)(2,1)S(1)}, u32[]{:S(2)}, u32[]{:S(2)}) collective-permute-start(bf16[4,48,256]{2,1,0:T(8,128)(2,1)S(1)} %get-tuple-element.51), channel_id=1, source_target_pairs={{0,8},{8,0},{16,24},{24,16},{1,9},{9,1},{17,25},{25,17},{2,10},{10... | collective-permute-start | bytes 294920 | tf_op jit(solution)/shard_map/ppermute | solution.py:810
  35.9 0.9 %collective-permute-done.3 = bf16[4,48,256]{2,1,0:T(8,128)(2,1)S(1)} collective-permute-done((bf16[4,48,256]{2,1,0:T(8,128)(2,1)S(1)}, bf16[4,48,256]{2,1,0:T(8,128)(2,1)S(1)}, u32[]{:S(2)}, u32[]{:S(2)}) %collective-permute-start.3) | collective-permute-done | bytes 98336 | tf_op jit(solution)/shard_map/ppermute | solution.py:810
  36.9 1.3 %collective-permute-start.4 = (bf16[4,48,256]{2,1,0:T(8,128)(2,1)S(1)}, bf16[4,48,256]{2,1,0:T(8,128)(2,1)S(1)}, u32[]{:S(2)}, u32[]{:S(2)}) collective-permute-start(bf16[4,48,256]{2,1,0:T(8,128)(2,1)S(1)} %add_convert_fusion.after_ref.mine_ref), channel_id=1, source_target_pairs={{0,16},{8,24},{16,0},{24,8},{1,17},{9,25},{17,1},{25,9},{2,18},{10... | collective-permute-start | bytes 294920 | tf_op jit(solution)/shard_map/ppermute | solution.py:810
  38.2 1.3 %prepare_refine.1 = (bf16[144,128]{1,0:T(8,128)(2,1)S(1)}, bf16[128,128]{1,0:T(8,128)(2,1)S(1)}, bf16[96,128]{1,0:T(8,128)(2,1)S(1)}, f32[64,128]{1,0:T(8,128)S(1)}) custom-call(bf16[4,48,256]{2,1,0:T(8,128)(2,1)S(1)} %add_convert_fusion.after_ref.mine_ref, bf16[48,144]{1,0:T(8,128)(2,1)} %qkv_source.1, bf16[48,48]{1,0:T(8,128)(2,1)} %proj_source.1, ...), custom_call_target="tpu_custom_call" | custom-call | tf_op jit(solution)/shard_map/prepare_refine/pallas_call | solution.py:992
  39.5 1.5 %collective-permute-done.4.other_ref = bf16[4,48,256]{2,1,0:T(8,128)(2,1)S(1)} collective-permute-done((bf16[4,48,256]{2,1,0:T(8,128)(2,1)S(1)}, bf16[4,48,256]{2,1,0:T(8,128)(2,1)S(1)}, u32[]{:S(2)}, u32[]{:S(2)}) %collective-permute-start.4) | collective-permute-done | bytes 98336 | tf_op jit(solution)/shard_map/ppermute | solution.py:810
  41.0 1.7 %refinement.1 = bf16[3,128,128]{2,1,0:T(8,128)(2,1)S(1)} custom-call(bf16[4,48,256]{2,1,0:T(8,128)(2,1)S(1)} %add_convert_fusion.after_ref.mine_ref, bf16[4,48,256]{2,1,0:T(8,128)(2,1)S(1)} %collective-permute-done.4.other_ref, bf16[8,256,128]{2,1,0:T(8,128)(2,1)S(1)} %get-tuple-element.52.marks_ref, f32[64,128]{1,0:T(8,128)S(1)} %get-tuple-element.53.bias_ref, ...), custom_call_target="tpu_custom_call" | custom-call | tf_op jit(solution)/shard_map/refinement/pallas_call | solution.py:1010
  42.7 1.3 %collective-permute-start.5 = (bf16[3,128,128]{2,1,0:T(8,128)(2,1)S(1)}, bf16[3,128,128]{2,1,0:T(8,128)(2,1)S(1)}, u32[]{:S(2)}, u32[]{:S(2)}) collective-permute-start(bf16[3,128,128]{2,1,0:T(8,128)(2,1)S(1)} %refinement.1), channel_id=1, source_target_pairs={{0,8},{8,0},{16,24},{24,16},{1,9},{9,1},{17,25},{25,17},{2,10},{10... | collective-permute-start | bytes 294920 | tf_op jit(solution)/shard_map/ppermute | solution.py:810
  44.0 0.9 %collective-permute-done.5 = bf16[3,128,128]{2,1,0:T(8,128)(2,1)S(1)} collective-permute-done((bf16[3,128,128]{2,1,0:T(8,128)(2,1)S(1)}, bf16[3,128,128]{2,1,0:T(8,128)(2,1)S(1)}, u32[]{:S(2)}, u32[]{:S(2)}) %collective-permute-start.5) | collective-permute-done | bytes 98336 | tf_op jit(solution)/shard_map/ppermute | solution.py:810
  44.9 0.8 %maximum_convert_fusion = f32[3,256,128]{2,1,0:T(8,128)} fusion(bf16[3,128,128]{2,1,0:T(8,128)(2,1)S(1)} %get-tuple-element.58, bf16[3,128,128]{2,1,0:T(8,128)(2,1)S(1)} %get-tuple-element.57), kind=kLoop, calls=%fused_computation | loop fusion | flops 393216 | bytes 589824 | tf_op jit(solution)/shard_map/convert_element_type | solution.py:1023
  (2 shorter events, 0.0 us)
Async XLA Ops:
  6.9 7.3 %collective-permute-start = (bf16[2,4,32,256]{3,2,1,0:T(8,128)(2,1)S(1)}, bf16[2,4,32,256]{3,2,1,0:T(8,128)(2,1)S(1)}, u32[]{:S(2)}, u32[]{:S(2)}) collective-permute-start(bf16[2,4,32,256]{3,2,1,0:T(8,128)(2,1)S(1)} %get-tuple-element.41), channel_id=1, source_target_pairs={{0,4},{4,0},{1,5},{5,1},{2,6},{6,2},{3,7},{7,3},{8,12},{12,8},{9,1... | collective-permute-start | bytes 393224 | tf_op jit(solution)/shard_map/ppermute | solution.py:805
  14.3 10.6 %collective-permute-start.1 = (bf16[2,288,256]{2,1,0:T(8,128)(2,1)S(1)}, bf16[2,288,256]{2,1,0:T(8,128)(2,1)S(1)}, u32[]{:S(2)}, u32[]{:S(2)}) collective-permute-start(bf16[2,288,256]{2,1,0:T(8,128)(2,1)S(1)} %get-tuple-element.46), channel_id=1, source_target_pairs={{0,1},{2,3},{1,0},{3,2},{4,5},{6,7},{5,4},{7,6},{8,9},{10,11},{9,8... | collective-permute-start | bytes 884744 | tf_op jit(solution)/shard_map/ppermute | solution.py:805
  14.6 10.4 %collective-permute-start.2 = (bf16[2,288,256]{2,1,0:T(8,128)(2,1)S(1)}, bf16[2,288,256]{2,1,0:T(8,128)(2,1)S(1)}, u32[]{:S(2)}, u32[]{:S(2)}) collective-permute-start(bf16[2,288,256]{2,1,0:T(8,128)(2,1)S(1)} %get-tuple-element.47), channel_id=1, source_target_pairs={{1,2},{2,1},{5,6},{6,5},{9,10},{10,9},{13,14},{14,13},{17,18},{18,... | collective-permute-start | bytes 884744 | tf_op jit(solution)/shard_map/ppermute | solution.py:805
  34.0 2.9 %collective-permute-start.3 = (bf16[4,48,256]{2,1,0:T(8,128)(2,1)S(1)}, bf16[4,48,256]{2,1,0:T(8,128)(2,1)S(1)}, u32[]{:S(2)}, u32[]{:S(2)}) collective-permute-start(bf16[4,48,256]{2,1,0:T(8,128)(2,1)S(1)} %get-tuple-element.51), channel_id=1, source_target_pairs={{0,8},{8,0},{16,24},{24,16},{1,9},{9,1},{17,25},{25,17},{2,10},{10... | collective-permute-start | bytes 294920 | tf_op jit(solution)/shard_map/ppermute | solution.py:810
  36.9 4.1 %collective-permute-start.4 = (bf16[4,48,256]{2,1,0:T(8,128)(2,1)S(1)}, bf16[4,48,256]{2,1,0:T(8,128)(2,1)S(1)}, u32[]{:S(2)}, u32[]{:S(2)}) collective-permute-start(bf16[4,48,256]{2,1,0:T(8,128)(2,1)S(1)} %add_convert_fusion.after_ref.mine_ref), channel_id=1, source_target_pairs={{0,16},{8,24},{16,0},{24,8},{1,17},{9,25},{17,1},{25,9},{2,18},{10... | collective-permute-start | bytes 294920 | tf_op jit(solution)/shard_map/ppermute | solution.py:810
  42.7 2.2 %collective-permute-start.5 = (bf16[3,128,128]{2,1,0:T(8,128)(2,1)S(1)}, bf16[3,128,128]{2,1,0:T(8,128)(2,1)S(1)}, u32[]{:S(2)}, u32[]{:S(2)}) collective-permute-start(bf16[3,128,128]{2,1,0:T(8,128)(2,1)S(1)} %refinement.1), channel_id=1, source_target_pairs={{0,8},{8,0},{16,24},{24,16},{1,9},{9,1},{17,25},{25,17},{2,10},{10... | collective-permute-start | bytes 294920 | tf_op jit(solution)/shard_map/ppermute | solution.py:810
